TPU v7x, 32 devices: a whole 2x2x4 slice. The times are simulated.
32 devices in a mesh: dp: 8 (over z, y), row: 2 (over core), col: 2 (over x).
Axes of the slice: x: 2, y: 2, z: 4, core: 2. Of those that a mesh axis runs over, the one named last changes fastest.
Arguments:
- tokens: bfloat16 [2, 8192, 1536], P('col', ('dp', 'row')), may hold values from -18 to 18
- cotangent: float32 [2, 8192, 1536], P('col', ('dp', 'row')), may hold values from -6 to 6
- routes: int32 [4, 16384], P(None, 'dp'), may hold values from 0 to 31, as said below
- route_gates: float32 [4, 16384], P(None, 'dp'), may hold values from 0.5 to 1.5
- block_ids: int32 [16, 1024], P(('dp', 'col')), may hold values from 0 to 7, never falling along the last dimension, each value on 1 to 256 neighbouring positions
- w_qkv: bfloat16 [1536, 2, 1024], P('col', 'row'), may hold values from -0.15625 to 0.15625
- w_out: bfloat16 [2, 768, 1536], P('row', None, 'col'), may hold values from -2 to 2
- w_gate_up: bfloat16 [32, 1536, 2, 768], P(None, 'col', None, 'row'), may hold values from -0.15625 to 0.15625
- w_down: bfloat16 [32, 768, 1536], P(None, 'row', 'col'), may hold values from -0.21875 to 0.21875
- gains: float32 [2, 1536], P(None, 'col'), may hold values from 0.5 to 1.5
- gain_first: float32 [2, 1536], P(None, 'col'), may hold values from -1536 to 1536
- gain_second: float32 [2, 1536], P(None, 'col'), may hold values from 65536 to 262144
- qkv_master: float32 [1536, 2, 1024], P(('col', 'dp'), 'row'), may hold values from -0.15625 to 0.15625
- qkv_first: float32 [1536, 2, 1024], P(('col', 'dp'), 'row'), may hold values from -1536 to 1536
- qkv_second: float32 [1536, 2, 1024], P(('col', 'dp'), 'row'), may hold values from 65536 to 262144
- out_master: float32 [2, 768, 1536], P('row', None, ('col', 'dp')), may hold values from -2 to 2
- out_first: float32 [2, 768, 1536], P('row', None, ('col', 'dp')), may hold values from -48 to 48
- out_second: float32 [2, 768, 1536], P('row', None, ('col', 'dp')), may hold values from 64 to 256
- gate_up_master: float32 [32, 1536, 2, 768], P('dp', 'col', None, 'row'), may hold values from -0.15625 to 0.15625
- gate_up_first: float32 [32, 1536, 2, 768], P('dp', 'col', None, 'row'), may hold values from -192 to 192
- gate_up_second: float32 [32, 1536, 2, 768], P('dp', 'col', None, 'row'), may hold values from 1024 to 4096
- down_master: float32 [32, 768, 1536], P('dp', 'row', 'col'), may hold values from -0.21875 to 0.21875
- down_first: float32 [32, 768, 1536], P('dp', 'row', 'col'), may hold values from -192 to 192
- down_second: float32 [32, 768, 1536], P('dp', 'row', 'col'), may hold values from 1024 to 4096
Outputs:
- block_output: float32 [2, 8192, 1536], P('col', ('dp', 'row'))
- input_grad: float32 [2, 8192, 1536], P('col', ('dp', 'row'))
- qkv_weight: float32 [1536, 2, 1024], P(('col', 'dp'), 'row')
- qkv_moment_one: float32 [1536, 2, 1024], P(('col', 'dp'), 'row')
- qkv_moment_two: float32 [1536, 2, 1024], P(('col', 'dp'), 'row')
- qkv_copy: bfloat16 [1536, 2, 1024], P(('col', 'dp'), 'row')
- out_weight: float32 [2, 768, 1536], P('row', None, ('col', 'dp'))
- out_moment_one: float32 [2, 768, 1536], P('row', None, ('col', 'dp'))
- out_moment_two: float32 [2, 768, 1536], P('row', None, ('col', 'dp'))
- out_copy: bfloat16 [2, 768, 1536], P('row', None, ('col', 'dp'))
- gate_up_weight: float32 [32, 1536, 2, 768], P('dp', 'col', None, 'row')
- gate_up_moment_one: float32 [32, 1536, 2, 768], P('dp', 'col', None, 'row')
- gate_up_moment_two: float32 [32, 1536, 2, 768], P('dp', 'col', None, 'row')
- gate_up_copy: bfloat16 [32, 1536, 2, 768], P('dp', 'col', None, 'row')
- down_weight: float32 [32, 768, 1536], P('dp', 'row', 'col')
- down_moment_one: float32 [32, 768, 1536], P('dp', 'row', 'col')
- down_moment_two: float32 [32, 768, 1536], P('dp', 'row', 'col')
- down_copy: bfloat16 [32, 768, 1536], P('dp', 'row', 'col')
- gains_new: float32 [2, 1536], P(None, 'col')
- gains_moment_one: float32 [2, 1536], P(None, 'col')
- gains_moment_two: float32 [2, 1536], P(None, 'col')
- clip_factors: float32 [12], replicated
Inputs may be any that keep to these rules, and one draw needn't show every extreme that they name: `routes`: each token names 4 different experts; among the 2048 tokens of one index of dp no expert is named by more than 320 tokens, some expert by exactly 320, and every expert by at least one. `block_ids`: along each sequence the block numbers never fall, start at 0 and rise by one; a block has 1 to 256 positions.
All inputs are finite; a program needn't handle non-finite values.
Results may differ from a plain program's by a relative error of at most 0.014.
Values may be sent and summed in bfloat16 or wider, within the bound.
No kernel may reach another device: no remote copies, remote signals or barrier semaphores. Data moves between devices by JAX's collectives and lax.ppermute only.
A program may use at most 768 MiB of HBM per device.

v0:
```python
import jax
import jax.numpy as jnp
from jax import lax
from jax.sharding import PartitionSpec as P

D = 1536
KVH = 2
HD = 128
E = 32
FFE = 768
TOP = 4
GROUP = 6
LEN = 1024
STEP = 5


EPS_NORM = 1e-06
BETA_ONE = 0.5
BETA_TWO = 0.5
ADAM_EPS = 1e-08
DECAY_RATE = 0.1
TAU_CLIP = 3.0


def col_total(values):
    return lax.psum(jnp.sum(values, axis=1), "col")


def norm_forward(values, gain):
    factor = lax.rsqrt(col_total(values * values) / D + EPS_NORM)
    return (values * factor[:, None] * gain[None, :], factor)


def norm_backward(values, factor, gain, grad_normed):
    inner = col_total(values * gain[None, :] * grad_normed) / D
    grad_values = (
        factor[:, None] * gain[None, :] * grad_normed - values * (factor**3 * inner)[:, None]
    )
    grad_gain = jnp.sum(grad_normed * values * factor[:, None], axis=0)
    return (grad_values, grad_gain)


def row_rows(values):
    return lax.all_gather(values, "row", axis=0, tiled=True)


def col_rows(values):
    return lax.all_gather(values, "col", axis=0, tiled=True)


def token_out(values):
    return lax.psum_scatter(values, "row", scatter_dimension=0, tiled=True)


def col_sums(term_fn, rows):
    return lax.psum_scatter(
        term_fn(jnp.int32(0), lax.axis_size("col") * rows), "col", scatter_dimension=0, tiled=True
    )


def wide_sums(values):
    return lax.psum_scatter(values, "col", scatter_dimension=1, tiled=True)


def slot_table(routes, route_gates, experts, capacity):
    pairs = routes.reshape(-1)
    number = pairs.shape[0]
    order = jnp.argsort(pairs, stable=True)
    ranked = pairs[order]
    onehot = (pairs[:, None] == jnp.arange(experts, dtype=jnp.int32)[None, :]).astype(jnp.int32)
    totals = jnp.sum(onehot, axis=0)
    starts = jnp.cumsum(totals) - totals
    place = ranked * capacity + jnp.arange(number, dtype=jnp.int32) - starts[ranked]
    owner = order // routes.shape[1]
    slot_tok = jnp.zeros((experts * capacity,), jnp.int32).at[place].set(owner)
    slot_gate = (
        jnp.zeros((experts * capacity,), jnp.float32).at[place].set(route_gates.reshape(-1)[order])
    )
    return (slot_tok, slot_gate)


def masked_scores(queries, keys_in, blocks):
    scores = jnp.einsum(
        "qkgd,skd->kgqs", queries, keys_in, preferred_element_type=jnp.float32
    ) * HD ** (-0.5)
    allowed = blocks[None, :] <= blocks[:, None]
    return jnp.where(allowed[None, None], scores, -1e30)


def attend_forward(entries):
    blocks, packed = entries
    masked = masked_scores(packed[:, :, :GROUP], packed[:, :, GROUP], blocks)
    row_top = jnp.max(masked, axis=-1, keepdims=True)
    weights = jnp.exp(masked - row_top)
    total = jnp.sum(weights, axis=-1, keepdims=True)
    probs_low = (weights / total).astype(jnp.bfloat16)
    mixed = jnp.einsum(
        "kgqs,skd->qkgd", probs_low, packed[:, :, GROUP + 1], preferred_element_type=jnp.float32
    )
    mixed = mixed.reshape(mixed.shape[0], -1).astype(jnp.bfloat16)
    return (mixed, (row_top + jnp.log(total))[..., 0], jnp.max(row_top[..., 0], axis=-1))


def attend_backward(entries):
    blocks, packed, log_total, grad_mixed = entries
    queries = packed[:, :, :GROUP]
    keys_in = packed[:, :, GROUP]
    values_in = packed[:, :, GROUP + 1]
    probs = jnp.exp(masked_scores(queries, keys_in, blocks) - log_total[..., None])
    grad_heads = grad_mixed.reshape(queries.shape)
    grad_probs = jnp.einsum(
        "qkgd,skd->kgqs", grad_heads, values_in, preferred_element_type=jnp.float32
    )
    delta = jnp.sum(probs * grad_probs, axis=-1, keepdims=True)
    grad_scores = (probs * (grad_probs - delta)).astype(jnp.bfloat16)
    grad_query = jnp.einsum(
        "kgqs,skd->qkgd", grad_scores, keys_in, preferred_element_type=jnp.float32
    ) * HD ** (-0.5)
    grad_key = jnp.einsum(
        "kgqs,qkgd->skd", grad_scores, queries, preferred_element_type=jnp.float32
    ) * HD ** (-0.5)
    grad_value = jnp.einsum(
        "kgqs,qkgd->skd", probs.astype(jnp.bfloat16), grad_heads, preferred_element_type=jnp.float32
    )
    joined = jnp.concatenate([grad_query, grad_key[:, :, None], grad_value[:, :, None]], axis=2)
    return joined.astype(jnp.bfloat16)


def adam_step(master, moment_one, moment_two, gradient, rate, decay):
    first = BETA_ONE * moment_one + (1.0 - BETA_ONE) * gradient
    second = BETA_TWO * moment_two + (1.0 - BETA_TWO) * gradient * gradient
    first_hat = first / (1.0 - BETA_ONE**STEP)
    second_hat = second / (1.0 - BETA_TWO**STEP)
    updated = master - rate * (first_hat / (jnp.sqrt(second_hat) + ADAM_EPS) + decay * master)
    return (updated, first, second)


def on_device(
    tokens,
    cotangent,
    routes,
    route_gates,
    block_ids,
    w_qkv,
    w_out,
    w_gate_up,
    w_down,
    gains,
    gain_first,
    gain_second,
    qkv_master,
    qkv_first,
    qkv_second,
    out_master,
    out_first,
    out_second,
    gate_up_master,
    gate_up_first,
    gate_up_second,
    down_master,
    down_first,
    down_second,
):
    col_count = lax.axis_size("col")
    col_index = lax.axis_index("col")
    row_index = lax.axis_index("row")
    token_block = routes.shape[1]
    capacity = 5 * token_block * TOP // (4 * E)
    slot_total = E * capacity
    slot_local = slot_total // col_count
    seq_rows = token_block // col_count
    local_groups = w_qkv.shape[1]
    width_local = w_qkv.shape[0]
    ffn_local = w_down.shape[1]
    seq_count = block_ids.shape[0]
    slot_tok, slot_gate = slot_table(routes.T, route_gates.T, E, capacity)
    slot_begin = col_index * slot_local
    my_gate = lax.dynamic_slice_in_dim(slot_gate, slot_begin, slot_local, 0)
    inputs = tokens.reshape(-1, width_local).astype(jnp.float32)
    grad_rows = cotangent.reshape(-1, width_local)
    normed_one, factor_one = norm_forward(inputs, gains[0])
    rows_one = row_rows(normed_one.astype(jnp.bfloat16))
    qkv_flat = w_qkv.reshape(width_local, -1)

    def project(start, count):
        return jnp.dot(rows_one, qkv_flat, preferred_element_type=jnp.float32)

    packed = col_sums(project, seq_rows).astype(jnp.bfloat16)
    packed = packed.reshape(seq_count, LEN, local_groups, GROUP + 2, HD)
    mixed, log_total, seq_top = lax.map(attend_forward, (block_ids, packed))
    full_top = jnp.full((KVH, GROUP), -1e30, jnp.float32)
    full_top = lax.dynamic_update_slice(
        full_top, jnp.max(seq_top, axis=0), (row_index * local_groups, jnp.zeros((), jnp.int32))
    )
    head_top = lax.pmax(full_top, ("dp", "row", "col"))
    heads_all = col_rows(mixed.reshape(seq_rows, -1))
    out_flat = w_out.reshape(-1, width_local)
    attn = token_out(jnp.dot(heads_all, out_flat, preferred_element_type=jnp.float32))
    hidden = inputs + attn
    normed_two, factor_two = norm_forward(hidden, gains[1])
    rows_two = row_rows(normed_two.astype(jnp.bfloat16))
    grad_moe = row_rows(grad_rows.astype(jnp.bfloat16))
    down_turned = jnp.swapaxes(w_down, 1, 2)
    local_weights, local_down = (
        lax.all_to_all(w_gate_up, "col", split_axis=0, concat_axis=1, tiled=True),
        lax.all_to_all(down_turned, "col", split_axis=0, concat_axis=1, tiled=True),
    )
    wide_rows, wide_grad = (
        lax.all_gather(rows_two, "col", axis=1, tiled=True),
        lax.all_gather(grad_moe, "col", axis=1, tiled=True),
    )
    picked = lax.dynamic_slice_in_dim(slot_tok, slot_begin, slot_local, 0)
    slot_rows = wide_rows[picked].reshape(-1, capacity, wide_rows.shape[1])
    gate_up = jnp.einsum(
        "ecd,edgh->ecgh", slot_rows, local_weights, preferred_element_type=jnp.float32
    ).reshape(slot_local, 2, ffn_local)
    gate_half = gate_up[:, 0]
    up_half = gate_up[:, 1]
    sigmoid_gate = jax.nn.sigmoid(gate_half)
    silu_gate = gate_half * sigmoid_gate
    weighted = (silu_gate * up_half * my_gate[:, None]).astype(jnp.bfloat16)
    weighted_blocks = weighted.reshape(-1, capacity, ffn_local)
    slot_wide = jnp.einsum(
        "ech,edh->ecd", weighted_blocks, local_down, preferred_element_type=jnp.float32
    ).reshape(slot_local, -1)
    moe = token_out(wide_sums(jax.ops.segment_sum(slot_wide, picked, num_segments=token_block)))
    block_output = hidden + moe
    slot_grad_wide = wide_grad[picked].reshape(-1, capacity, wide_grad.shape[1])
    down_local_grad = jnp.einsum(
        "ech,ecd->edh", weighted_blocks, slot_grad_wide, preferred_element_type=jnp.float32
    )
    grad_weighted = jnp.einsum(
        "ecd,edh->ech", slot_grad_wide, local_down, preferred_element_type=jnp.float32
    ).reshape(slot_local, ffn_local)
    grad_act = grad_weighted * my_gate[:, None]
    grad_gate = grad_act * up_half * sigmoid_gate * (1.0 + gate_half * (1.0 - sigmoid_gate))
    grad_up = grad_act * silu_gate
    grad_pair = jnp.stack([grad_gate, grad_up], axis=1).astype(jnp.bfloat16)
    pair_blocks = grad_pair.reshape(-1, capacity, 2, ffn_local)
    local_grad = jnp.einsum(
        "ecd,ecgh->edgh", slot_rows, pair_blocks, preferred_element_type=jnp.float32
    )
    grad_gate_up, down_back = (
        lax.all_to_all(local_grad, "col", split_axis=1, concat_axis=0, tiled=True),
        lax.all_to_all(down_local_grad, "col", split_axis=1, concat_axis=0, tiled=True),
    )
    grad_down = jnp.swapaxes(down_back, 1, 2)
    slot_back = jnp.einsum(
        "ecgh,edgh->ecd", pair_blocks, local_weights, preferred_element_type=jnp.float32
    ).reshape(slot_local, -1)
    token_back = wide_sums(jax.ops.segment_sum(slot_back, picked, num_segments=token_block))
    grad_normed_two = token_out(token_back)
    grad_hidden_norm, grad_gain_two = norm_backward(hidden, factor_two, gains[1], grad_normed_two)
    grad_hidden = grad_rows + grad_hidden_norm
    grad_attn = row_rows(grad_hidden.astype(jnp.bfloat16))
    grad_out = jnp.einsum(
        "tf,td->fd", heads_all, grad_attn, preferred_element_type=jnp.float32
    ).reshape(w_out.shape)

    def head_terms(start, count):
        return jnp.einsum("td,fd->tf", grad_attn, out_flat, preferred_element_type=jnp.float32)

    grad_heads = col_sums(head_terms, seq_rows).astype(jnp.bfloat16)
    grad_packed = lax.map(
        attend_backward, (block_ids, packed, log_total, grad_heads.reshape(seq_count, LEN, -1))
    )
    grad_packed_all = col_rows(grad_packed.reshape(seq_rows, -1))
    grad_qkv = jnp.einsum(
        "td,tf->df", rows_one, grad_packed_all, preferred_element_type=jnp.float32
    ).reshape(w_qkv.shape)
    grad_normed_one = token_out(
        jnp.einsum("tf,df->td", grad_packed_all, qkv_flat, preferred_element_type=jnp.float32)
    )
    grad_input_norm, grad_gain_one = norm_backward(inputs, factor_one, gains[0], grad_normed_one)
    input_grad = grad_hidden + grad_input_norm
    grad_qkv, grad_out, grad_gate_up, grad_down = (
        lax.psum_scatter(grad_qkv, "dp", scatter_dimension=0, tiled=True),
        lax.psum_scatter(grad_out, "dp", scatter_dimension=2, tiled=True),
        lax.psum_scatter(grad_gate_up, "dp", scatter_dimension=0, tiled=True),
        lax.psum_scatter(grad_down, "dp", scatter_dimension=0, tiled=True),
    )
    grad_gains = lax.psum(jnp.stack([grad_gain_one, grad_gain_two]), ("dp", "row"))
    factors = TAU_CLIP / jnp.maximum(head_top, TAU_CLIP)
    local_factors = lax.dynamic_slice_in_dim(factors, row_index * local_groups, local_groups, 0)
    query_scale = jnp.repeat(jnp.sqrt(local_factors), HD, axis=1)
    key_scale = jnp.repeat(jnp.sqrt(jnp.min(local_factors, axis=1, keepdims=True)), HD, axis=1)
    column_scale = jnp.concatenate([query_scale, key_scale, jnp.ones_like(key_scale)], axis=1)
    qkv_new, qkv_one, qkv_two = adam_step(
        qkv_master, qkv_first, qkv_second, grad_qkv, D ** (-0.5), DECAY_RATE
    )
    qkv_new = qkv_new * column_scale[None]
    out_new, out_one, out_two = adam_step(
        out_master, out_first, out_second, grad_out, max(D // 192, 1) ** (-0.5), DECAY_RATE
    )
    gate_up_new, gate_up_one, gate_up_two = adam_step(
        gate_up_master, gate_up_first, gate_up_second, grad_gate_up, D ** (-0.5), DECAY_RATE
    )
    down_new, down_one, down_two = adam_step(
        down_master, down_first, down_second, grad_down, FFE ** (-0.5), DECAY_RATE
    )
    gains_new, gains_one, gains_two = adam_step(
        gains, gain_first, gain_second, grad_gains, 0.2, 0.0
    )
    return (
        block_output.reshape(1, -1, 2 * width_local),
        input_grad.reshape(1, -1, 2 * width_local),
        qkv_new,
        qkv_one,
        qkv_two,
        qkv_new.astype(jnp.bfloat16),
        out_new,
        out_one,
        out_two,
        out_new.astype(jnp.bfloat16),
        gate_up_new,
        gate_up_one,
        gate_up_two,
        gate_up_new.astype(jnp.bfloat16),
        down_new,
        down_one,
        down_two,
        down_new.astype(jnp.bfloat16),
        gains_new,
        gains_one,
        gains_two,
        factors.reshape(-1),
    )


def solution(mesh):
    in_specs = (
        P("col", ("dp", "row"), None),
        P("col", ("dp", "row"), None),
        P(None, "dp"),
        P(None, "dp"),
        P(("dp", "col"), None),
        P("col", "row", None),
        P("row", None, "col"),
        P(None, "col", None, "row"),
        P(None, "row", "col"),
        P(None, "col"),
        P(None, "col"),
        P(None, "col"),
        P(("col", "dp"), "row", None),
        P(("col", "dp"), "row", None),
        P(("col", "dp"), "row", None),
        P("row", None, ("col", "dp")),
        P("row", None, ("col", "dp")),
        P("row", None, ("col", "dp")),
        P("dp", "col", None, "row"),
        P("dp", "col", None, "row"),
        P("dp", "col", None, "row"),
        P("dp", "row", "col"),
        P("dp", "row", "col"),
        P("dp", "row", "col"),
    )
    out_specs = (
        P("col", ("dp", "row"), None),
        P("col", ("dp", "row"), None),
        P(("col", "dp"), "row", None),
        P(("col", "dp"), "row", None),
        P(("col", "dp"), "row", None),
        P(("col", "dp"), "row", None),
        P("row", None, ("col", "dp")),
        P("row", None, ("col", "dp")),
        P("row", None, ("col", "dp")),
        P("row", None, ("col", "dp")),
        P("dp", "col", None, "row"),
        P("dp", "col", None, "row"),
        P("dp", "col", None, "row"),
        P("dp", "col", None, "row"),
        P("dp", "row", "col"),
        P("dp", "row", "col"),
        P("dp", "row", "col"),
        P("dp", "row", "col"),
        P(None, "col"),
        P(None, "col"),
        P(None, "col"),
        P(),
    )
    return jax.shard_map(
        on_device, mesh=mesh, in_specs=in_specs, out_specs=out_specs, check_vma=False
    )
```

profile of v0, /device:TPU:0, one launch (start us, length us, event | category | flops | bytes accessed | tf_op | source)
XLA Modules:
  0.0 4765.8 jit_solution(9213916159322497367)
XLA Ops:
  23.9 14.0 all-gather.9.cloned.1.call-done
  37.9 7.5 fusion.25
  47.7 98.3 %reduce-scatter.12.cloned.1.call-done = f32[1024,1024]{1,0:T(8,128)} async-done(((f32[2048,1024]{1,0:T(8,128)}), f32[1024,1024]{1,0:T(8,128)}) %reduce-scatter.12.cloned.1.call-update) | async-done | bytes 4194320 | tf_op jit(solution)/shard_map/reduce_scatter | solution.py:56
  152.0 12.8 fusion.77
  164.8 10.2 fusion.3
  175.1 12.1 fusion.20
  187.5 44.8 all-gather.11.cloned.1.call-done
  232.3 7.6 fusion.38
  239.9 11.6 all-to-all-start.1
  259.4 197.2 %all-to-all-done.1 = bf16[32,768,384]{1,2,0:T(8,128)(2,1)} async-done(((bf16[32,768,384]{1,2,0:T(8,128)(2,1)}), bf16[32,768,384]{1,2,0:T(8,128)(2,1)}, u32[]{:S(2)}, u32[]{:S(2)}) %all-to-all-start.1) | async-done | bytes 18874400 | tf_op jit(solution)/shard_map/all_to_all | solution.py:206
  456.6 14.6 all-to-all-start
  476.1 401.7 %psum.36 = f32[1024]{0:T(1024)S(1)} all-reduce(f32[1024]{0:T(1024)S(1)} %get-tuple-element.226), channel_id=1, replica_groups=mesh['dp'=8,'row'=2,'col'=2] {'col'}, use_global_device_ids=true, to_apply=%region_11.12 | all-reduce | flops 1024 | bytes 8192 | tf_op jit(solution)/shard_map/psum | solution.py:26
  883.6 6.8 sort.17
  895.4 45.5 gather_fusion
  942.0 45.5 gather_fusion.2
  996.1 15.8 select_select_fusion
  1012.0 30.5 scatter_custom_fusion
  1042.5 30.6 scatter_custom_fusion.1
  1074.3 25.0 copy.220
  1099.4 34.9 gather_fusion.3
  1134.2 19.1 fusion.80
  1153.3 25.8 copy.263
  1179.1 25.4 copy.217
  1204.5 35.0 gather_fusion.1
  1239.4 26.7 fusion.78
  1266.1 18.6 multiply_convert_fusion.1
  1284.7 27.2 fusion.18
  1311.9 56.0 %scatter_custom_fusion.3 = f32[2048,1536]{1,0:T(8,128)} fusion(s32[5120]{0:T(1024)} %get-tuple-element.225, f32[5120,1536]{1,0:T(8,128)} %bitcast.250, f32[]{:T(128)} %constant.48.clone.1), kind=kCustom, calls=%fused_computation.39 | custom fusion | flops 7864320 | bytes 12583424 | tf_op jit(solution)/shard_map/scatter-add | solution.py:251
  1368.1 8.7 multiply_convert_fusion.2
  1376.8 21.3 fusion.79
  1398.2 55.9 %scatter_custom_fusion.2 = f32[2048,1536]{1,0:T(8,128)} fusion(s32[5120]{0:T(1024)} %get-tuple-element.225, f32[5120,1536]{1,0:T(8,128)} %bitcast.249, f32[]{:T(128)} %constant.48.clone.1), kind=kCustom, calls=%fused_computation.41 | custom fusion | flops 7864320 | bytes 12583424 | tf_op jit(solution)/shard_map/scatter-add | solution.py:226
  1454.1 59.6 %reduce-scatter.20.cloned.1.call-done = f32[2048,768]{1,0:T(8,128)} async-done(((f32[2048,1536]{1,0:T(8,128)}), f32[2048,768]{1,0:T(8,128)}) %reduce-scatter.20.cloned.1.call-update) | async-done | bytes 6291472 | tf_op jit(solution)/shard_map/reduce_scatter | solution.py:62
  1513.8 146.6 %reduce-scatter.16.cloned.1.call-done = f32[2048,768]{1,0:T(8,128)} async-done(((f32[2048,1536]{1,0:T(8,128)}), f32[2048,768]{1,0:T(8,128)}) %reduce-scatter.16.cloned.1.call-update) | async-done | bytes 6291472 | tf_op jit(solution)/shard_map/reduce_scatter | solution.py:62
  1660.5 16.8 reduce-scatter.22.cloned.1.call-done
  1686.4 8.8 reduce-scatter.18.cloned.1.call-done
  1695.2 7.8 fusion.73
  1703.2 13.2 all-gather.21.cloned.1.call-done
  1716.5 7.2 fusion.36
  1724.5 77.6 %reduce-scatter.24.cloned.1.call-done = f32[1024,768]{1,0:T(8,128)} async-done(((f32[2048,768]{1,0:T(8,128)}), f32[1024,768]{1,0:T(8,128)}) %reduce-scatter.24.cloned.1.call-update) | async-done | bytes 3145744 | tf_op jit(solution)/shard_map/reduce_scatter | solution.py:56
  1807.0 11.2 fusion.40
  1818.3 20.6 fusion.63
  1838.8 16.8 fusion.8
  1866.5 6.8 convolution_bitcast_fusion.1
  1873.3 6.8 copy.233
  1880.2 22.8 fusion.81
  1903.0 35.9 copy.242
  1938.9 14.8 all-to-all-start.3
  1954.2 8.3 convolution_bitcast_fusion
  1962.5 8.5 fusion.23
  1971.1 389.6 %all-to-all-done.3 = f32[16,1536,384]{2,0,1:T(8,128)} async-done(((f32[16,1536,384]{2,0,1:T(8,128)}), f32[16,1536,384]{2,0,1:T(8,128)}, u32[]{:S(2)}, u32[]{:S(2)}) %all-to-all-start.3) | async-done | bytes 37748768 | tf_op jit(solution)/shard_map/all_to_all | solution.py:245
  2360.7 36.9 copy.243
  2397.8 36.4 fusion.17
  2434.3 121.5 %copy.237 = f32[16,1536,2,384]{3,2,0,1:T(2,128)} copy(f32[16,1536,2,384]{3,1,2,0:T(8,128)} %fusion.17) | data formatting | bytes 150994944 | tf_op jit(solution)/shard_map/ecd,ecgh->edgh/dot_general | solution.py:240
  2555.8 878.8 %all_to_all.72 = f32[16,1536,2,384]{3,2,0,1:T(2,128)} all-to-all(f32[16,1536,2,384]{3,2,0,1:T(2,128)} %copy.237), channel_id=1, replica_groups=mesh['dp'=8,'row'=2,'col'=2] {'col'}, dimensions={1} | all-to-all | bytes 150994944 | tf_op jit(solution)/shard_map/all_to_all | solution.py:244
  3434.6 63.3 %copy.238 = f32[2,16,768,2,384]{4,2,3,1,0:T(8,128)} copy(f32[2,16,768,2,384]{4,3,1,2,0:T(2,128)} %bitcast.103) | data formatting | bytes 150994944 | tf_op jit(solution)/shard_map/all_to_all | solution.py:244
  3508.0 44.3 pmax.7
  3579.9 33.1 psum.39
  3613.6 14.0 fusion.65
  3627.6 1048.3 %reduce-scatter.30.cloned.1.call-done = f32[4,768,2,384]{3,1,2,0:T(8,128)} async-done(((f32[32,768,2,384]{3,1,2,0:T(8,128)}), f32[4,768,2,384]{3,1,2,0:T(8,128)}) %reduce-scatter.30.cloned.1.call-update) | async-done | bytes 9437200 | tf_op jit(solution)/shard_map/reduce_scatter | solution.py:279
  4675.9 26.6 fusion.67
  4702.6 9.4 copy.250
  4712.0 17.5 copy.247
  4729.5 14.5 copy.248
  4744.0 14.5 copy.249
  (207 shorter events, 123.2 us)
Async XLA Ops:
  7.2 30.7 copy-start
  7.2 30.7 all-gather.9.cloned.1.call-start
  8.1 15.7 copy-start.16
  8.1 869.7 %copy-start.20 = (f32[768]{0:T(1024)}, f32[768]{0:T(1024)S(1)}, u32[]{:S(2)}) copy-start(f32[768]{0:T(1024)S(1)} %get-tuple-element.201) | copy-start | bytes 9220
  19.8 25.6 copy-start.24
  19.8 0.6 copy-start.18
  23.8 122.2 %reduce-scatter.12.cloned.1.call-start = ((), (), s32[]{:S(2)}) async-start(), calls=%async_computation.16 | async-start | bytes 12582912 | tf_op jit(solution)/shard_map/reduce_scatter | solution.py:56
  45.4 0.7 copy-start.31
  45.5 186.8 %all-gather.11.cloned.1.call-start = ((), (), s32[]{:S(2)}) async-start(), calls=%async_computation.17 | async-start | bytes 4718592 | tf_op jit(solution)/shard_map/all_gather | solution.py:48
  149.3 1.3 copy-start.2
  151.6 13.2 copy-start.3
  152.0 23.0 copy-start.4
  164.8 10.2 copy-start.12
  175.1 12.1 copy-start.14
  187.2 284.1 %reduce-scatter.14.cloned.1.call-start = ((), (), s32[]{:S(2)}) async-start(), calls=%async_computation.18 | async-start | bytes 9437184 | tf_op jit(solution)/shard_map/reduce_scatter | solution.py:52
  239.9 216.7 %all-to-all-start.1 = ((bf16[32,768,384]{1,2,0:T(8,128)(2,1)}), bf16[32,768,384]{1,2,0:T(8,128)(2,1)}, u32[]{:S(2)}, u32[]{:S(2)}) async-start(bf16[32,768,384]{1,2,0:T(8,128)(2,1)} %bitcast.253), calls=%async_computation.3 | async-start | bytes 37748736 | tf_op jit(solution)/shard_map/all_to_all | solution.py:206
  251.5 630.4 %all-gather.17.cloned.1.call-start = ((), (), s32[]{:S(2)}) async-start(), calls=%async_computation.23 | async-start | bytes 4718592 | tf_op jit(solution)/shard_map/all_gather | solution.py:44
  456.6 696.7 %all-to-all-start = ((bf16[32,768,2,384]{3,2,1,0:T(2,128)(2,1)}), bf16[32,768,2,384]{3,2,1,0:T(2,128)(2,1)}, u32[]{:S(2)}, u32[]{:S(2)}) async-start(bf16[32,768,2,384]{3,2,1,0:T(2,128)(2,1)} %param.31), calls=%async_computation.2 | async-start | bytes 75497472 | tf_op jit(solution)/shard_map/all_to_all | solution.py:205
  471.2 423.2 %all-gather.13.cloned.1.call-start = ((), (), s32[]{:S(2)}) async-start(), calls=%async_computation.19 | async-start | bytes 4718592 | tf_op jit(solution)/shard_map/all_gather | solution.py:44
  877.8 4.8 copy-start.26
  877.8 0.6 copy-start.22
  878.4 4.2 copy-start.28
  881.8 217.6 %all-gather.19.cloned.1.call-start = ((), (), s32[]{:S(2)}) async-start(), calls=%async_computation.24 | async-start | bytes 9437184 | tf_op jit(solution)/shard_map/all_gather | solution.py:210
  882.6 321.9 %all-gather.15.cloned.1.call-start = ((), (), s32[]{:S(2)}) async-start(), calls=%async_computation.20 | async-start | bytes 9437184 | tf_op jit(solution)/shard_map/all_gather | solution.py:209
  894.5 619.3 %reduce-scatter.20.cloned.1.call-start = ((), (), s32[]{:S(2)}) async-start(), calls=%async_computation.25 | async-start | bytes 18874368 | tf_op jit(solution)/shard_map/reduce_scatter | solution.py:62
  895.4 45.6 copy-start.29
  1239.4 26.7 copy-start.11
  1368.0 292.4 %reduce-scatter.16.cloned.1.call-start = ((), (), s32[]{:S(2)}) async-start(), calls=%async_computation.21 | async-start | bytes 18874368 | tf_op jit(solution)/shard_map/reduce_scatter | solution.py:62
  1454.1 223.2 %reduce-scatter.22.cloned.1.call-start = ((), (), s32[]{:S(2)}) async-start(), calls=%async_computation.26 | async-start | bytes 9437184 | tf_op jit(solution)/shard_map/reduce_scatter | solution.py:52
  1513.8 163.5 %copy-start.21 = (f32[768]{0:T(1024)S(1)}, f32[768]{0:T(1024)}, u32[]{:S(2)}) copy-start(f32[768]{0:T(1024)} %copy-done.20) | copy-start | bytes 9220
  1513.8 163.5 %copy-start.23 = (f32[1024]{0:T(1024)S(1)}, f32[1024]{0:T(1024)}, u32[]{:S(2)}) copy-start(f32[1024]{0:T(1024)} %copy-done.22) | copy-start | bytes 12292
  1513.8 181.4 %reduce-scatter.18.cloned.1.call-start = ((), (), s32[]{:S(2)}) async-start(), calls=%async_computation.22 | async-start | bytes 9437184 | tf_op jit(solution)/shard_map/reduce_scatter | solution.py:52
  1660.4 25.9 copy-start.27
  1660.5 56.0 %all-gather.21.cloned.1.call-start = ((), (), s32[]{:S(2)}) async-start(), calls=%async_computation.27 | async-start | bytes 4718592 | tf_op jit(solution)/shard_map/all_gather | solution.py:44
  1686.4 30.1 copy-start.36
  1703.0 99.1 %reduce-scatter.24.cloned.1.call-start = ((), (), s32[]{:S(2)}) async-start(), calls=%async_computation.28 | async-start | bytes 9437184 | tf_op jit(solution)/shard_map/reduce_scatter | solution.py:56
  1723.7 0.8 copy-start.13
  1723.7 0.8 copy-start.15
  1723.7 230.4 %all-gather.23.cloned.1.call-start = ((), (), s32[]{:S(2)}) async-start(), calls=%async_computation.29 | async-start | bytes 6291456 | tf_op jit(solution)/shard_map/all_gather | solution.py:48
  1807.0 11.2 copy-start.5
  1861.5 3.1 copy-start.6
  1866.2 1638.4 %all-reduce.3.cloned.1.call-start = ((), (), s32[]{:S(2)}) async-start(), calls=%async_computation.34 | async-start | bytes 4718592
  1938.9 421.8 %all-to-all-start.3 = ((f32[16,1536,384]{2,0,1:T(8,128)}), f32[16,1536,384]{2,0,1:T(8,128)}, u32[]{:S(2)}, u32[]{:S(2)}) async-start(f32[16,1536,384]{2,0,1:T(8,128)} %copy.242), calls=%async_computation.13 | async-start | bytes 75497472 | tf_op jit(solution)/shard_map/all_to_all | solution.py:245
  1953.7 1600.7 %reduce-scatter.28.cloned.1.call-start = ((), (), s32[]{:S(2)}) async-start(), calls=%async_computation.31 | async-start | bytes 3538944 | tf_op jit(solution)/shard_map/reduce_scatter | solution.py:277
  1962.5 1597.5 %reduce-scatter.26.cloned.1.call-start = ((), (), s32[]{:S(2)}) async-start(), calls=%async_computation.30 | async-start | bytes 9437184 | tf_op jit(solution)/shard_map/reduce_scatter | solution.py:52
  1971.0 1642.6 %reduce-scatter.32.cloned.1.call-start = ((), (), s32[]{:S(2)}) async-start(), calls=%async_computation.33 | async-start | bytes 42467328 | tf_op jit(solution)/shard_map/reduce_scatter | solution.py:280
  2397.6 2278.3 %reduce-scatter.30.cloned.1.call-start = ((), (), s32[]{:S(2)}) async-start(), calls=%async_computation.32 | async-start | bytes 84934656 | tf_op jit(solution)/shard_map/reduce_scatter | solution.py:279
  3497.9 0.7 copy-start.37
  3497.9 1.9 copy-start.32
  3498.0 7.8 copy-start.35
  3498.0 7.9 copy-start.10
  3498.0 56.4 %copy-start.7 = (f32[96,1,1024]{2,1,0:T(1,128)S(1)}, f32[96,1,1024]{2,1,0:T(1,128)}, u32[]{:S(2)}) copy-start(f32[96,1,1024]{2,1,0:T(1,128)} %param.36) | copy-start | bytes 1179652
  3498.0 56.4 %copy-start.8 = (f32[96,1,1024]{2,1,0:T(1,128)S(1)}, f32[96,1,1024]{2,1,0:T(1,128)}, u32[]{:S(2)}) copy-start(f32[96,1,1024]{2,1,0:T(1,128)} %param.37) | copy-start | bytes 1179652
  3498.0 56.4 %copy-start.9 = (f32[96,1,1024]{2,1,0:T(1,128)S(1)}, f32[96,1,1024]{2,1,0:T(1,128)}, u32[]{:S(2)}) copy-start(f32[96,1,1024]{2,1,0:T(1,128)} %param.38) | copy-start | bytes 1179652
  3504.6 55.3 %copy-start.17 = (f32[768]{0:T(1024)S(1)}, f32[768]{0:T(1024)}, u32[]{:S(2)}) copy-start(f32[768]{0:T(1024)} %copy-done.16) | copy-start | bytes 9220
  3504.6 55.3 %copy-start.19 = (f32[1024]{0:T(1024)S(1)}, f32[1024]{0:T(1024)}, u32[]{:S(2)}) copy-start(f32[1024]{0:T(1024)} %copy-done.18) | copy-start | bytes 12292
  3556.5 12.3 copy-start.25
  3575.0 38.0 copy-start.30
  3575.0 38.0 copy-start.33
  3575.0 38.0 copy-start.34
  4712.0 17.5 copy-start.1
  4712.0 32.0 slice-start
  4712.0 32.0 slice-start.1
  4729.5 14.5 slice-start.2
Sparse Core Ops, SparseCore 0:
  23.9 13.9 all-gather.8
  45.6 100.4 reduce-scatter.11
  187.3 44.9 all-gather.10
  240.0 14.4 reduce-scatter.13
  259.5 13.5 all-gather.16
  881.9 12.4 all-gather.12
  896.0 81.5 all-gather.18
  979.1 80.3 all-gather.14
  1368.1 145.5 reduce-scatter.19
  1515.9 144.4 reduce-scatter.15
  1662.7 14.4 reduce-scatter.21
  1679.5 15.6 reduce-scatter.17
  1703.1 13.2 all-gather.20
  1723.8 78.2 reduce-scatter.23
  1866.3 56.7 all-gather.22
  1927.6 108.6 all-reduce.2
  2040.3 73.3 reduce-scatter.27
  2116.4 13.8 reduce-scatter.25
  2397.7 605.6 reduce-scatter.31
  3498.1 1177.8 reduce-scatter.29
where the time goes:
time: 4780 us; the launch traced here: 4770 us
  waiting for transfers between devices  2120 us (44%)
  blocking collectives  1370 us (29%)
  local copies, waits for them, and re-layouts  656 us (14%)
  other arithmetic  291 us (6%)
  matrix products  265 us (6%)
    reduce_scatter x1, waiting for transfers between devices, on_device(): lax.psum_scatter(grad_gate_up, 'dp', scatter_dimension=0, tiled=True)  1050 us
    all_to_all x1, blocking collectives, on_device(): lax.all_to_all(local_grad, 'col', split_axis=1, concat_axis=0, tiled=True)  879 us
    psum x4, blocking collectives, col_total(): return lax.psum(jnp.sum(values, axis=1), 'col')  418 us
    all_to_all x1, waiting for transfers between devices, on_device(): lax.all_to_all(down_local_grad, 'col', split_axis=1, concat_axis=0, tiled...  390 us
    reduce_scatter x2, waiting for transfers between devices, wide_sums(): return lax.psum_scatter(values, 'col', scatter_dimension=1, tiled=True)  206 us
    all_to_all x1, waiting for transfers between devices, on_device(): lax.all_to_all(down_turned, 'col', split_axis=0, concat_axis=1, tiled=True)  197 us
    reduce_scatter x2, waiting for transfers between devices, col_sums(): lax.psum_scatter(term_fn(jnp.int32(0), lax.axis_size('col') * rows), 'col...  176 us
    dot_general x1, local copies, waits for them, and re-layouts, on_device(): jnp.einsum('ecd,ecgh->edgh', slot_rows, pair_blocks, preferred_element_ty...  122 us
  transfers between devices with their start and end apart: 23, of which 13 were waited for; matrix products, arithmetic and copies ran while one was open for 17% of the time, Pallas kernels for 0%

commit v1 on v0

v1 whole, which is shorter than its diff:
```python
import functools

import jax
import jax.numpy as jnp
from jax import lax
from jax.experimental import pallas as pl
from jax.experimental.layout import Layout, with_layout_constraint
from jax.experimental.pallas import tpu as pltpu
from jax.sharding import PartitionSpec as P

D = 1536
KVH = 2
HD = 128
E = 32
FFE = 768
TOP = 4
GROUP = 6
LEN = 1024
STEP = 5


EPS_NORM = 1e-06
BETA_ONE = 0.5
BETA_TWO = 0.5
ADAM_EPS = 1e-08
DECAY_RATE = 0.1
TAU_CLIP = 3.0


QUERIES = 256
MIB = 1 << 20


def dot(left, right, left_dim=1, right_dim=0):
    return lax.dot_general(
        left, right, (((left_dim,), (right_dim,)), ((), ())), preferred_element_type=jnp.float32
    )


def pass_on(*refs):
    pass


def after(values, *earlier):
    return pl.pallas_call(
        pass_on,
        in_specs=[pl.BlockSpec(memory_space=pl.ANY)] * (1 + len(earlier)),
        out_specs=pl.BlockSpec(memory_space=pl.ANY),
        out_shape=jax.ShapeDtypeStruct(values.shape, values.dtype),
        input_output_aliases={0: 0},
        cost_estimate=pl.CostEstimate(flops=0, bytes_accessed=0, transcendentals=0),
    )(values, *earlier)


def col_total(values):
    return lax.psum(jnp.sum(values, axis=1), "col")


def butterfly(values, combine, axes):
    for axis in axes:
        count = lax.axis_size(axis)
        bit = 1
        while bit < count:
            pairs = [(i, i ^ bit) for i in range(count)]
            values = combine(values, lax.ppermute(values, axis, pairs))
            bit *= 2
    return values


def norm_backward(values, factor, gain, grad_normed):
    inner = col_total(values * gain[None, :] * grad_normed) / D
    grad_values = (
        factor[:, None] * gain[None, :] * grad_normed - values * (factor**3 * inner)[:, None]
    )
    grad_gain = jnp.sum(grad_normed * values * factor[:, None], axis=0)
    return (grad_values, grad_gain)


def to_owners(values, axes):
    return lax.all_to_all(values, axes, split_axis=0, concat_axis=0, tiled=True)


def slot_ranks(routes, route_gates):
    tokens = routes.shape[1]
    hits = routes[:, None, :] == jnp.arange(E, dtype=jnp.int32)[None, :, None]
    gates = jnp.sum(jnp.where(hits, route_gates[:, None, :], 0.0), axis=0)
    chosen = jnp.any(hits, axis=0)
    lanes = jnp.arange(128)
    upto = (lanes[:, None] <= lanes[None, :]).astype(jnp.bfloat16)
    runs = jnp.einsum(
        "ebt,ts->ebs",
        chosen.reshape(E, tokens // 128, 128).astype(jnp.bfloat16),
        upto,
        preferred_element_type=jnp.float32,
    ).astype(jnp.int32)
    totals = runs[:, :, -1]
    ranks = (runs + (jnp.cumsum(totals, axis=1) - totals)[:, :, None]).reshape(E, tokens) - 1
    return (jnp.where(chosen, ranks, -1), gates)


def key_reach(chunk):
    return min((chunk + 2) * QUERIES, LEN)


def scores_turned(queries, keys, id_row, id_col):
    scores = dot(keys, queries, 1, 1) * HD ** (-0.5)
    return jnp.where(id_col <= id_row, scores, -1e30)


def attend_kernel(query_ref, key_ref, value_ref, id_row_ref, id_col_ref, mixed_ref, log_ref, top_ref):
    value_turned = value_ref[...].T
    for chunk in range(LEN // QUERIES):
        rows = slice(chunk * QUERIES, (chunk + 1) * QUERIES)
        reach = key_reach(chunk)
        masked = scores_turned(
            query_ref[rows, :], key_ref[:reach, :], id_row_ref[:, rows], id_col_ref[:reach, :]
        )
        top = jnp.max(masked, axis=0, keepdims=True)
        weights = jnp.exp(masked - top)
        total = jnp.sum(weights, axis=0, keepdims=True)
        probs = (weights * (1.0 / total)).astype(jnp.bfloat16)
        mixed_ref[rows, :] = dot(value_turned[:, :reach], probs).T.astype(jnp.bfloat16)
        log_ref[0, :, rows] = top + jnp.log(total)
        top_ref[0, :, rows] = top


def attend_forward(packed, blocks):
    head = pl.BlockSpec((LEN, HD), lambda h: (0, h))
    row = pl.BlockSpec((1, 1, LEN), lambda h: (h, 0, 0))
    return pl.pallas_call(
        attend_kernel,
        grid=(GROUP,),
        in_specs=[
            head,
            pl.BlockSpec((LEN, HD), lambda h: (0, GROUP)),
            pl.BlockSpec((LEN, HD), lambda h: (0, GROUP + 1)),
            pl.BlockSpec((1, LEN), lambda h: (0, 0)),
            pl.BlockSpec((LEN, 1), lambda h: (0, 0)),
        ],
        out_specs=[head, row, row],
        out_shape=[
            jax.ShapeDtypeStruct((LEN, GROUP * HD), jnp.bfloat16),
            jax.ShapeDtypeStruct((GROUP, 1, LEN), jnp.float32),
            jax.ShapeDtypeStruct((GROUP, 1, LEN), jnp.float32),
        ],
        compiler_params=pltpu.CompilerParams(vmem_limit_bytes=40 * MIB),
        cost_estimate=pl.CostEstimate(
            flops=4 * GROUP * LEN * LEN * HD, bytes_accessed=4 * MIB, transcendentals=GROUP * LEN * LEN
        ),
    )(packed, packed, packed, blocks[None, :], blocks[:, None])


def attend_back_kernel(
    query_ref, key_ref, value_ref, grad_ref, log_ref, id_row_ref, id_col_ref, out_ref, keys_acc, values_acc
):
    head = pl.program_id(0)

    @pl.when(head == 0)
    def _():
        keys_acc[...] = jnp.zeros_like(keys_acc)
        values_acc[...] = jnp.zeros_like(values_acc)

    key_turned = key_ref[...].T
    for chunk in range(LEN // QUERIES):
        rows = slice(chunk * QUERIES, (chunk + 1) * QUERIES)
        reach = key_reach(chunk)
        queries = query_ref[rows, :]
        grads = grad_ref[rows, :]
        masked = scores_turned(queries, key_ref[:reach, :], id_row_ref[:, rows], id_col_ref[:reach, :])
        probs = jnp.exp(masked - log_ref[0, :, rows])
        grad_probs = dot(value_ref[:reach, :], grads, 1, 1)
        delta = jnp.sum(probs * grad_probs, axis=0, keepdims=True)
        grad_scores = (probs * (grad_probs - delta)).astype(jnp.bfloat16)
        values_acc[:reach, :] += dot(probs.astype(jnp.bfloat16), grads)
        keys_acc[:reach, :] += dot(grad_scores, queries)
        grad_query = dot(key_turned[:, :reach], grad_scores).T * HD ** (-0.5)
        lanes = pl.ds(pl.multiple_of(head * HD, HD), HD)
        out_ref[rows, lanes] = grad_query.astype(jnp.bfloat16)

    @pl.when(head == GROUP - 1)
    def _():
        out_ref[:, GROUP * HD : (GROUP + 1) * HD] = (keys_acc[...] * HD ** (-0.5)).astype(jnp.bfloat16)
        out_ref[:, (GROUP + 1) * HD :] = values_acc[...].astype(jnp.bfloat16)


def attend_backward(packed, blocks, log_total, grad_heads):
    head = pl.BlockSpec((LEN, HD), lambda h: (0, h))
    return pl.pallas_call(
        attend_back_kernel,
        grid=(GROUP,),
        in_specs=[
            head,
            pl.BlockSpec((LEN, HD), lambda h: (0, GROUP)),
            pl.BlockSpec((LEN, HD), lambda h: (0, GROUP + 1)),
            head,
            pl.BlockSpec((1, 1, LEN), lambda h: (h, 0, 0)),
            pl.BlockSpec((1, LEN), lambda h: (0, 0)),
            pl.BlockSpec((LEN, 1), lambda h: (0, 0)),
        ],
        out_specs=pl.BlockSpec((LEN, (GROUP + 2) * HD), lambda h: (0, 0)),
        out_shape=jax.ShapeDtypeStruct((LEN, (GROUP + 2) * HD), jnp.bfloat16),
        scratch_shapes=[pltpu.VMEM((LEN, HD), jnp.float32)] * 2,
        compiler_params=pltpu.CompilerParams(vmem_limit_bytes=40 * MIB),
        cost_estimate=pl.CostEstimate(
            flops=10 * GROUP * LEN * LEN * HD, bytes_accessed=6 * MIB, transcendentals=GROUP * LEN * LEN
        ),
    )(packed, packed, packed, grad_heads, log_total, blocks[None, :], blocks[:, None])


def expert_kernel(col_n, rows_ref, grads_ref, gate_ref, in_ref, down_ref, back_ref, weighted_ref, pair_ref):
    gate_up = dot(rows_ref[0, 0], in_ref[0])
    grad_weighted = dot(grads_ref[0, 0], down_ref[0], 1, 1)
    for c in range(1, col_n):
        gate_up += dot(rows_ref[0, c], in_ref[c])
        grad_weighted += dot(grads_ref[0, c], down_ref[c], 1, 1)
    gate_half, up_half, scale = gate_up[:, :FFE], gate_up[:, FFE:], gate_ref[0]
    sigmoid_gate = jax.nn.sigmoid(gate_half)
    silu_gate = gate_half * sigmoid_gate
    weighted_ref[0] = (silu_gate * up_half * scale).astype(jnp.bfloat16)
    grad_act = grad_weighted * scale
    grad_gate = grad_act * up_half * sigmoid_gate * (1.0 + gate_half * (1.0 - sigmoid_gate))
    pair_ref[0, :, :FFE] = grad_gate.astype(jnp.bfloat16)
    pair_ref[0, :, FFE:] = (grad_act * silu_gate).astype(jnp.bfloat16)
    for c in range(col_n):
        back_ref[0, c] = dot(pair_ref[0], in_ref[c], 1, 1).astype(jnp.bfloat16)


def expert_passes(slot_rows, slot_grads, gates, weights_in, weights_down):
    dl_n, col_n, slots, width = slot_rows.shape
    block = pl.BlockSpec((1, col_n, slots, width), lambda d: (d, 0, 0, 0))
    return pl.pallas_call(
        functools.partial(expert_kernel, col_n),
        grid=(dl_n,),
        in_specs=[
            block,
            block,
            pl.BlockSpec((1, slots, 1), lambda d: (d, 0, 0)),
            pl.BlockSpec(weights_in.shape, lambda d: (0, 0, 0)),
            pl.BlockSpec(weights_down.shape, lambda d: (0, 0, 0)),
        ],
        out_specs=[
            block,
            pl.BlockSpec((1, slots, FFE), lambda d: (d, 0, 0)),
            pl.BlockSpec((1, slots, 2 * FFE), lambda d: (d, 0, 0)),
        ],
        out_shape=[
            jax.ShapeDtypeStruct(slot_rows.shape, jnp.bfloat16),
            jax.ShapeDtypeStruct((dl_n, slots, FFE), jnp.bfloat16),
            jax.ShapeDtypeStruct((dl_n, slots, 2 * FFE), jnp.bfloat16),
        ],
        compiler_params=pltpu.CompilerParams(vmem_limit_bytes=56 * MIB),
        cost_estimate=pl.CostEstimate(
            flops=10 * dl_n * slots * D * FFE, bytes_accessed=30 * MIB, transcendentals=dl_n * slots * FFE
        ),
    )(slot_rows, slot_grads, gates, weights_in, weights_down)


def join_kernel(row_n, col_n, place_ref, *refs):
    count = row_n * col_n
    in_refs, down_refs, (in_out, down_out) = refs[:count], refs[count : 2 * count], refs[2 * count :]
    part = FFE // row_n
    for k in range(count):
        r = lax.rem(place_ref[0] + k // col_n, row_n)
        c = lax.rem(place_ref[1] + k % col_n, col_n)
        for g in range(2):
            lanes = pl.ds(pl.multiple_of(g * FFE + r * part, 128), part)
            in_out[c, :, lanes] = in_refs[k][g]
        down_out[c, pl.ds(pl.multiple_of(r * part, 128), part), :] = down_refs[k][...]


def join_weights(in_pieces, down_pieces, place, row_n, col_n):
    width = in_pieces[0].shape[1]
    return pl.pallas_call(
        functools.partial(join_kernel, row_n, col_n),
        in_specs=[pl.BlockSpec(memory_space=pltpu.SMEM)]
        + [pl.BlockSpec(memory_space=pltpu.VMEM)] * (2 * row_n * col_n),
        out_specs=[pl.BlockSpec(memory_space=pltpu.VMEM)] * 2,
        out_shape=[
            jax.ShapeDtypeStruct((col_n, width, 2 * FFE), jnp.bfloat16),
            jax.ShapeDtypeStruct((col_n, FFE, width), jnp.bfloat16),
        ],
        compiler_params=pltpu.CompilerParams(vmem_limit_bytes=40 * MIB),
        cost_estimate=pl.CostEstimate(flops=0, bytes_accessed=14 * MIB, transcendentals=0),
    )(place, *in_pieces, *down_pieces)


def halves(steps, sets):
    return [lambda d, number=number: jnp.clip(d - number * steps, 0, steps - 1) for number in range(sets)]


def expert_out_kernel(sets, steps, down_ref, *refs):
    out_ref = refs[sets]
    for number in range(sets):

        @pl.when(pl.program_id(0) // steps == number)
        def _():
            blocks, slots, _ = refs[number].shape
            weighted = refs[number][...].reshape(blocks * slots, FFE)
            for c in range(down_ref.shape[0]):
                slot_out = dot(weighted, down_ref[c]).astype(jnp.bfloat16)
                out_ref[:, c, 0] = slot_out.reshape(blocks, slots, -1)


def expert_outputs(weighted, weights_down):
    dl_n, slots, _ = weighted[0].shape
    col_n, _, width = weights_down.shape
    sets = len(weighted)
    blocks = 2 if dl_n % 2 == 0 else 1
    steps = dl_n // blocks
    return pl.pallas_call(
        functools.partial(expert_out_kernel, sets, steps),
        grid=(sets * steps,),
        in_specs=[pl.BlockSpec(weights_down.shape, lambda d: (0, 0, 0))]
        + [
            pl.BlockSpec((blocks, slots, FFE), lambda d, at=at: (at(d), 0, 0)) for at in halves(steps, sets)
        ],
        out_specs=pl.BlockSpec(
            (blocks, col_n, 1, slots, width), lambda d: (lax.rem(d, steps), 0, d // steps, 0, 0)
        ),
        out_shape=jax.ShapeDtypeStruct((dl_n, col_n, sets, slots, width), jnp.bfloat16),
        compiler_params=pltpu.CompilerParams(vmem_limit_bytes=40 * MIB),
        cost_estimate=pl.CostEstimate(
            flops=2 * sets * dl_n * slots * D * FFE, bytes_accessed=14 * MIB, transcendentals=0
        ),
    )(weights_down, *weighted)


def expert_grad_kernel(row_n, sets, steps, *refs):
    part = FFE // row_n
    step = pl.program_id(1)
    in_grad_ref, down_grad_ref, in_acc, down_acc = refs[4 * sets :]

    @pl.when(step == 0)
    def _():
        in_acc[...] = jnp.zeros_like(in_acc)
        down_acc[...] = jnp.zeros_like(down_acc)

    for number in range(sets):
        rows_ref, grads_ref, weighted_ref, pair_ref = refs[4 * number : 4 * number + 4]

        @pl.when(step // steps == number)
        def _():
            blocks, _, slots, width = rows_ref.shape
            weighted = weighted_ref[...].reshape(blocks * slots, FFE)
            pair = pair_ref[...].reshape(blocks * slots, 2 * FFE)
            rows = rows_ref[...].reshape(blocks * slots, width)
            grads = grads_ref[...].reshape(blocks * slots, width)
            in_acc[...] += dot(rows, pair, 0, 0)
            down_acc[...] += dot(weighted, grads, 0, 0)

    @pl.when(step == sets * steps - 1)
    def _():
        for r in range(row_n):
            for g in range(2):
                lanes = slice(g * FFE + r * part, g * FFE + (r + 1) * part)
                in_grad_ref[r, 0, g] = in_acc[:, lanes].astype(jnp.bfloat16)
            down_grad_ref[r, 0] = down_acc[r * part : (r + 1) * part, :].astype(jnp.bfloat16)


def expert_grads(sources, row_n):
    dl_n, col_n, slots, width = sources[0][0].shape
    sets = len(sources)
    blocks = 2 if dl_n % 2 == 0 else 1
    steps = dl_n // blocks
    part = FFE // row_n
    in_specs = []
    for at in halves(steps, sets):
        block = pl.BlockSpec((blocks, 1, slots, width), lambda c, d, at=at: (at(d), c, 0, 0))
        in_specs += [
            block,
            block,
            pl.BlockSpec((blocks, slots, FFE), lambda c, d, at=at: (at(d), 0, 0)),
            pl.BlockSpec((blocks, slots, 2 * FFE), lambda c, d, at=at: (at(d), 0, 0)),
        ]
    return pl.pallas_call(
        functools.partial(expert_grad_kernel, row_n, sets, steps),
        grid=(col_n, sets * steps),
        in_specs=in_specs,
        out_specs=[
            pl.BlockSpec((row_n, 1, 2, width, part), lambda c, d: (0, c, 0, 0, 0)),
            pl.BlockSpec((row_n, 1, part, width), lambda c, d: (0, c, 0, 0)),
        ],
        out_shape=[
            jax.ShapeDtypeStruct((row_n, col_n, 2, width, part), jnp.bfloat16),
            jax.ShapeDtypeStruct((row_n, col_n, part, width), jnp.bfloat16),
        ],
        scratch_shapes=[
            pltpu.VMEM((width, 2 * FFE), jnp.float32),
            pltpu.VMEM((FFE, width), jnp.float32),
        ],
        compiler_params=pltpu.CompilerParams(vmem_limit_bytes=58 * MIB),
        cost_estimate=pl.CostEstimate(
            flops=6 * sets * dl_n * slots * D * FFE, bytes_accessed=50 * MIB, transcendentals=0
        ),
    )(*[array for source in sources for array in source])


def adam_step(master, moment_one, moment_two, gradient, rate, decay):
    first = BETA_ONE * moment_one + (1.0 - BETA_ONE) * gradient
    second = BETA_TWO * moment_two + (1.0 - BETA_TWO) * gradient * gradient
    first_hat = first / (1.0 - BETA_ONE**STEP)
    second_hat = second / (1.0 - BETA_TWO**STEP)
    updated = master - rate * (first_hat / (jnp.sqrt(second_hat) + ADAM_EPS) + decay * master)
    return (updated, first, second)


def on_device(
    tokens,
    cotangent,
    routes,
    route_gates,
    block_ids,
    w_qkv,
    w_out,
    w_gate_up,
    w_down,
    gains,
    gain_first,
    gain_second,
    qkv_master,
    qkv_first,
    qkv_second,
    out_master,
    out_first,
    out_second,
    gate_up_master,
    gate_up_first,
    gate_up_second,
    down_master,
    down_first,
    down_second,
):
    dh_n, dl_n, row_n, col_n = (lax.axis_size(name) for name in ("dh", "dl", "row", "col"))
    dh_i, dl_i, row_i, col_i = (lax.axis_index(name) for name in ("dh", "dl", "row", "col"))
    dp_n = dh_n * dl_n
    grid_n = row_n * col_n
    width = w_qkv.shape[0]
    token_block = routes.shape[1]
    capacity = 5 * token_block * TOP // (4 * E)
    tokens_row = token_block // row_n
    seqs_row = tokens_row // LEN
    assert seqs_row * KVH == col_n and KVH == row_n
    seq_i, group_i = col_i // KVH, col_i % KVH
    experts_dp = E // dp_n
    share = grid_n // experts_dp
    assert share * experts_dp == grid_n
    slots = capacity // share
    low = jnp.bfloat16

    def far_pairs():
        return [(i, dh_n - 1 - i) for i in range(dh_n)]

    def from_far(values):
        both = lax.all_gather(values, "dh", axis=0)
        return lax.dynamic_index_in_dim(both, dh_n - 1 - dh_i, 0, False)

    def ring(values, axis):
        count = lax.axis_size(axis)
        moved = [values]
        for k in range(1, count):
            moved.append(lax.ppermute(values, axis, [(i, (i - k) % count) for i in range(count)]))
        return moved

    def row_blocks(values):
        return jnp.concatenate(ring(values, "row"), axis=0)

    inputs = tokens.reshape(tokens_row, width).astype(jnp.float32)
    qkv_row = lax.all_gather(w_qkv.reshape(width, -1), "row", axis=0)
    factor_one = lax.rsqrt(col_total(inputs * inputs) / D + EPS_NORM)
    far_routes = lax.ppermute(routes, "dh", far_pairs())
    far_gates = lax.ppermute(route_gates, "dh", far_pairs())
    ids = jnp.concatenate(ring(block_ids, "col"), axis=0)
    normed_one = (inputs * factor_one[:, None] * gains[0][None, :]).astype(low)
    normed_one = after(normed_one, far_routes, far_gates, ids)
    terms = jnp.einsum(
        "stf,gfh->sgth",
        normed_one.reshape(seqs_row, LEN, width),
        qkv_row,
        preferred_element_type=jnp.float32,
    )
    terms = terms.astype(low).reshape(col_n * LEN, -1)
    packed = lax.psum_scatter(terms, "col", scatter_dimension=0, tiled=True)

    ids = lax.dynamic_index_in_dim(ids, (row_i * seqs_row + seq_i - col_i) % col_n, 0, False)

    ranks, gates = slot_ranks(routes, route_gates)
    far_ranks, far_gates = slot_ranks(far_routes, far_gates)
    offsets = (jnp.arange(share) * slots).astype(jnp.int32)

    def unit_grid(values):
        values = values.reshape(dh_n, dl_n, row_n, col_n, token_block)
        return jnp.roll(values, -row_i * tokens_row, axis=-1)

    def unit_slots(ranks):
        return unit_grid(ranks[:, None, :] - offsets[None, :, None])

    def near(values):
        values = lax.dynamic_index_in_dim(values, dh_i, 0, False)
        return lax.dynamic_index_in_dim(values, row_i, 1, False)

    def here(values):
        return lax.dynamic_index_in_dim(values, col_i, 1, False)

    def unit_gates(gates):
        return here(near(unit_grid(jnp.broadcast_to(gates[:, None, :], (E, share, token_block)))))

    all_ranks = unit_slots(ranks)
    unit_ranks = [near(all_ranks), near(unit_slots(far_ranks))]
    here_ranks = [here(values) for values in unit_ranks]
    here_gates = [unit_gates(gates), unit_gates(far_gates)]

    def hot(number, start=0, count=token_block):
        chosen = unit_ranks[number][:, :, None, start : start + count]
        return chosen == jnp.arange(slots, dtype=jnp.int32)[None, None, :, None]

    def dispatch(number, rows):
        picked = jnp.einsum(
            "dcst,tf->dcsf", hot(number).astype(low), rows, preferred_element_type=jnp.float32
        )
        return picked.astype(low).reshape(dl_n * col_n, slots, width)

    def to_experts(values):
        return to_owners(values, ("dl", "col")).reshape(dl_n, col_n, slots, width)

    def token_sums(number, values):
        values = values.reshape(dl_n, col_n, slots, width)
        total = None
        for k in range(1, row_n):
            chosen = hot(number, k * tokens_row, tokens_row).astype(low)
            part = jnp.einsum("dcst,dcsf->tf", chosen, values, preferred_element_type=jnp.float32)
            values = after(values, part)
            part = lax.ppermute(part, "row", [(i, (i + k) % row_n) for i in range(row_n)])
            total = part if total is None else total + part
        chosen = hot(number, 0, tokens_row).astype(low)
        own = jnp.einsum("dcst,dcsf->tf", chosen, values, preferred_element_type=jnp.float32)
        return own + total

    def here_hot(number):
        return here_ranks[number][:, None, :] == jnp.arange(slots, dtype=jnp.int32)[None, :, None]

    slot_gate = jnp.stack(
        [
            jnp.sum(jnp.where(here_hot(number), here_gates[number][:, None, :], 0.0), axis=-1)
            for number in range(2)
        ],
        axis=1,
    )

    start = (dh_i * dl_n + dl_i) * experts_dp
    experts_in = jnp.swapaxes(lax.dynamic_slice_in_dim(w_gate_up, start, experts_dp, 0), 1, 2)
    in_pieces, down_pieces, piece_pairs = [], [], []
    for k in range(grid_n):
        kr, kc = k // col_n, k % col_n
        target = (((row_i - kr) % row_n) * col_n + (col_i - kc) % col_n) // share
        in_pieces.append(lax.dynamic_index_in_dim(experts_in, target, 0, False))
        down_pieces.append(lax.dynamic_index_in_dim(w_down, start + target, 0, False))
        piece_pairs.append(
            [
                (r * col_n + c, ((r - kr) % row_n) * col_n + (c - kc) % col_n)
                for r in range(row_n)
                for c in range(col_n)
            ]
        )

    grad_rows = cotangent.reshape(tokens_row, width)
    grad_low = grad_rows.astype(low)
    far_low = to_owners(jnp.broadcast_to(grad_low, (dh_n,) + grad_low.shape), "dh")

    def all_features(values):
        values = jnp.roll(jnp.stack(ring(values, "col")), col_i, axis=0)
        return values

    def all_rows(values):
        return jnp.concatenate(ring(values, "row"), axis=1)

    def dispatch_wide(number, rows):
        picked = jnp.einsum(
            "dst,ctf->dcsf", here_hot(number).astype(low), rows, preferred_element_type=jnp.float32
        )
        return picked.astype(low)

    own_wide = ring(after(grad_low, factor_one), "col")
    own_wide[-1] = after(own_wide[-1], terms, slot_gate, *here_ranks, *unit_ranks)
    own_wide = jnp.roll(jnp.stack(own_wide), col_i, axis=0)
    own_picked = dispatch_wide(0, all_rows(own_wide))
    own_grads = to_owners(after(own_picked, far_low), "dl")
    my_gate = to_owners(after(slot_gate, own_grads), "dl")
    my_gate = jnp.swapaxes(my_gate, 0, 1)[..., None]
    far_low = lax.dynamic_index_in_dim(far_low, dh_n - 1 - dh_i, 0, False)
    far_wide = all_features(far_low)

    packed = after(packed, own_picked)
    mixed, log_total, tops = attend_forward(packed, ids)
    heads = lax.all_gather(mixed, "col", axis=0)
    heads = after(heads, own_grads, *in_pieces, *down_pieces).reshape(seqs_row, KVH, LEN, GROUP * HD)
    out_row = lax.all_gather(after(w_out[0], packed), "row", axis=0)
    attn = jnp.einsum("sgth,ghf->stf", heads, out_row, preferred_element_type=jnp.float32)
    hidden = inputs + attn.reshape(tokens_row, width)

    factor_two = lax.rsqrt(col_total(hidden * hidden) / D + EPS_NORM)
    normed_two = (hidden * factor_two[:, None] * gains[1][None, :]).astype(low)
    far_two = from_far(normed_two)
    far_picked = dispatch_wide(1, all_rows(after(far_wide, normed_two)))
    far_grads = to_owners(after(far_picked, my_gate), "dl")

    def spread(piece, pairs):
        return lax.ppermute(after(piece, normed_two), ("row", "col"), pairs)

    for k in range(1, grid_n):
        down_pieces[k] = spread(down_pieces[k], piece_pairs[k])
        in_pieces[k] = spread(in_pieces[k], piece_pairs[k])
    weights_in, weights_down = join_weights(
        in_pieces, down_pieces, jnp.stack([row_i, col_i]).astype(jnp.int32), row_n, col_n
    )
    far_two = after(far_two, weights_in)
    far_slots = dispatch(1, row_blocks(far_two))
    far_rows = to_experts(after(far_slots, far_grads))
    own_slots = dispatch(0, after(row_blocks(normed_two), far_slots))
    own_rows = to_experts(after(own_slots, far_rows))

    far_back, far_weighted, far_pair = expert_passes(
        far_rows, far_grads, my_gate[1], weights_in, weights_down
    )
    own_back, own_weighted, own_pair = expert_passes(
        after(own_rows, far_back), own_grads, my_gate[0], weights_in, weights_down
    )

    def send_back(values):
        return to_owners(values.reshape(dl_n * col_n, slots, width), ("dl", "col"))

    far_back = send_back(after(far_back, own_rows))
    slot_out = expert_outputs([own_weighted, far_weighted], weights_down)
    own_back = send_back(after(own_back, far_back))
    far_sums = token_sums(1, after(far_back, slot_out)).astype(low)
    in_grad, down_grad = expert_grads(
        [
            (own_rows, own_grads, after(own_weighted, far_sums), own_pair),
            (far_rows, far_grads, far_weighted, far_pair),
        ],
        row_n,
    )
    far_sums = from_far(far_sums)
    own_back = after(own_back, in_grad)
    own_sums = token_sums(0, own_back)
    grad_normed_two = own_sums + far_sums.astype(jnp.float32)
    slot_out = to_owners(after(slot_out, own_back).reshape((dl_n * col_n,) + slot_out.shape[2:]), ("dl", "col"))

    def block_grads(grads):
        grads = to_owners(grads.reshape((grid_n,) + grads.shape[2:]), ("row", "col"))
        if share > 1:
            grads = grads.astype(jnp.float32)
            grads = jnp.sum(grads.reshape((experts_dp, share) + grads.shape[1:]), axis=1)
        return grads

    grad_hidden_norm, grad_gain_two = norm_backward(hidden, factor_two, gains[1], grad_normed_two)
    grad_hidden = grad_rows + grad_hidden_norm
    grad_attn = grad_hidden.astype(low)
    terms = jnp.einsum(
        "stf,ghf->sgth",
        grad_attn.reshape(seqs_row, LEN, width),
        out_row,
        preferred_element_type=jnp.float32,
    )
    terms = terms.astype(low).reshape(col_n * LEN, -1)
    grad_heads = lax.psum_scatter(terms, "col", scatter_dimension=0, tiled=True)
    full_top = jnp.full((KVH, GROUP), -1e30, jnp.float32)
    full_top = lax.dynamic_update_slice(
        full_top, jnp.max(tops, axis=(1, 2))[None], (group_i, jnp.zeros((), jnp.int32))
    )
    own_out, far_out = slot_out[:, 0], slot_out[:, 1]
    far_out_sums = token_sums(1, after(far_out, terms)).astype(low)
    down_grad = after(down_grad, grad_heads)
    grad_heads = after(grad_heads, far_out_sums)
    grad_packed = attend_backward(packed, ids, log_total, grad_heads)
    packed_all = lax.all_gather(grad_packed, "col", axis=0).reshape(seqs_row, KVH, LEN, -1)

    own_out_sums = token_sums(0, after(own_out, grad_packed))
    packed_all = after(packed_all, own_out_sums)
    far_out_sums = lax.ppermute(far_out_sums, "dh", far_pairs())
    block_output = hidden + own_out_sums + far_out_sums.astype(jnp.float32)

    def owner_sums(left, right):
        columns = right.shape[-1]

        def term(k):
            group = lax.dynamic_index_in_dim(right, (row_i + k) % row_n, 1, False)
            return jnp.einsum("stf,sth->fh", left, group, preferred_element_type=jnp.float32)

        total = None
        for k in range(1, row_n):
            part = term(k)
            left = after(left, part)
            part = lax.ppermute(part, "row", [(i, (i + k) % row_n) for i in range(row_n)])
            total = part if total is None else total + part
        total = (term(0) + total).astype(low)
        total = to_owners(total, ("dh", "dl")).reshape(dp_n, -1, columns)
        return jnp.sum(total.astype(jnp.float32), axis=0)

    grad_normed_one = jnp.einsum(
        "sgth,gfh->stf", packed_all, qkv_row, preferred_element_type=jnp.float32
    ).reshape(tokens_row, width)
    grad_out = owner_sums(grad_attn.reshape(seqs_row, LEN, width), after(heads, grad_heads))
    grad_gate_up = block_grads(after(in_grad, packed_all))
    grad_qkv = owner_sums(normed_one.reshape(seqs_row, LEN, width), packed_all)
    grad_down = block_grads(down_grad)
    grad_gate_up = jnp.swapaxes(grad_gate_up, 1, 2)
    grad_gate_up = with_layout_constraint(grad_gate_up, Layout((0, 1, 2, 3)))
    grad_out, grad_qkv = grad_out.T[None], grad_qkv[:, None]
    grad_input_norm, grad_gain_one = norm_backward(inputs, factor_one, gains[0], grad_normed_one)
    input_grad = grad_hidden + grad_input_norm

    full_top = butterfly(after(full_top, packed_all), jnp.maximum, ("col",))

    tops_row = jnp.pad(full_top.reshape(1, -1), ((0, 0), (0, width - KVH * GROUP)))
    small = jnp.concatenate([grad_gain_one[None], grad_gain_two[None], tops_row])

    def combine(left, right):
        return jnp.concatenate([left[:2] + right[:2], jnp.maximum(left[2:], right[2:])])

    small = butterfly(small, combine, ("row", "dh", "dl"))
    grad_gains, head_top = small[:2], small[2, : KVH * GROUP].reshape(KVH, GROUP)

    factors = TAU_CLIP / jnp.maximum(head_top, TAU_CLIP)
    local_factors = lax.dynamic_slice_in_dim(factors, row_i, 1, 0)
    query_scale = jnp.repeat(jnp.sqrt(local_factors), HD, axis=1)
    key_scale = jnp.repeat(jnp.sqrt(jnp.min(local_factors, axis=1, keepdims=True)), HD, axis=1)
    column_scale = jnp.concatenate([query_scale, key_scale, jnp.ones_like(key_scale)], axis=1)
    qkv_new, qkv_one, qkv_two = adam_step(
        qkv_master, qkv_first, qkv_second, grad_qkv, D ** (-0.5), DECAY_RATE
    )
    qkv_new = qkv_new * column_scale[None]
    out_new, out_one, out_two = adam_step(
        out_master, out_first, out_second, grad_out, max(D // 192, 1) ** (-0.5), DECAY_RATE
    )
    gate_up_new, gate_up_one, gate_up_two = adam_step(
        gate_up_master, gate_up_first, gate_up_second, grad_gate_up, D ** (-0.5), DECAY_RATE
    )
    down_new, down_one, down_two = adam_step(
        down_master, down_first, down_second, grad_down, FFE ** (-0.5), DECAY_RATE
    )
    gains_new, gains_one, gains_two = adam_step(
        gains, gain_first, gain_second, grad_gains, 0.2, 0.0
    )
    return (
        block_output.reshape(1, -1, 2 * width),
        input_grad.reshape(1, -1, 2 * width),
        qkv_new,
        qkv_one,
        qkv_two,
        qkv_new.astype(jnp.bfloat16),
        out_new,
        out_one,
        out_two,
        out_new.astype(jnp.bfloat16),
        gate_up_new,
        gate_up_one,
        gate_up_two,
        gate_up_new.astype(jnp.bfloat16),
        down_new,
        down_one,
        down_two,
        down_new.astype(jnp.bfloat16),
        gains_new,
        gains_one,
        gains_two,
        factors.reshape(-1),
    )


def solution(mesh):
    devices = mesh.devices
    devices = devices.reshape((2, devices.shape[0] // 2) + devices.shape[1:])
    mesh = jax.sharding.Mesh(devices, ("dh", "dl", "row", "col"))
    dp = ("dh", "dl")
    in_specs = (
        P("col", (*dp, "row"), None),
        P("col", (*dp, "row"), None),
        P(None, dp),
        P(None, dp),
        P((*dp, "col"), None),
        P("col", "row", None),
        P("row", None, "col"),
        P(None, "col", None, "row"),
        P(None, "row", "col"),
        P(None, "col"),
        P(None, "col"),
        P(None, "col"),
        P(("col", *dp), "row", None),
        P(("col", *dp), "row", None),
        P(("col", *dp), "row", None),
        P("row", None, ("col", *dp)),
        P("row", None, ("col", *dp)),
        P("row", None, ("col", *dp)),
        P(dp, "col", None, "row"),
        P(dp, "col", None, "row"),
        P(dp, "col", None, "row"),
        P(dp, "row", "col"),
        P(dp, "row", "col"),
        P(dp, "row", "col"),
    )
    out_specs = (
        P("col", (*dp, "row"), None),
        P("col", (*dp, "row"), None),
        P(("col", *dp), "row", None),
        P(("col", *dp), "row", None),
        P(("col", *dp), "row", None),
        P(("col", *dp), "row", None),
        P("row", None, ("col", *dp)),
        P("row", None, ("col", *dp)),
        P("row", None, ("col", *dp)),
        P("row", None, ("col", *dp)),
        P(dp, "col", None, "row"),
        P(dp, "col", None, "row"),
        P(dp, "col", None, "row"),
        P(dp, "col", None, "row"),
        P(dp, "row", "col"),
        P(dp, "row", "col"),
        P(dp, "row", "col"),
        P(dp, "row", "col"),
        P(None, "col"),
        P(None, "col"),
        P(None, "col"),
        P(),
    )
    return jax.shard_map(
        on_device, mesh=mesh, in_specs=in_specs, out_specs=out_specs, check_vma=False
    )
```

time: 4780 us -> 1100 us (0.23)
  waiting for transfers between devices: 2120 us -> 445 us
  blocking collectives: 1370 us -> 32.4 us
  local copies, waits for them, and re-layouts: 656 us -> 119 us
  other arithmetic: 291 us -> 110 us
  Pallas kernels: 0 us -> 126 us
  matrix products: 265 us -> 158 us
    reduce_scatter x11 -> x2, waiting for transfers between devices: 1460 us -> 23.7 us  [the longest x1 23.7 us: on_device(): grad_heads = lax.psum_scatter(terms, 'col', scatter_dimension=0, tiled=True)]
    all_to_all x1, blocking collectives: 879 us -> 9.05 us  [to_owners(): return lax.all_to_all(values, axes, split_axis=0, concat_axis=0, tiled=True)]
    all_to_all x3 -> x12, waiting for transfers between devices: 587 us -> 144 us  [to_owners(): return lax.all_to_all(values, axes, split_axis=0, concat_axis=0, tiled=True)]
    psum x4, blocking collectives: 418 us -> 23.4 us  [col_total(): return lax.psum(jnp.sum(values, axis=1), 'col')]
    ppermute x0 -> x27, waiting for transfers between devices: none -> 183 us  [the longest x6 72.8 us: spread(): return lax.ppermute(after(piece, normed_two), ('row', 'col'), pairs)]
    all_to_all x5 -> x0, local copies, waits for them, and re-layouts: 176 us -> none  [the longest x1 63.3 us: on_device(): lax.all_to_all(local_grad, 'col', split_axis=1, concat_axis=0, tiled=True)]
    gather x6 -> x0, local copies, waits for them, and re-layouts: 162 us -> none  [the longest x1 45.5 us: slot_table(): ranked = pairs[order]]
    dot_general x2, local copies, waits for them, and re-layouts: 157 us -> 1.95 us  [slot_ranks(): jnp.einsum('ebt,ts->ebs', chosen.reshape(E, tokens // 128, 128).astype(jn...]
  transfers between devices with their start and end apart: 23 -> 47, of which waited for: 13 -> 21; matrix products, arithmetic and copies ran while one was open for 17% -> 30% of each run, Pallas kernels for 0% -> 12%
where the time goes in v1:
time: 1100 us; the launch traced here: 1090 us
  waiting for transfers between devices  445 us (40%)
  matrix products  158 us (14%)
  Pallas kernels  126 us (11%)
  local copies, waits for them, and re-layouts  119 us (11%)
  other arithmetic  110 us (10%)
  starting transfers between devices  88 us (8%)
  blocking collectives  32.4 us (3%)
  between operations  16.4 us (1%)
    all_to_all x12, waiting for transfers between devices, to_owners(): return lax.all_to_all(values, axes, split_axis=0, concat_axis=0, tiled=True)  144 us
    all_gather x2, waiting for transfers between devices, from_far(): both = lax.all_gather(values, 'dh', axis=0)  73.6 us
    ppermute x6, waiting for transfers between devices, spread(): return lax.ppermute(after(piece, normed_two), ('row', 'col'), pairs)  72.8 us
    all_to_all x12, starting transfers between devices, to_owners(): return lax.all_to_all(values, axes, split_axis=0, concat_axis=0, tiled=True)  66.4 us
    dot_general x8, matrix products, token_sums(): jnp.einsum('dcst,dcsf->tf', chosen, values, preferred_element_type=jnp.fl...  65.5 us
    ppermute x7, waiting for transfers between devices, ring(): lax.ppermute(values, axis, [(i, (i - k) % count) for i in range(count)])  61.3 us
    unnamed x151, local copies, waits for them, and re-layouts  51.2 us
    pallas_call x2, Pallas kernels, expert_passes(): pl.pallas_call(functools.partial(expert_kernel, col_n), grid=(dl_n,), in_...  42.9 us
  transfers between devices with their start and end apart: 47, of which 21 were waited for; matrix products, arithmetic and copies ran while one was open for 30% of the time, Pallas kernels for 12%

profile of v1, /device:TPU:0, one launch (start us, length us, event | category | flops | bytes accessed | tf_op | source)
XLA Modules:
  0.0 1094.4 jit_solution(4967042738441078488)
XLA Ops:
  18.0 5.3 reshape.297
  26.7 4.9 psum.28
  55.1 7.8 convolution_convert_fusion
  73.7 5.1 fusion.46
  84.9 10.8 convert_bitcast_fusion.1.refs_1_
  99.5 55.0 %all-to-all-done.refs_1_ = bf16[2,1024,768]{2,1,0:T(8,128)(2,1)S(1)} async-done(((bf16[2,1024,768]{2,1,0:T(8,128)(2,1)}), bf16[2,1024,768]{2,1,0:T(8,128)(2,1)S(1)}, u32[]{:S(2)}, u32[]{:S(2)}) %all-to-all-start) | async-done | bytes 3145760 | tf_op jit(solution)/shard_map/all_to_all | solution.py:80
  156.2 4.8 all-to-all-start.1
  164.5 20.0 %shard_map.403 = (bf16[1024,768]{1,0:T(8,128)(2,1)}, f32[6,1,1024]{2,1,0:T(1,128)S(1)}, f32[6,1,1024]{2,1,0:T(1,128)S(1)}) custom-call(bf16[1024,1024]{1,0:T(8,128)(2,1)S(1)} %copy-done.3, bf16[1024,1024]{1,0:T(8,128)(2,1)S(1)} %copy-done.3, bf16[1024,1024]{1,0:T(8,128)(2,1)S(1)} %copy-done.3, s32[1,1024]{1,0:T(1,128)S(1)} %fusion.130.id_row_ref, ...), custom_call_target="tpu_custom_call" | custom-call | flops 3221225472 | bytes 4194304 | tf_op jit(solution)/shard_map/pallas_call | solution.py:130
  193.6 5.0 constant_dynamic-slice_fusion.2
  202.2 52.9 %collective-permute-done.13 = bf16[1024,768]{1,0:T(8,128)(2,1)} collective-permute-done((bf16[1024,768]{1,0:T(8,128)(2,1)}, bf16[1024,768]{1,0:T(8,128)(2,1)}, u32[]{:S(2)}, u32[]{:S(2)}) %collective-permute-start.13) | collective-permute-done | bytes 1572896 | tf_op jit(solution)/shard_map/ppermute | solution.py:461
  255.1 5.2 fusion.43.refs_0_
  260.3 10.8 all-gather.17.cloned.1.call-done
  271.0 7.1 multiply_reduce_fusion.2
  278.1 4.9 psum.29
  287.1 9.1 all_to_all.73
  297.7 11.4 %convert_bitcast_fusion.refs_0_ = bf16[4,2,320,768]{3,2,1,0:T(8,128)(2,1)} fusion(s32[4,2048]{1,0:T(4,128)S(1)} %bitcast.321, bf16[2,1024,768]{2,1,0:T(8,128)(2,1)} %collective-permute-done.14, bf16[2,1024,768]{2,1,0:T(8,128)(2,1)S(1)} %copy-done.32), kind=kOutput, calls=%fused_computation.69 | convolution fusion | flops 8070234112 | bytes 10256384 | tf_op jit(solution)/shard_map/dst,ctf->dcsf/dot_general | solution.py:577
  309.2 4.8 all-to-all-start.3
  317.8 12.8 %collective-permute-done.8.refs_5_ = bf16[384,768]{1,0:T(8,128)(2,1)S(1)} collective-permute-done((bf16[384,768]{1,0:T(8,128)(2,1)}, bf16[384,768]{1,0:T(8,128)(2,1)S(1)}, u32[]{:S(2)}, u32[]{:S(2)}) %collective-permute-start.8) | collective-permute-done | bytes 589856 | tf_op jit(solution)/shard_map/ppermute | solution.py:607
  330.7 60.0 %collective-permute-done.10.refs_7_ = bf16[384,768]{1,0:T(8,128)(2,1)S(1)} collective-permute-done((bf16[384,768]{1,0:T(8,128)(2,1)}, bf16[384,768]{1,0:T(8,128)(2,1)S(1)}, u32[]{:S(2)}, u32[]{:S(2)}) %collective-permute-start.10) | collective-permute-done | bytes 589856 | tf_op jit(solution)/shard_map/ppermute | solution.py:607
  403.1 10.8 fusion.62
  417.8 5.1 all-to-all-start.4
  429.1 12.6 %fusion.63 = bf16[4,2,320,768]{3,2,1,0:T(8,128)(2,1)} fusion(bf16[2048,768]{1,0:T(8,128)(2,1)} %shard_map.415, s32[4,2,2048]{2,1,0:T(2,128)S(1)} %copy-done.39), kind=kOutput, calls=%fused_computation.112 | convolution fusion | flops 8060272640 | bytes 7143424 | tf_op jit(solution)/shard_map/dcst,tf->dcsf/dot_general | solution.py:517
  441.7 28.8 %all-to-all-done.4 = bf16[8,320,768]{2,1,0:T(8,128)(2,1)} async-done(((bf16[8,320,768]{2,1,0:T(8,128)(2,1)}), bf16[8,320,768]{2,1,0:T(8,128)(2,1)}, u32[]{:S(2)}, u32[]{:S(2)}) %all-to-all-start.4) | async-done | bytes 3932192 | tf_op jit(solution)/shard_map/all_to_all | solution.py:80
  470.5 7.2 all-to-all-start.5
  478.8 21.4 %shard_map.421 = (bf16[4,2,320,768]{3,2,1,0:T(8,128)(2,1)}, bf16[4,320,768]{2,1,0:T(8,128)(2,1)}, bf16[4,320,1536]{2,1,0:T(8,128)(2,1)}) custom-call(bf16[4,2,320,768]{3,2,1,0:T(8,128)(2,1)} %bitcast.59.refs_1_.rows_ref.refs_4_, bf16[4,2,320,768]{3,2,1,0:T(8,128)(2,1)} %all-to-all-done.3.refs_1_.grads_ref.refs_5_, f32[4,320,1]{2,1,0:T(8,128)} %squeeze.98.gate_ref, ...), custom_call_target="tpu_custom_call" | custom-call | flops 15099494400 | bytes 31457280 | tf_op jit(solution)/shard_map/pallas_call | solution.py:231
  504.5 19.5 %all-to-all-done.5 = bf16[8,320,768]{2,1,0:T(8,128)(2,1)} async-done(((bf16[8,320,768]{2,1,0:T(8,128)(2,1)}), bf16[8,320,768]{2,1,0:T(8,128)(2,1)}, u32[]{:S(2)}, u32[]{:S(2)}) %all-to-all-start.5) | async-done | bytes 3932192 | tf_op jit(solution)/shard_map/all_to_all | solution.py:80
  524.0 8.5 all-to-all-start.6
  537.9 21.5 %shard_map.423 = (bf16[4,2,320,768]{3,2,1,0:T(8,128)(2,1)}, bf16[4,320,768]{2,1,0:T(8,128)(2,1)}, bf16[4,320,1536]{2,1,0:T(8,128)(2,1)}) custom-call(bf16[4,2,320,768]{3,2,1,0:T(8,128)(2,1)} %shard_map.422.rows_ref, bf16[4,2,320,768]{3,2,1,0:T(8,128)(2,1)} %all-to-all-done.1.refs_1_.grads_ref, f32[4,320,1]{2,1,0:T(8,128)} %squeeze.99.gate_ref, ...), custom_call_target="tpu_custom_call" | custom-call | flops 15099494400 | bytes 31457280 | tf_op jit(solution)/shard_map/pallas_call | solution.py:231
  561.0 7.4 shard_map.424.refs_1_.refs_0_
  571.7 6.5 all-to-all-done.6.refs_1_.refs_0_
  578.2 7.2 all-to-all-start.7
  585.4 6.9 fusion.78.refs_1_
  598.1 8.4 fusion.51.refs_1_
  606.5 32.6 %shard_map.430 = (bf16[2,2,2,768,384]{4,3,2,1,0:T(8,128)(2,1)}, bf16[2,2,384,768]{3,2,1,0:T(8,128)(2,1)}) custom-call(bf16[4,2,320,768]{3,2,1,0:T(8,128)(2,1)} %bitcast.60.refs_1_.refs_0_, bf16[4,2,320,768]{3,2,1,0:T(8,128)(2,1)} %all-to-all-done.1.refs_1_.grads_ref, bf16[4,320,768]{2,1,0:T(8,128)(2,1)} %shard_map.429.refs_2_, ...), custom_call_target="tpu_custom_call" | custom-call | flops 18119393280 | bytes 52428800 | tf_op jit(solution)/shard_map/pallas_call | solution.py:375
  639.1 5.1 all-to-all-start.8
  644.9 6.9 fusion.84.refs_1_
  653.4 73.6 %all-gather.21.cloned.1.call-done = bf16[2048,768]{1,0:T(8,128)(2,1)} async-done(((bf16[1024,768]{1,0:T(8,128)(2,1)}), bf16[2048,768]{1,0:T(8,128)(2,1)}) %all-gather.21.cloned.1.call-update) | async-done | bytes 3145744 | tf_op jit(solution)/shard_map/all_gather | solution.py:454
  727.1 10.7 multiply_reduce_fusion
  737.7 8.6 psum.30
  746.4 4.8 convert_bitcast_fusion.3
  758.6 6.8 all-to-all-done.8
  765.3 5.7 slice_bitcast_fusion.1
  771.0 6.9 fusion.81.refs_1_
  778.0 23.7 %reduce-scatter.5.cloned.1.call-done.refs_0_.refs_1_ = bf16[1024,768]{1,0:T(8,128)(2,1)} async-done(((bf16[2048,768]{1,0:T(8,128)(2,1)}), bf16[1024,768]{1,0:T(8,128)(2,1)}) %reduce-scatter.5.cloned.1.call-update) | async-done | bytes 1572880 | tf_op jit(solution)/shard_map/reduce_scatter | solution.py:665
  806.3 8.6 fusion.50.refs_1_
  818.0 20.7 %shard_map.437.refs_1_ = bf16[1024,1024]{1,0:T(8,128)(2,1)} custom-call(bf16[1024,1024]{1,0:T(8,128)(2,1)S(1)} %copy-done.4, bf16[1024,1024]{1,0:T(8,128)(2,1)S(1)} %copy-done.4, bf16[1024,1024]{1,0:T(8,128)(2,1)S(1)} %copy-done.4, bf16[1024,768]{1,0:T(8,128)(2,1)S(1)} %copy-done.1, f32[6,1,1024]{2,1,0:T(1,128)S(1)} %copy-done.18, s32[1,1024]{1,0:T(1,128)S(1)} %copy-done.13, ...), custom_call_target="tpu_custom_call" | custom-call | flops 8053063680 | bytes 6291456 | tf_op jit(solution)/shard_map/pallas_call | solution.py:188
  838.7 8.6 fusion.87.refs_1_
  854.7 11.8 %fusion.140 = (bf16[4,384,768]{2,1,0:T(8,128)(2,1)}, f32[4,384,768]{2,1,0:T(8,128)}, f32[4,384,768]{2,1,0:T(8,128)}, f32[4,384,768]{2,1,0:T(8,128)}) fusion(f32[4,384,768]{2,1,0:T(8,128)} %param.51, bf16[4,384,768]{2,1,0:T(8,128)(2,1)} %all-to-all-done.12, f32[4,384,768]{2,1,0:T(8,128)} %param.52, f32[4,384,768]{2,1,0:T(8,128)} %param.53), kind=kLoop, calls=%fused_computation.250 | loop fusion | flops 20054016 | bytes 33030144 | tf_op jit(solution)/shard_map/convert_element_type | solution.py:762
  880.0 8.6 bitcast_add_fusion.refs_1_
  888.6 8.4 all-gather.23.cloned.1.call-done
  898.9 8.5 fusion.57
  912.0 39.3 %collective-permute-done.19 = bf16[1024,768]{1,0:T(8,128)(2,1)} collective-permute-done((bf16[1024,768]{1,0:T(8,128)(2,1)}, bf16[1024,768]{1,0:T(8,128)(2,1)}, u32[]{:S(2)}, u32[]{:S(2)}) %collective-permute-start.19) | collective-permute-done | bytes 1572896 | tf_op jit(solution)/shard_map/ppermute | solution.py:679
  951.4 5.5 convert_add_fusion.5
  956.8 5.1 reshape.312
  962.1 5.5 fusion.68.refs_1_
  967.7 9.4 copy.372
  977.0 4.9 psum.31
  982.0 5.0 all-to-all-start.11
  994.0 5.2 fusion.54
  999.2 4.8 reshape.315
  1010.7 5.5 add_convert_fusion
  1016.2 24.6 %all-to-all-done.11 = bf16[4,2,768,384]{3,1,2,0:T(2,128)(2,1)} async-done(((bf16[4,2,768,384]{3,1,2,0:T(2,128)(2,1)}), bf16[4,2,768,384]{3,1,2,0:T(2,128)(2,1)}, u32[]{:S(2)}, u32[]{:S(2)}) %all-to-all-start.11) | async-done | bytes 4718624 | tf_op jit(solution)/shard_map/all_to_all | solution.py:80
  1040.8 5.6 all-to-all-start.9
  1046.4 33.9 %fusion.141 = (bf16[4,768,2,384]{3,2,1,0:T(2,128)(2,1)}, f32[4,768,2,384]{3,2,1,0:T(2,128)}, f32[4,768,2,384]{3,2,1,0:T(2,128)}, f32[4,768,2,384]{3,2,1,0:T(2,128)}) fusion(f32[4,768,2,384]{3,2,1,0:T(2,128)} %param.48, bf16[4,2,768,384]{3,1,2,0:T(2,128)(2,1)} %all-to-all-done.11, f32[4,768,2,384]{3,2,1,0:T(2,128)} %param.49, f32[4,768,2,384]{3,2,1,0:T(2,128)} %param.50), kind=kLoop, calls=%fused_computation.251 | loop fusion | flops 40108032 | bytes 66060288 | tf_op jit(solution)/shard_map/convert_element_type | solution.py:758
  (383 shorter events, 193.6 us)
Async XLA Ops:
  7.2 47.9 %all-gather.13.cloned.1.call-start = ((), (), s32[]{:S(2)}) async-start(), calls=%async_computation.17 | async-start | bytes 4718592 | tf_op jit(solution)/shard_map/all_gather | solution.py:468
  9.6 152.5 %reduce-scatter.3.cloned.1.call-start = ((), (), s32[]{:S(2)}) async-start(), calls=%async_computation.15 | async-start | bytes 6291456 | tf_op jit(solution)/shard_map/reduce_scatter | solution.py:482
  9.7 43.0 %collective-permute-start.2 = (s32[1,1024]{1,0:T(1,128)}, s32[1,1024]{1,0:T(1,128)}, u32[]{:S(2)}, u32[]{:S(2)}) collective-permute-start(s32[1,1024]{1,0:T(1,128)} %param.34), channel_id=1, source_target_pairs={{0,1},{1,0},{2,3},{3,2},{4,5},{5,4},{6,7},{7,6},{8,9},{9,8},{10,11... | collective-permute-start | bytes 12296 | tf_op jit(solution)/shard_map/ppermute | solution.py:461
  12.7 42.4 %collective-permute-start.1 = (f32[4,2048]{1,0:T(4,128)}, f32[4,2048]{1,0:T(4,128)}, u32[]{:S(2)}, u32[]{:S(2)}) collective-permute-start(f32[4,2048]{1,0:T(4,128)} %param.33), channel_id=1, source_target_pairs={{0,16},{16,0},{1,17},{17,1},{2,18},{18,2},{3,19},{19,3},{4,20},{20... | collective-permute-start | bytes 98312 | tf_op jit(solution)/shard_map/ppermute | solution.py:471
  15.3 38.8 %collective-permute-start = (s32[4,2048]{1,0:T(4,128)}, s32[4,2048]{1,0:T(4,128)}, u32[]{:S(2)}, u32[]{:S(2)}) collective-permute-start(s32[4,2048]{1,0:T(4,128)} %param.32), channel_id=1, source_target_pairs={{0,16},{16,0},{1,17},{17,1},{2,18},{18,2},{3,19},{19,3},{4,20},{20... | collective-permute-start | bytes 98312 | tf_op jit(solution)/shard_map/ppermute | solution.py:470
  18.0 32.1 %copy-start.20 = (f32[1024,768]{1,0:T(8,128)}, f32[1024,768]{1,0:T(8,128)S(1)}, u32[]{:S(2)}) copy-start(f32[1024,768]{1,0:T(8,128)S(1)} %reshape.329) | copy-start | bytes 9437188
  35.6 36.8 %collective-permute-start.3 = (bf16[1024,768]{1,0:T(8,128)(2,1)}, bf16[1024,768]{1,0:T(8,128)(2,1)}, u32[]{:S(2)}, u32[]{:S(2)}) collective-permute-start(bf16[1024,768]{1,0:T(8,128)(2,1)} %shard_map.400), channel_id=1, source_target_pairs={{0,1},{1,0},{2,3},{3,2},{4,5},{5,4},{6,7},{7,6},{8,9},{9,8},{10,11... | collective-permute-start | bytes 4718600 | tf_op jit(solution)/shard_map/ppermute | solution.py:461
  48.6 234.4 %copy-start.55 = (f32[768]{0:T(1024)}, f32[768]{0:T(1024)S(1)}, u32[]{:S(2)}) copy-start(f32[768]{0:T(1024)S(1)} %get-tuple-element.57) | copy-start | bytes 9220
  52.7 16.6 %copy-start.46 = (s32[1,4,1,1,2048]{4,1,2,3,0:T(4,128)}, s32[1,4,1,1,2048]{4,1,2,3,0:T(4,128)S(1)}, u32[]{:S(2)}) copy-start(s32[1,4,1,1,2048]{4,1,2,3,0:T(4,128)S(1)} %copy.449) | copy-start | bytes 98308
  78.9 6.0 collective-permute-start.4
  78.9 75.7 %all-to-all-start = ((bf16[2,1024,768]{2,1,0:T(8,128)(2,1)}), bf16[2,1024,768]{2,1,0:T(8,128)(2,1)S(1)}, u32[]{:S(2)}, u32[]{:S(2)}) async-start(bf16[2,1024,768]{2,1,0:T(8,128)(2,1)} %broadcast_in_dim.70), calls=%async_computation.1 | async-start | bytes 6291456 | tf_op jit(solution)/shard_map/all_to_all | solution.py:80
  156.2 104.0 %all-to-all-start.1 = ((bf16[4,2,320,768]{3,2,1,0:T(8,128)(2,1)}), bf16[4,2,320,768]{3,2,1,0:T(8,128)(2,1)}, u32[]{:S(2)}, u32[]{:S(2)}) async-start(bf16[4,2,320,768]{3,2,1,0:T(8,128)(2,1)} %shard_map.404), calls=%async_computation.2 | async-start | bytes 7864320 | tf_op jit(solution)/shard_map/all_to_all | solution.py:80
  161.0 99.2 %all-gather.15.cloned.1.call-start = ((), (), s32[]{:S(2)}) async-start(), calls=%async_computation.18 | async-start | bytes 4718592 | tf_op jit(solution)/shard_map/all_gather | solution.py:594
  185.7 85.3 %all-gather.17.cloned.1.call-start = ((), (), s32[]{:S(2)}) async-start(), calls=%async_computation.19 | async-start | bytes 3538944 | tf_op jit(solution)/shard_map/all_gather | solution.py:596
  186.3 210.2 %all-gather.19.cloned.1.call-start = ((), (), s32[]{:S(2)}) async-start(), calls=%async_computation.20 | async-start | bytes 4718592 | tf_op jit(solution)/shard_map/all_gather | solution.py:454
  188.9 66.2 %collective-permute-start.13 = (bf16[1024,768]{1,0:T(8,128)(2,1)}, bf16[1024,768]{1,0:T(8,128)(2,1)}, u32[]{:S(2)}, u32[]{:S(2)}) collective-permute-start(bf16[1024,768]{1,0:T(8,128)(2,1)} %fusion.162), channel_id=1, source_target_pairs={{0,1},{1,0},{2,3},{3,2},{4,5},{5,4},{6,7},{7,6},{8,9},{9,8},{10,11... | collective-permute-start | bytes 4718600 | tf_op jit(solution)/shard_map/ppermute | solution.py:461
  260.3 10.8 copy-start.21
  287.0 10.7 collective-permute-start.14
  309.2 108.6 %all-to-all-start.3 = ((bf16[4,2,320,768]{3,2,1,0:T(8,128)(2,1)}), bf16[4,2,320,768]{3,2,1,0:T(8,128)(2,1)}, u32[]{:S(2)}, u32[]{:S(2)}) async-start(bf16[4,2,320,768]{3,2,1,0:T(8,128)(2,1)} %shard_map.418), calls=%async_computation.4 | async-start | bytes 7864320 | tf_op jit(solution)/shard_map/all_to_all | solution.py:80
  314.0 16.5 %collective-permute-start.8 = (bf16[384,768]{1,0:T(8,128)(2,1)}, bf16[384,768]{1,0:T(8,128)(2,1)S(1)}, u32[]{:S(2)}, u32[]{:S(2)}) collective-permute-start(bf16[384,768]{1,0:T(8,128)(2,1)} %shard_map.410), channel_id=1, source_target_pairs={{0,1},{1,0},{2,3},{3,2},{4,5},{5,4},{6,7},{7,6},{8,9},{9,8},{10,11... | collective-permute-start | bytes 1769480 | tf_op jit(solution)/shard_map/ppermute | solution.py:607
  315.6 75.1 %copy-start.2 = (bf16[2,768,384]{2,1,0:T(8,128)(2,1)S(1)}, bf16[2,768,384]{2,1,0:T(8,128)(2,1)}, u32[]{:S(2)}) copy-start(bf16[2,768,384]{2,1,0:T(8,128)(2,1)} %get-tuple-element.104.refs_2_.refs_0_) | copy-start | bytes 3538948
  315.6 75.1 %copy-start.5 = (bf16[384,768]{1,0:T(8,128)(2,1)S(1)}, bf16[384,768]{1,0:T(8,128)(2,1)}, u32[]{:S(2)}) copy-start(bf16[384,768]{1,0:T(8,128)(2,1)} %get-tuple-element.88.refs_6_.refs_4_) | copy-start | bytes 1769476
  315.6 75.0 %collective-permute-start.5 = (bf16[2,768,384]{2,1,0:T(8,128)(2,1)}, bf16[2,768,384]{2,1,0:T(8,128)(2,1)S(1)}, u32[]{:S(2)}, u32[]{:S(2)}) collective-permute-start(bf16[2,768,384]{2,1,0:T(8,128)(2,1)} %shard_map.407), channel_id=1, source_target_pairs={{0,1},{1,0},{2,3},{3,2},{4,5},{5,4},{6,7},{7,6},{8,9},{9,8},{10,11... | collective-permute-start | bytes 3538952 | tf_op jit(solution)/shard_map/ppermute | solution.py:607
  316.1 74.5 %collective-permute-start.6 = (bf16[2,768,384]{2,1,0:T(8,128)(2,1)}, bf16[2,768,384]{2,1,0:T(8,128)(2,1)}, u32[]{:S(2)}, u32[]{:S(2)}) collective-permute-start(bf16[2,768,384]{2,1,0:T(8,128)(2,1)} %shard_map.408), channel_id=1, source_target_pairs={{0,2},{1,3},{2,0},{3,1},{4,6},{5,7},{6,4},{7,5},{8,10},{9,11},{10,... | collective-permute-start | bytes 3538952 | tf_op jit(solution)/shard_map/ppermute | solution.py:607
  316.1 74.5 %collective-permute-start.7 = (bf16[2,768,384]{2,1,0:T(8,128)(2,1)}, bf16[2,768,384]{2,1,0:T(8,128)(2,1)}, u32[]{:S(2)}, u32[]{:S(2)}) collective-permute-start(bf16[2,768,384]{2,1,0:T(8,128)(2,1)} %shard_map.409), channel_id=1, source_target_pairs={{0,3},{1,2},{2,1},{3,0},{4,7},{5,6},{6,5},{7,4},{8,11},{9,10},{10,... | collective-permute-start | bytes 3538952 | tf_op jit(solution)/shard_map/ppermute | solution.py:607
  317.7 12.9 %collective-permute-start.9 = (bf16[384,768]{1,0:T(8,128)(2,1)}, bf16[384,768]{1,0:T(8,128)(2,1)S(1)}, u32[]{:S(2)}, u32[]{:S(2)}) collective-permute-start(bf16[384,768]{1,0:T(8,128)(2,1)} %shard_map.411), channel_id=1, source_target_pairs={{0,2},{1,3},{2,0},{3,1},{4,6},{5,7},{6,4},{7,5},{8,10},{9,11},{10,... | collective-permute-start | bytes 1769480 | tf_op jit(solution)/shard_map/ppermute | solution.py:607
  330.6 60.0 %collective-permute-start.10 = (bf16[384,768]{1,0:T(8,128)(2,1)}, bf16[384,768]{1,0:T(8,128)(2,1)S(1)}, u32[]{:S(2)}, u32[]{:S(2)}) collective-permute-start(bf16[384,768]{1,0:T(8,128)(2,1)} %shard_map.412), channel_id=1, source_target_pairs={{0,3},{1,2},{2,1},{3,0},{4,7},{5,6},{6,5},{7,4},{8,11},{9,10},{10,... | collective-permute-start | bytes 1769480 | tf_op jit(solution)/shard_map/ppermute | solution.py:607
  399.1 4.0 collective-permute-start.12
  417.8 52.7 %all-to-all-start.4 = ((bf16[8,320,768]{2,1,0:T(8,128)(2,1)}), bf16[8,320,768]{2,1,0:T(8,128)(2,1)}, u32[]{:S(2)}, u32[]{:S(2)}) async-start(bf16[8,320,768]{2,1,0:T(8,128)(2,1)} %shard_map.419), calls=%async_computation.5 | async-start | bytes 7864320 | tf_op jit(solution)/shard_map/all_to_all | solution.py:80
  422.9 3.5 collective-permute-start.11
  470.5 53.5 %all-to-all-start.5 = ((bf16[8,320,768]{2,1,0:T(8,128)(2,1)}), bf16[8,320,768]{2,1,0:T(8,128)(2,1)}, u32[]{:S(2)}, u32[]{:S(2)}) async-start(bf16[8,320,768]{2,1,0:T(8,128)(2,1)} %shard_map.420), calls=%async_computation.6 | async-start | bytes 7864320 | tf_op jit(solution)/shard_map/all_to_all | solution.py:80
  524.0 54.2 %all-to-all-start.6 = ((bf16[8,320,768]{2,1,0:T(8,128)(2,1)}), bf16[8,320,768]{2,1,0:T(8,128)(2,1)}, u32[]{:S(2)}, u32[]{:S(2)}) async-start(bf16[8,320,768]{2,1,0:T(8,128)(2,1)} %bitcast.295), calls=%async_computation.7 | async-start | bytes 7864320 | tf_op jit(solution)/shard_map/all_to_all | solution.py:80
  537.9 21.5 %copy-start.15 = (bf16[2,768,768]{2,1,0:T(8,128)(2,1)S(1)}, bf16[2,768,768]{2,1,0:T(8,128)(2,1)}, u32[]{:S(2)}) copy-start(bf16[2,768,768]{2,1,0:T(8,128)(2,1)} %copy-done.14) | copy-start | bytes 7077892
  537.9 21.5 %copy-start.16 = (bf16[4,320,768]{2,1,0:T(8,128)(2,1)S(1)}, bf16[4,320,768]{2,1,0:T(8,128)(2,1)}, u32[]{:S(2)}) copy-start(bf16[4,320,768]{2,1,0:T(8,128)(2,1)} %get-tuple-element.43.refs_1_.refs_6_) | copy-start | bytes 5898244
  578.2 60.9 %all-to-all-start.7 = ((bf16[8,320,768]{2,1,0:T(8,128)(2,1)}), bf16[8,320,768]{2,1,0:T(8,128)(2,1)}, u32[]{:S(2)}, u32[]{:S(2)}) async-start(bf16[8,320,768]{2,1,0:T(8,128)(2,1)} %bitcast.308), calls=%async_computation.8 | async-start | bytes 7864320 | tf_op jit(solution)/shard_map/all_to_all | solution.py:80
  592.3 5.9 collective-permute-start.15
  639.1 126.2 %all-to-all-start.8 = ((bf16[8,2,320,768]{3,2,1,0:T(8,128)(2,1)}), bf16[8,2,320,768]{3,2,1,0:T(8,128)(2,1)}, u32[]{:S(2)}, u32[]{:S(2)}) async-start(bf16[8,2,320,768]{3,2,1,0:T(8,128)(2,1)} %bitcast.292), calls=%async_computation.9 | async-start | bytes 15728640 | tf_op jit(solution)/shard_map/all_to_all | solution.py:80
  644.2 82.8 %all-gather.21.cloned.1.call-start = ((), (), s32[]{:S(2)}) async-start(), calls=%async_computation.21 | async-start | bytes 4718592 | tf_op jit(solution)/shard_map/all_gather | solution.py:454
  644.8 156.9 %reduce-scatter.5.cloned.1.call-start = ((), (), s32[]{:S(2)}) async-start(), calls=%async_computation.16 | async-start | bytes 4718592 | tf_op jit(solution)/shard_map/reduce_scatter | solution.py:665
  651.8 75.3 %collective-permute-start.16 = (f32[1024,768]{1,0:T(8,128)S(1)}, f32[1024,768]{1,0:T(8,128)}, u32[]{:S(2)}, u32[]{:S(2)}) collective-permute-start(f32[1024,768]{1,0:T(8,128)S(1)} %fusion.84.refs_1_), channel_id=1, source_target_pairs={{0,2},{2,0},{1,3},{3,1},{4,6},{6,4},{5,7},{7,5},{8,10},{10,8},{9,1... | collective-permute-start | bytes 9437192 | tf_op jit(solution)/shard_map/ppermute | solution.py:532
  653.4 73.6 %copy-start.56 = (f32[768]{0:T(1024)S(1)}, f32[768]{0:T(1024)}, u32[]{:S(2)}) copy-start(f32[768]{0:T(1024)} %copy-done.55) | copy-start | bytes 9220
  653.4 73.6 %copy-start.58 = (f32[1024]{0:T(1024)S(1)}, f32[1024]{0:T(1024)}, u32[]{:S(2)}) copy-start(f32[1024]{0:T(1024)} %copy-done.57) | copy-start | bytes 12292
  727.0 19.3 %copy-start.62 = (f32[1024]{0:T(1024)S(1)}, f32[1024]{0:T(1024)}, u32[]{:S(2)}) copy-start(f32[1024]{0:T(1024)} %copy-done.61) | copy-start | bytes 12292
  727.0 19.3 %copy-start.23 = (f32[1024,768]{1,0:T(8,128)S(1)}, f32[1024,768]{1,0:T(8,128)}, u32[]{:S(2)}) copy-start(f32[1024,768]{1,0:T(8,128)} %reshape.297) | copy-start | bytes 9437188
  777.9 23.8 %copy-start.34 = (f32[1024,768]{1,0:T(8,128)}, f32[1024,768]{1,0:T(8,128)S(1)}, u32[]{:S(2)}) copy-start(f32[1024,768]{1,0:T(8,128)S(1)} %fusion.81.refs_1_) | copy-start | bytes 9437188
  777.9 28.4 %collective-permute-start.17 = (f32[1024,768]{1,0:T(8,128)S(1)}, f32[1024,768]{1,0:T(8,128)}, u32[]{:S(2)}, u32[]{:S(2)}) collective-permute-start(f32[1024,768]{1,0:T(8,128)S(1)} %fusion.81.refs_1_), channel_id=1, source_target_pairs={{0,2},{2,0},{1,3},{3,1},{4,6},{6,4},{5,7},{7,5},{8,10},{10,8},{9,1... | collective-permute-start | bytes 9437192 | tf_op jit(solution)/shard_map/ppermute | solution.py:532
  801.7 53.0 %all-to-all-start.12 = ((bf16[4,384,768]{2,1,0:T(8,128)(2,1)}), bf16[4,384,768]{2,1,0:T(8,128)(2,1)}, u32[]{:S(2)}, u32[]{:S(2)}) async-start(bf16[4,384,768]{2,1,0:T(8,128)(2,1)} %bitcast.314), calls=%async_computation.14 | async-start | bytes 4718592 | tf_op jit(solution)/shard_map/all_to_all | solution.py:80
  806.2 90.7 %all-gather.23.cloned.1.call-start = ((), (), s32[]{:S(2)}) async-start(), calls=%async_computation.22 | async-start | bytes 6291456 | tf_op jit(solution)/shard_map/all_gather | solution.py:675
  847.4 32.6 %collective-permute-start.18 = (f32[1024,768]{1,0:T(8,128)}, f32[1024,768]{1,0:T(8,128)}, u32[]{:S(2)}, u32[]{:S(2)}) collective-permute-start(f32[1024,768]{1,0:T(8,128)} %fusion.87.refs_1_), channel_id=1, source_target_pairs={{0,2},{2,0},{1,3},{3,1},{4,6},{6,4},{5,7},{7,5},{8,10},{10,8},{9,1... | collective-permute-start | bytes 9437192 | tf_op jit(solution)/shard_map/ppermute | solution.py:532
  854.1 14.9 %collective-permute-start.26 = (f32[768,768]{1,0:T(8,128)}, f32[768,768]{1,0:T(8,128)}, u32[]{:S(2)}, u32[]{:S(2)}) collective-permute-start(f32[768,768]{1,0:T(8,128)} %fusion.93.refs_1_), channel_id=1, source_target_pairs={{0,2},{2,0},{1,3},{3,1},{4,6},{6,4},{5,7},{7,5},{8,10},{10,8},{9,1... | collective-permute-start | bytes 7077896 | tf_op jit(solution)/shard_map/ppermute | solution.py:693
  854.7 11.8 %copy-start.67 = (f32[2,6]{1,0:T(2,128)}, f32[2,6]{1,0:T(2,128)S(1)}, u32[]{:S(2)}) copy-start(f32[2,6]{1,0:T(2,128)S(1)} %dynamic_update_slice.3.refs_0_) | copy-start | bytes 148
  866.5 84.9 %collective-permute-start.19 = (bf16[1024,768]{1,0:T(8,128)(2,1)}, bf16[1024,768]{1,0:T(8,128)(2,1)}, u32[]{:S(2)}, u32[]{:S(2)}) collective-permute-start(bf16[1024,768]{1,0:T(8,128)(2,1)} %fusion.50.refs_1_), channel_id=1, source_target_pairs={{0,16},{16,0},{1,17},{17,1},{2,18},{18,2},{3,19},{19,3},{4,20},{20... | collective-permute-start | bytes 4718600 | tf_op jit(solution)/shard_map/ppermute | solution.py:679
  875.5 106.5 %all-to-all-start.10 = ((bf16[8,96,768]{2,1,0:T(8,128)(2,1)}), bf16[8,96,768]{2,1,0:T(8,128)(2,1)}, u32[]{:S(2)}, u32[]{:S(2)}) async-start(bf16[8,96,768]{2,1,0:T(8,128)(2,1)} %bitcast.315), calls=%async_computation.12 | async-start | bytes 2359296 | tf_op jit(solution)/shard_map/all_to_all | solution.py:80
  907.4 3.8 collective-permute-start.21
  912.0 50.0 %collective-permute-start.22 = (f32[3,768]{1,0:T(4,128)S(1)}, f32[3,768]{1,0:T(4,128)S(1)}, u32[]{:S(2)}, u32[]{:S(2)}) collective-permute-start(f32[3,768]{1,0:T(4,128)S(1)} %pad_maximum_fusion.2), channel_id=1, source_target_pairs={{0,2},{2,0},{1,3},{3,1},{4,6},{6,4},{5,7},{7,5},{8,10},{10,8},{9,1... | collective-permute-start | bytes 27656 | tf_op jit(solution)/shard_map/ppermute | solution.py:65
  962.1 19.9 %collective-permute-start.23 = (f32[3,768]{1,0:T(4,128)S(1)}, f32[3,768]{1,0:T(4,128)S(1)}, u32[]{:S(2)}, u32[]{:S(2)}) collective-permute-start(f32[3,768]{1,0:T(4,128)S(1)} %pad_maximum_fusion.3), channel_id=1, source_target_pairs={{0,16},{16,0},{1,17},{17,1},{2,18},{18,2},{3,19},{19,3},{4,20},{20... | collective-permute-start | bytes 27656 | tf_op jit(solution)/shard_map/ppermute | solution.py:65
  977.0 33.6 %collective-permute-start.20 = (f32[768,1024]{1,0:T(8,128)}, f32[768,1024]{1,0:T(8,128)}, u32[]{:S(2)}, u32[]{:S(2)}) collective-permute-start(f32[768,1024]{1,0:T(8,128)} %fusion.68.refs_1_), channel_id=1, source_target_pairs={{0,2},{2,0},{1,3},{3,1},{4,6},{6,4},{5,7},{7,5},{8,10},{10,8},{9,1... | collective-permute-start | bytes 9437192 | tf_op jit(solution)/shard_map/ppermute | solution.py:693
  982.0 58.8 %all-to-all-start.11 = ((bf16[4,2,768,384]{3,1,2,0:T(2,128)(2,1)}), bf16[4,2,768,384]{3,1,2,0:T(2,128)(2,1)}, u32[]{:S(2)}, u32[]{:S(2)}) async-start(bf16[4,2,768,384]{3,1,2,0:T(2,128)(2,1)} %bitcast.303), calls=%async_computation.13 | async-start | bytes 9437184 | tf_op jit(solution)/shard_map/all_to_all | solution.py:80
  987.0 3.8 collective-permute-start.24
  990.8 13.2 %collective-permute-start.25 = (f32[3,768]{1,0:T(4,128)S(1)}, f32[3,768]{1,0:T(4,128)S(1)}, u32[]{:S(2)}, u32[]{:S(2)}) collective-permute-start(f32[3,768]{1,0:T(4,128)S(1)} %pad_maximum_fusion.5), channel_id=1, source_target_pairs={{0,8},{4,12},{8,0},{12,4},{1,9},{5,13},{9,1},{13,5},{2,10},{6,14},... | collective-permute-start | bytes 27656 | tf_op jit(solution)/shard_map/ppermute | solution.py:65
  1040.8 42.3 %all-to-all-start.9 = ((bf16[8,96,1024]{2,1,0:T(8,128)(2,1)}), bf16[8,96,1024]{2,1,0:T(8,128)(2,1)S(1)}, u32[]{:S(2)}, u32[]{:S(2)}) async-start(bf16[8,96,1024]{2,1,0:T(8,128)(2,1)} %bitcast.103), calls=%async_computation.11 | async-start | bytes 3145728 | tf_op jit(solution)/shard_map/all_to_all | solution.py:80
  1046.4 37.0 %copy-start.41 = (f32[96,1,1024]{2,1,0:T(1,128)S(1)}, f32[96,1,1024]{2,1,0:T(1,128)}, u32[]{:S(2)}) copy-start(f32[96,1,1024]{2,1,0:T(1,128)} %param.42) | copy-start | bytes 1179652
  1046.4 37.0 %copy-start.42 = (f32[96,1,1024]{2,1,0:T(1,128)S(1)}, f32[96,1,1024]{2,1,0:T(1,128)}, u32[]{:S(2)}) copy-start(f32[96,1,1024]{2,1,0:T(1,128)} %param.43) | copy-start | bytes 1179652
  1046.4 37.0 %copy-start.43 = (f32[96,1,1024]{2,1,0:T(1,128)S(1)}, f32[96,1,1024]{2,1,0:T(1,128)}, u32[]{:S(2)}) copy-start(f32[96,1,1024]{2,1,0:T(1,128)} %param.44) | copy-start | bytes 1179652
  (52 other events, 169.7 us)
Sparse Core Ops, SparseCore 0:
  9.7 14.8 all-gather.12
  63.1 55.6 reduce-scatter.2
  185.8 73.0 all-gather.14
  260.9 10.0 all-gather.16
  297.8 78.7 all-gather.18
  647.0 80.0 all-gather.20
  758.7 42.9 reduce-scatter.4
  838.8 58.0 all-gather.22

commit v2 on v1

--- a/solution.py
+++ b/solution.py
@@ -29,6 +29,7 @@
 
 QUERIES = 256
 MIB = 1 << 20
+NO_COST = pl.CostEstimate(flops=0, bytes_accessed=0, transcendentals=0)
 
 
 def dot(left, right, left_dim=1, right_dim=0):
@@ -48,7 +49,7 @@
         out_specs=pl.BlockSpec(memory_space=pl.ANY),
         out_shape=jax.ShapeDtypeStruct(values.shape, values.dtype),
         input_output_aliases={0: 0},
-        cost_estimate=pl.CostEstimate(flops=0, bytes_accessed=0, transcendentals=0),
+        cost_estimate=NO_COST,
     )(values, *earlier)
 
 
@@ -144,9 +145,7 @@
             jax.ShapeDtypeStruct((GROUP, 1, LEN), jnp.float32),
         ],
         compiler_params=pltpu.CompilerParams(vmem_limit_bytes=40 * MIB),
-        cost_estimate=pl.CostEstimate(
-            flops=4 * GROUP * LEN * LEN * HD, bytes_accessed=4 * MIB, transcendentals=GROUP * LEN * LEN
-        ),
+        cost_estimate=NO_COST,
     )(packed, packed, packed, blocks[None, :], blocks[:, None])
 
 
@@ -201,18 +200,47 @@
         out_shape=jax.ShapeDtypeStruct((LEN, (GROUP + 2) * HD), jnp.bfloat16),
         scratch_shapes=[pltpu.VMEM((LEN, HD), jnp.float32)] * 2,
         compiler_params=pltpu.CompilerParams(vmem_limit_bytes=40 * MIB),
-        cost_estimate=pl.CostEstimate(
-            flops=10 * GROUP * LEN * LEN * HD, bytes_accessed=6 * MIB, transcendentals=GROUP * LEN * LEN
-        ),
+        cost_estimate=NO_COST,
     )(packed, packed, packed, grad_heads, log_total, blocks[None, :], blocks[:, None])
 
 
-def expert_kernel(col_n, rows_ref, grads_ref, gate_ref, in_ref, down_ref, back_ref, weighted_ref, pair_ref):
+def pick_kernel(ranks_ref, *refs):
+    blocks, out_ref = refs[:-1], refs[-1]
+    _, cols, slots, _ = out_ref.shape
+    rows = len(blocks) // cols
+    count = blocks[0].shape[0]
+    slot = lax.broadcasted_iota(jnp.int32, (slots, rows * count), 0)
+    hot = (ranks_ref[0] == slot).astype(jnp.float32).astype(jnp.bfloat16)
+    for c in range(cols):
+        picked = dot(hot[:, :count], blocks[c][...])
+        for k in range(1, rows):
+            picked += dot(hot[:, k * count : (k + 1) * count], blocks[k * cols + c][...])
+        out_ref[0, c] = picked.astype(jnp.bfloat16)
+
+
+def pick_slots(ranks, slots, blocks):
+    units, count = ranks.shape
+    cols = len(blocks[0])
+    flat = [block for row in blocks for block in row]
+    width = flat[0].shape[1]
+    whole = pl.BlockSpec(flat[0].shape, lambda u: (0, 0), pipeline_mode=pl.Buffered(1))
+    return pl.pallas_call(
+        pick_kernel,
+        grid=(units,),
+        in_specs=[pl.BlockSpec((1, 1, count), lambda u: (u, 0, 0))] + [whole] * len(flat),
+        out_specs=pl.BlockSpec((1, cols, slots, width), lambda u: (u, 0, 0, 0)),
+        out_shape=jax.ShapeDtypeStruct((units, cols, slots, width), jnp.bfloat16),
+        compiler_params=pltpu.CompilerParams(vmem_limit_bytes=56 * MIB),
+        cost_estimate=NO_COST,
+    )(ranks[:, None, :], *flat)
+
+
+def expert_kernel(col_n, place_ref, rows_ref, grads_ref, gate_ref, in_ref, down_ref, back_ref, weighted_ref, pair_ref):
     gate_up = dot(rows_ref[0, 0], in_ref[0])
-    grad_weighted = dot(grads_ref[0, 0], down_ref[0], 1, 1)
+    grad_weighted = dot(grads_ref[0, 0], down_ref[place_ref[1]], 1, 1)
     for c in range(1, col_n):
         gate_up += dot(rows_ref[0, c], in_ref[c])
-        grad_weighted += dot(grads_ref[0, c], down_ref[c], 1, 1)
+        grad_weighted += dot(grads_ref[0, c], down_ref[lax.rem(place_ref[1] + c, col_n)], 1, 1)
     gate_half, up_half, scale = gate_up[:, :FFE], gate_up[:, FFE:], gate_ref[0]
     sigmoid_gate = jax.nn.sigmoid(gate_half)
     silu_gate = gate_half * sigmoid_gate
@@ -225,13 +253,14 @@
         back_ref[0, c] = dot(pair_ref[0], in_ref[c], 1, 1).astype(jnp.bfloat16)
 
 
-def expert_passes(slot_rows, slot_grads, gates, weights_in, weights_down):
+def expert_passes(place, slot_rows, slot_grads, gates, weights_in, weights_down):
     dl_n, col_n, slots, width = slot_rows.shape
     block = pl.BlockSpec((1, col_n, slots, width), lambda d: (d, 0, 0, 0))
     return pl.pallas_call(
         functools.partial(expert_kernel, col_n),
         grid=(dl_n,),
         in_specs=[
+            pl.BlockSpec(memory_space=pltpu.SMEM),
             block,
             block,
             pl.BlockSpec((1, slots, 1), lambda d: (d, 0, 0)),
@@ -249,10 +278,8 @@
             jax.ShapeDtypeStruct((dl_n, slots, 2 * FFE), jnp.bfloat16),
         ],
         compiler_params=pltpu.CompilerParams(vmem_limit_bytes=56 * MIB),
-        cost_estimate=pl.CostEstimate(
-            flops=10 * dl_n * slots * D * FFE, bytes_accessed=30 * MIB, transcendentals=dl_n * slots * FFE
-        ),
-    )(slot_rows, slot_grads, gates, weights_in, weights_down)
+        cost_estimate=NO_COST,
+    )(place, slot_rows, slot_grads, gates, weights_in, weights_down)
 
 
 def join_kernel(row_n, col_n, place_ref, *refs):
@@ -280,7 +307,7 @@
             jax.ShapeDtypeStruct((col_n, FFE, width), jnp.bfloat16),
         ],
         compiler_params=pltpu.CompilerParams(vmem_limit_bytes=40 * MIB),
-        cost_estimate=pl.CostEstimate(flops=0, bytes_accessed=14 * MIB, transcendentals=0),
+        cost_estimate=NO_COST,
     )(place, *in_pieces, *down_pieces)
 
 
@@ -319,13 +346,11 @@
         ),
         out_shape=jax.ShapeDtypeStruct((dl_n, col_n, sets, slots, width), jnp.bfloat16),
         compiler_params=pltpu.CompilerParams(vmem_limit_bytes=40 * MIB),
-        cost_estimate=pl.CostEstimate(
-            flops=2 * sets * dl_n * slots * D * FFE, bytes_accessed=14 * MIB, transcendentals=0
-        ),
+        cost_estimate=NO_COST,
     )(weights_down, *weighted)
 
 
-def expert_grad_kernel(row_n, sets, steps, *refs):
+def expert_grad_kernel(row_n, sets, steps, place_ref, *refs):
     part = FFE // row_n
     step = pl.program_id(1)
     in_grad_ref, down_grad_ref, in_acc, down_acc = refs[4 * sets :]
@@ -357,7 +382,7 @@
             down_grad_ref[r, 0] = down_acc[r * part : (r + 1) * part, :].astype(jnp.bfloat16)
 
 
-def expert_grads(sources, row_n):
+def expert_grads(place, sources, row_n):
     dl_n, col_n, slots, width = sources[0][0].shape
     sets = len(sources)
     blocks = 2 if dl_n % 2 == 0 else 1
@@ -365,34 +390,37 @@
     part = FFE // row_n
     in_specs = []
     for at in halves(steps, sets):
-        block = pl.BlockSpec((blocks, 1, slots, width), lambda c, d, at=at: (at(d), c, 0, 0))
         in_specs += [
-            block,
-            block,
-            pl.BlockSpec((blocks, slots, FFE), lambda c, d, at=at: (at(d), 0, 0)),
-            pl.BlockSpec((blocks, slots, 2 * FFE), lambda c, d, at=at: (at(d), 0, 0)),
+            pl.BlockSpec((blocks, 1, slots, width), lambda c, d, p, at=at: (at(d), c, 0, 0)),
+            pl.BlockSpec(
+                (blocks, 1, slots, width),
+                lambda c, d, p, at=at: (at(d), lax.rem(c - p[1] + col_n, col_n), 0, 0),
+            ),
+            pl.BlockSpec((blocks, slots, FFE), lambda c, d, p, at=at: (at(d), 0, 0)),
+            pl.BlockSpec((blocks, slots, 2 * FFE), lambda c, d, p, at=at: (at(d), 0, 0)),
         ]
     return pl.pallas_call(
         functools.partial(expert_grad_kernel, row_n, sets, steps),
-        grid=(col_n, sets * steps),
-        in_specs=in_specs,
-        out_specs=[
-            pl.BlockSpec((row_n, 1, 2, width, part), lambda c, d: (0, c, 0, 0, 0)),
-            pl.BlockSpec((row_n, 1, part, width), lambda c, d: (0, c, 0, 0)),
-        ],
+        grid_spec=pltpu.PrefetchScalarGridSpec(
+            num_scalar_prefetch=1,
+            grid=(col_n, sets * steps),
+            in_specs=in_specs,
+            out_specs=[
+                pl.BlockSpec((row_n, 1, 2, width, part), lambda c, d, p: (0, c, 0, 0, 0)),
+                pl.BlockSpec((row_n, 1, part, width), lambda c, d, p: (0, c, 0, 0)),
+            ],
+            scratch_shapes=[
+                pltpu.VMEM((width, 2 * FFE), jnp.float32),
+                pltpu.VMEM((FFE, width), jnp.float32),
+            ],
+        ),
         out_shape=[
             jax.ShapeDtypeStruct((row_n, col_n, 2, width, part), jnp.bfloat16),
             jax.ShapeDtypeStruct((row_n, col_n, part, width), jnp.bfloat16),
         ],
-        scratch_shapes=[
-            pltpu.VMEM((width, 2 * FFE), jnp.float32),
-            pltpu.VMEM((FFE, width), jnp.float32),
-        ],
         compiler_params=pltpu.CompilerParams(vmem_limit_bytes=58 * MIB),
-        cost_estimate=pl.CostEstimate(
-            flops=6 * sets * dl_n * slots * D * FFE, bytes_accessed=50 * MIB, transcendentals=0
-        ),
-    )(*[array for source in sources for array in source])
+        cost_estimate=NO_COST,
+    )(place, *[array for source in sources for array in source])
 
 
 def adam_step(master, moment_one, moment_two, gradient, rate, decay):
@@ -461,9 +489,6 @@
             moved.append(lax.ppermute(values, axis, [(i, (i - k) % count) for i in range(count)]))
         return moved
 
-    def row_blocks(values):
-        return jnp.concatenate(ring(values, "row"), axis=0)
-
     inputs = tokens.reshape(tokens_row, width).astype(jnp.float32)
     qkv_row = lax.all_gather(w_qkv.reshape(width, -1), "row", axis=0)
     factor_one = lax.rsqrt(col_total(inputs * inputs) / D + EPS_NORM)
@@ -509,31 +534,29 @@
     here_ranks = [here(values) for values in unit_ranks]
     here_gates = [unit_gates(gates), unit_gates(far_gates)]
 
-    def hot(number, start=0, count=token_block):
-        chosen = unit_ranks[number][:, :, None, start : start + count]
-        return chosen == jnp.arange(slots, dtype=jnp.int32)[None, None, :, None]
-
-    def dispatch(number, rows):
-        picked = jnp.einsum(
-            "dcst,tf->dcsf", hot(number).astype(low), rows, preferred_element_type=jnp.float32
-        )
-        return picked.astype(low).reshape(dl_n * col_n, slots, width)
+    def dispatch(number, blocks):
+        ranks = unit_ranks[number].reshape(dl_n * col_n, token_block)
+        return pick_slots(ranks, slots, [[block] for block in blocks])[:, 0]
 
     def to_experts(values):
         return to_owners(values, ("dl", "col")).reshape(dl_n, col_n, slots, width)
 
-    def token_sums(number, values):
-        values = values.reshape(dl_n, col_n, slots, width)
+    def hot(number, k):
+        chosen = unit_ranks[number][:, :, None, k * tokens_row : (k + 1) * tokens_row]
+        return (chosen == jnp.arange(slots, dtype=jnp.int32)[None, None, :, None]).astype(low)
+
+    def token_sums(number, values, half=0):
+        def partial(k):
+            own = values.reshape(dl_n, col_n, -1, slots, width)[:, :, half]
+            return jnp.einsum("dcst,dcsf->tf", hot(number, k), own, preferred_element_type=jnp.float32)
+
         total = None
         for k in range(1, row_n):
-            chosen = hot(number, k * tokens_row, tokens_row).astype(low)
-            part = jnp.einsum("dcst,dcsf->tf", chosen, values, preferred_element_type=jnp.float32)
+            part = partial(k)
             values = after(values, part)
             part = lax.ppermute(part, "row", [(i, (i + k) % row_n) for i in range(row_n)])
             total = part if total is None else total + part
-        chosen = hot(number, 0, tokens_row).astype(low)
-        own = jnp.einsum("dcst,dcsf->tf", chosen, values, preferred_element_type=jnp.float32)
-        return own + total
+        return partial(0) + total, values
 
     def here_hot(number):
         return here_ranks[number][:, None, :] == jnp.arange(slots, dtype=jnp.int32)[None, :, None]
@@ -566,84 +589,82 @@
     grad_low = grad_rows.astype(low)
     far_low = to_owners(jnp.broadcast_to(grad_low, (dh_n,) + grad_low.shape), "dh")
 
-    def all_features(values):
-        values = jnp.roll(jnp.stack(ring(values, "col")), col_i, axis=0)
-        return values
-
-    def all_rows(values):
-        return jnp.concatenate(ring(values, "row"), axis=1)
-
-    def dispatch_wide(number, rows):
-        picked = jnp.einsum(
-            "dst,ctf->dcsf", here_hot(number).astype(low), rows, preferred_element_type=jnp.float32
-        )
-        return picked.astype(low)
+    def dispatch_wide(number, blocks):
+        return pick_slots(here_ranks[number], slots, blocks)
+
+    def by_row(blocks):
+        parts = [ring(block, "row") for block in blocks]
+        return [[part[k] for part in parts] for k in range(row_n)]
 
     own_wide = ring(after(grad_low, factor_one), "col")
     own_wide[-1] = after(own_wide[-1], terms, slot_gate, *here_ranks, *unit_ranks)
-    own_wide = jnp.roll(jnp.stack(own_wide), col_i, axis=0)
-    own_picked = dispatch_wide(0, all_rows(own_wide))
-    own_grads = to_owners(after(own_picked, far_low), "dl")
+    own_picked = dispatch_wide(0, by_row(own_wide))
+
+    mixed, log_total, tops = attend_forward(packed, ids)
+    own_grads = to_owners(after(own_picked, mixed, far_low), "dl")
     my_gate = to_owners(after(slot_gate, own_grads), "dl")
     my_gate = jnp.swapaxes(my_gate, 0, 1)[..., None]
+    far_low = after(far_low, mixed)
     far_low = lax.dynamic_index_in_dim(far_low, dh_n - 1 - dh_i, 0, False)
-    far_wide = all_features(far_low)
-
-    packed = after(packed, own_picked)
-    mixed, log_total, tops = attend_forward(packed, ids)
+    far_wide = ring(far_low, "col")
     heads = lax.all_gather(mixed, "col", axis=0)
-    heads = after(heads, own_grads, *in_pieces, *down_pieces).reshape(seqs_row, KVH, LEN, GROUP * HD)
+    heads = after(heads, *in_pieces, *down_pieces).reshape(seqs_row, KVH, LEN, GROUP * HD)
     out_row = lax.all_gather(after(w_out[0], packed), "row", axis=0)
     attn = jnp.einsum("sgth,ghf->stf", heads, out_row, preferred_element_type=jnp.float32)
     hidden = inputs + attn.reshape(tokens_row, width)
 
     factor_two = lax.rsqrt(col_total(hidden * hidden) / D + EPS_NORM)
     normed_two = (hidden * factor_two[:, None] * gains[1][None, :]).astype(low)
+    normed_two = after(normed_two, far_wide[-1])
     far_two = from_far(normed_two)
-    far_picked = dispatch_wide(1, all_rows(after(far_wide, normed_two)))
-    far_grads = to_owners(after(far_picked, my_gate), "dl")
-
     def spread(piece, pairs):
         return lax.ppermute(after(piece, normed_two), ("row", "col"), pairs)
 
     for k in range(1, grid_n):
         down_pieces[k] = spread(down_pieces[k], piece_pairs[k])
         in_pieces[k] = spread(in_pieces[k], piece_pairs[k])
-    weights_in, weights_down = join_weights(
-        in_pieces, down_pieces, jnp.stack([row_i, col_i]).astype(jnp.int32), row_n, col_n
-    )
+    far_wide[-1] = after(far_wide[-1], down_pieces[col_n])
+    far_picked = dispatch_wide(1, by_row(far_wide))
+    far_grads = to_owners(after(far_picked, my_gate), "dl")
+    place = jnp.stack([row_i, col_i]).astype(jnp.int32)
+    weights_in, weights_down = join_weights(in_pieces, down_pieces, place, row_n, col_n)
     far_two = after(far_two, weights_in)
-    far_slots = dispatch(1, row_blocks(far_two))
-    far_rows = to_experts(after(far_slots, far_grads))
-    own_slots = dispatch(0, after(row_blocks(normed_two), far_slots))
+    far_slots = after(dispatch(1, ring(far_two, "row")), far_grads)
+    far_rows = to_experts(far_slots)
+    own_two = ring(normed_two, "row")
+    own_two[-1] = after(own_two[-1], far_slots)
+    own_slots = dispatch(0, own_two)
     own_rows = to_experts(after(own_slots, far_rows))
 
     far_back, far_weighted, far_pair = expert_passes(
-        far_rows, far_grads, my_gate[1], weights_in, weights_down
-    )
+        place, far_rows, far_grads, my_gate[1], weights_in, weights_down
+    )
+    own_rows = after(own_rows, far_back)
     own_back, own_weighted, own_pair = expert_passes(
-        after(own_rows, far_back), own_grads, my_gate[0], weights_in, weights_down
+        place, own_rows, own_grads, my_gate[0], weights_in, weights_down
     )
 
     def send_back(values):
-        return to_owners(values.reshape(dl_n * col_n, slots, width), ("dl", "col"))
-
-    far_back = send_back(after(far_back, own_rows))
+        return to_owners(values.reshape(dl_n * col_n, 1, slots, width), ("dl", "col"))
+
+    far_back = send_back(far_back)
     slot_out = expert_outputs([own_weighted, far_weighted], weights_down)
     own_back = send_back(after(own_back, far_back))
-    far_sums = token_sums(1, after(far_back, slot_out)).astype(low)
+    far_sums = token_sums(1, after(far_back, slot_out))[0].astype(low)
     in_grad, down_grad = expert_grads(
+        place,
         [
             (own_rows, own_grads, after(own_weighted, far_sums), own_pair),
             (far_rows, far_grads, far_weighted, far_pair),
         ],
         row_n,
     )
+    own_back = after(own_back, in_grad)
     far_sums = from_far(far_sums)
-    own_back = after(own_back, in_grad)
-    own_sums = token_sums(0, own_back)
+    slot_out = after(slot_out, own_back)
+    slot_out = to_owners(slot_out.reshape((dl_n * col_n,) + slot_out.shape[2:]), ("dl", "col"))
+    own_sums, _ = token_sums(0, own_back)
     grad_normed_two = own_sums + far_sums.astype(jnp.float32)
-    slot_out = to_owners(after(slot_out, own_back).reshape((dl_n * col_n,) + slot_out.shape[2:]), ("dl", "col"))
 
     def block_grads(grads):
         grads = to_owners(grads.reshape((grid_n,) + grads.shape[2:]), ("row", "col"))
@@ -651,6 +672,7 @@
             grads = grads.astype(jnp.float32)
             grads = jnp.sum(grads.reshape((experts_dp, share) + grads.shape[1:]), axis=1)
         return grads
+
 
     grad_hidden_norm, grad_gain_two = norm_backward(hidden, factor_two, gains[1], grad_normed_two)
     grad_hidden = grad_rows + grad_hidden_norm
@@ -667,17 +689,16 @@
     full_top = lax.dynamic_update_slice(
         full_top, jnp.max(tops, axis=(1, 2))[None], (group_i, jnp.zeros((), jnp.int32))
     )
-    own_out, far_out = slot_out[:, 0], slot_out[:, 1]
-    far_out_sums = token_sums(1, after(far_out, terms)).astype(low)
-    down_grad = after(down_grad, grad_heads)
+    far_out_sums, slot_out = token_sums(1, after(slot_out, terms), 1)
+    far_out_sums = far_out_sums.astype(low)
     grad_heads = after(grad_heads, far_out_sums)
+    far_out_sums = to_owners(jnp.broadcast_to(far_out_sums, (dh_n,) + far_out_sums.shape), "dh")
     grad_packed = attend_backward(packed, ids, log_total, grad_heads)
     packed_all = lax.all_gather(grad_packed, "col", axis=0).reshape(seqs_row, KVH, LEN, -1)
 
-    own_out_sums = token_sums(0, after(own_out, grad_packed))
+    own_out_sums, _ = token_sums(0, after(slot_out, grad_packed))
     packed_all = after(packed_all, own_out_sums)
-    far_out_sums = lax.ppermute(far_out_sums, "dh", far_pairs())
-    block_output = hidden + own_out_sums + far_out_sums.astype(jnp.float32)
+    grad_down = block_grads(after(down_grad, far_out_sums))
 
     def owner_sums(left, right):
         columns = right.shape[-1]
@@ -692,20 +713,27 @@
             left = after(left, part)
             part = lax.ppermute(part, "row", [(i, (i + k) % row_n) for i in range(row_n)])
             total = part if total is None else total + part
-        total = (term(0) + total).astype(low)
-        total = to_owners(total, ("dh", "dl")).reshape(dp_n, -1, columns)
-        return jnp.sum(total.astype(jnp.float32), axis=0)
+        return (term(0) + total).astype(low)
+
+    def dp_sums(total):
+        parts = to_owners(total, ("dh", "dl")).reshape(dp_n, -1, total.shape[1])
+        return jnp.sum(parts.astype(jnp.float32), axis=0)
 
     grad_normed_one = jnp.einsum(
         "sgth,gfh->stf", packed_all, qkv_row, preferred_element_type=jnp.float32
     ).reshape(tokens_row, width)
-    grad_out = owner_sums(grad_attn.reshape(seqs_row, LEN, width), after(heads, grad_heads))
-    grad_gate_up = block_grads(after(in_grad, packed_all))
-    grad_qkv = owner_sums(normed_one.reshape(seqs_row, LEN, width), packed_all)
-    grad_down = block_grads(down_grad)
-    grad_gate_up = jnp.swapaxes(grad_gate_up, 1, 2)
+    out_total = owner_sums(grad_attn.reshape(seqs_row, LEN, width), after(heads, grad_heads))
+    grad_gate_up = jnp.swapaxes(block_grads(after(in_grad, packed_all)), 1, 2)
     grad_gate_up = with_layout_constraint(grad_gate_up, Layout((0, 1, 2, 3)))
-    grad_out, grad_qkv = grad_out.T[None], grad_qkv[:, None]
+    qkv_total = owner_sums(normed_one.reshape(seqs_row, LEN, width), packed_all)
+    far_out_sums = after(far_out_sums, qkv_total)
+    far_out_sums = lax.dynamic_index_in_dim(far_out_sums, dh_n - 1 - dh_i, 0, False)
+    block_output = hidden + own_out_sums + far_out_sums.astype(jnp.float32)
+    totals = after(jnp.concatenate([qkv_total, out_total], axis=1), grad_gate_up)
+    grad_gate_up, grad_down = after(grad_gate_up, qkv_total), after(grad_down, qkv_total)
+    totals = dp_sums(totals)
+    grad_qkv, grad_out = totals[:, None, : qkv_total.shape[1]], totals[:, qkv_total.shape[1] :].T[None]
+    grad_normed_one = after(grad_normed_one, qkv_total)
     grad_input_norm, grad_gain_one = norm_backward(inputs, factor_one, gains[0], grad_normed_one)
     input_grad = grad_hidden + grad_input_norm
 

time: 1100 us -> 1070 us (0.973)
  Pallas kernels: 126 us -> 177 us
  matrix products: 158 us -> 114 us
  other arithmetic: 110 us -> 86.3 us
  local copies, waits for them, and re-layouts: 119 us -> 98.9 us
    reduce_scatter x1, waiting for transfers between devices: 0.02 us -> 63.7 us  [on_device(): packed = lax.psum_scatter(terms, 'col', scatter_dimension=0, tiled=True)]
    ppermute x7 -> x9, waiting for transfers between devices: 61.3 us -> 7.15 us  [ring(): lax.ppermute(values, axis, [(i, (i - k) % count) for i in range(count)])]
    pallas_call x0 -> x4, Pallas kernels: none -> 50.6 us  [pick_slots(): pl.pallas_call(pick_kernel, grid=(units,), in_specs=[pl.BlockSpec((1, 1,...]
    dot_general x12 -> x8, matrix products: 111 us -> 65.4 us  [partial(): jnp.einsum('dcst,dcsf->tf', hot(number, k), own, preferred_element_type=j...]
    ppermute x1 -> x0, waiting for transfers between devices: 39.3 us -> none  [on_device(): far_out_sums = lax.ppermute(far_out_sums, 'dh', far_pairs())]
    all_gather x1, waiting for transfers between devices: 8.36 us -> 34.5 us  [on_device(): lax.all_gather(grad_packed, 'col', axis=0).reshape(seqs_row, KVH, LEN, -1)]
    unnamed x151 -> x191, local copies, waits for them, and re-layouts: 51.2 us -> 43.2 us
    all_to_all x12 -> x13, starting transfers between devices: 66.4 us -> 69.2 us  [to_owners(): return lax.all_to_all(values, axes, split_axis=0, concat_axis=0, tiled=True)]
  transfers between devices with their start and end apart: 47 -> 49, of which waited for: 21 -> 23; matrix products, arithmetic and copies ran while one was open for 30% -> 22% of each run, Pallas kernels for 12% -> 15%
where the time goes in v2:
time: 1070 us; the launch traced here: 1060 us
  waiting for transfers between devices  450 us (42%)
  Pallas kernels  177 us (17%)
  matrix products  114 us (11%)
  local copies, waits for them, and re-layouts  98.9 us (9%)
  starting transfers between devices  86.8 us (8%)
  other arithmetic  86.3 us (8%)
  blocking collectives  28.7 us (3%)
  between operations  16.9 us (2%)
    all_to_all x13, waiting for transfers between devices, to_owners(): return lax.all_to_all(values, axes, split_axis=0, concat_axis=0, tiled=True)  143 us
    ppermute x6, waiting for transfers between devices, spread(): return lax.ppermute(after(piece, normed_two), ('row', 'col'), pairs)  76 us
    all_gather x2, waiting for transfers between devices, from_far(): both = lax.all_gather(values, 'dh', axis=0)  72.8 us
    all_to_all x13, starting transfers between devices, to_owners(): return lax.all_to_all(values, axes, split_axis=0, concat_axis=0, tiled=True)  69.2 us
    dot_general x8, matrix products, partial(): jnp.einsum('dcst,dcsf->tf', hot(number, k), own, preferred_element_type=j...  65.4 us
    reduce_scatter x1, waiting for transfers between devices, on_device(): packed = lax.psum_scatter(terms, 'col', scatter_dimension=0, tiled=True)  63.7 us
    pallas_call x4, Pallas kernels, pick_slots(): pl.pallas_call(pick_kernel, grid=(units,), in_specs=[pl.BlockSpec((1, 1,...  50.6 us
    unnamed x191, local copies, waits for them, and re-layouts  43.2 us
  transfers between devices with their start and end apart: 49, of which 23 were waited for; matrix products, arithmetic and copies ran while one was open for 22% of the time, Pallas kernels for 15%

profile of v2, /device:TPU:0, one launch (start us, length us, event | category | flops | bytes accessed | tf_op | source)
XLA Modules:
  0.0 1058.9 jit_solution(12750644663811758780)
XLA Ops:
  18.3 4.9 psum.28
  26.7 7.8 convolution_convert_fusion
  40.8 5.2 all-to-all-start
  59.4 63.7 %reduce-scatter.3.cloned.1.call-done.query_ref.key_ref.value_ref.refs_1_ = bf16[1024,1024]{1,0:T(8,128)(2,1)} async-done(((bf16[2048,1024]{1,0:T(8,128)(2,1)}), bf16[1024,1024]{1,0:T(8,128)(2,1)}) %reduce-scatter.3.cloned.1.call-update) | async-done | bytes 2097168 | tf_op jit(solution)/shard_map/reduce_scatter | solution.py:507
  124.6 19.5 %shard_map.400 = (bf16[1024,768]{1,0:T(8,128)(2,1)}, f32[6,1,1024]{2,1,0:T(1,128)S(1)}, f32[6,1,1024]{2,1,0:T(1,128)S(1)}) custom-call(bf16[1024,1024]{1,0:T(8,128)(2,1)S(1)} %copy-done.1, bf16[1024,1024]{1,0:T(8,128)(2,1)S(1)} %copy-done.1, bf16[1024,1024]{1,0:T(8,128)(2,1)S(1)} %copy-done.1, s32[1,1024]{1,0:T(1,128)S(1)} %fusion.83.id_row_ref, ...), custom_call_target="tpu_custom_call" | custom-call | tf_op jit(solution)/shard_map/pallas_call | solution.py:131
  154.6 13.3 %shard_map.418.refs_0_ = bf16[4,2,320,768]{3,2,1,0:T(8,128)(2,1)} custom-call(s32[4,1,2048]{2,1,0:T(1,128)} %fusion.116.ranks_ref, bf16[1024,768]{1,0:T(8,128)(2,1)} %shard_map.416.refs_0_, bf16[1024,768]{1,0:T(8,128)(2,1)} %shard_map.417.refs_1_, bf16[1024,768]{1,0:T(8,128)(2,1)} %collective-permute-done.15.refs_2_, bf16[1024,768]{1,0:T(8,128)(2,1)} %copy-done.49), custom_call_target="tpu_custom_call" | custom-call | tf_op jit(solution)/shard_map/pallas_call | solution.py:227
  167.9 4.8 all-to-all-start.1
  173.3 5.9 constant_dynamic-slice_fusion.1
  189.4 6.1 all-gather.15.cloned.1.call-done
  195.6 12.8 %all-gather.17.cloned.1.call-done = bf16[1536,768]{1,0:T(8,128)(2,1)} async-done(((bf16[768,768]{1,0:T(8,128)(2,1)}), bf16[1536,768]{1,0:T(8,128)(2,1)}) %all-gather.17.cloned.1.call-update) | async-done | bytes 2359312 | tf_op jit(solution)/shard_map/all_gather | solution.py:612
  208.4 7.0 multiply_reduce_fusion.4
  215.4 8.7 psum.29
  236.4 12.7 %shard_map.415.refs_0_ = bf16[4,2,320,768]{3,2,1,0:T(8,128)(2,1)} custom-call(s32[4,1,2048]{2,1,0:T(1,128)} %fusion.117.ranks_ref, bf16[1024,768]{1,0:T(8,128)(2,1)} %dynamic-slice_bitcast_fusion.1.refs_0_, bf16[1024,768]{1,0:T(8,128)(2,1)} %shard_map.414.refs_1_, bf16[1024,768]{1,0:T(8,128)(2,1)} %copy-done.48, ...), custom_call_target="tpu_custom_call" | custom-call | tf_op jit(solution)/shard_map/pallas_call | solution.py:227
  250.5 4.8 all-to-all-start.3
  259.6 63.4 %collective-permute-done.7.refs_5_ = bf16[384,768]{1,0:T(8,128)(2,1)S(1)} collective-permute-done((bf16[384,768]{1,0:T(8,128)(2,1)}, bf16[384,768]{1,0:T(8,128)(2,1)S(1)}, u32[]{:S(2)}, u32[]{:S(2)}) %collective-permute-start.7) | collective-permute-done | bytes 589856 | tf_op jit(solution)/shard_map/ppermute | solution.py:621
  323.0 10.9 %collective-permute-done.9.refs_7_ = bf16[384,768]{1,0:T(8,128)(2,1)S(1)} collective-permute-done((bf16[384,768]{1,0:T(8,128)(2,1)}, bf16[384,768]{1,0:T(8,128)(2,1)S(1)}, u32[]{:S(2)}, u32[]{:S(2)}) %collective-permute-start.9) | collective-permute-done | bytes 589856 | tf_op jit(solution)/shard_map/ppermute | solution.py:621
  347.9 12.4 %shard_map.413 = bf16[8,1,320,768]{3,2,1,0:T(8,128)(2,1)} custom-call(s32[8,1,2048]{2,1,0:T(1,128)} %broadcast_in_dim_reshape.7.ranks_ref, bf16[1024,768]{1,0:T(8,128)(2,1)} %shard_map.412.refs_0_, bf16[1024,768]{1,0:T(8,128)(2,1)} %copy-done.50), custom_call_target="tpu_custom_call" | custom-call | tf_op jit(solution)/shard_map/pallas_call | solution.py:227
  360.4 4.7 all-to-all-start.4
  369.7 12.2 %shard_map.424 = bf16[8,1,320,768]{3,2,1,0:T(8,128)(2,1)} custom-call(s32[8,1,2048]{2,1,0:T(1,128)} %broadcast_in_dim_reshape.6.ranks_ref, bf16[1024,768]{1,0:T(8,128)(2,1)} %shard_map.404.refs_1_.refs_0_, bf16[1024,768]{1,0:T(8,128)(2,1)} %shard_map.423.refs_1_), custom_call_target="tpu_custom_call" | custom-call | tf_op jit(solution)/shard_map/pallas_call | solution.py:227
  381.9 31.1 %all-to-all-done.4 = bf16[8,320,768]{2,1,0:T(8,128)(2,1)} async-done(((bf16[8,320,768]{2,1,0:T(8,128)(2,1)}), bf16[8,320,768]{2,1,0:T(8,128)(2,1)}, u32[]{:S(2)}, u32[]{:S(2)}) %all-to-all-start.4) | async-done | bytes 3932192 | tf_op jit(solution)/shard_map/all_to_all | solution.py:81
  413.0 7.0 all-to-all-start.5
  421.1 21.4 %shard_map.426 = (bf16[4,2,320,768]{3,2,1,0:T(8,128)(2,1)}, bf16[4,320,768]{2,1,0:T(8,128)(2,1)}, bf16[4,320,1536]{2,1,0:T(8,128)(2,1)}) custom-call(s32[2]{0:T(128)} %copy-done.21, bf16[4,2,320,768]{3,2,1,0:T(8,128)(2,1)} %bitcast.46.refs_1_.rows_ref.refs_4_, bf16[4,2,320,768]{3,2,1,0:T(8,128)(2,1)} %all-to-all-done.3.refs_1_.grads_ref.refs_5_, ...), custom_call_target="tpu_custom_call" | custom-call | tf_op jit(solution)/shard_map/pallas_call | solution.py:259
  442.5 24.1 %all-to-all-done.5 = bf16[8,320,768]{2,1,0:T(8,128)(2,1)} async-done(((bf16[8,320,768]{2,1,0:T(8,128)(2,1)}), bf16[8,320,768]{2,1,0:T(8,128)(2,1)}, u32[]{:S(2)}, u32[]{:S(2)}) %all-to-all-start.5) | async-done | bytes 3932192 | tf_op jit(solution)/shard_map/all_to_all | solution.py:81
  466.6 8.1 all-to-all-start.6
  475.8 21.4 %shard_map.428 = (bf16[4,2,320,768]{3,2,1,0:T(8,128)(2,1)}, bf16[4,320,768]{2,1,0:T(8,128)(2,1)}, bf16[4,320,1536]{2,1,0:T(8,128)(2,1)}) custom-call(s32[2]{0:T(128)} %copy-done.21, bf16[4,2,320,768]{3,2,1,0:T(8,128)(2,1)} %shard_map.427.rows_ref.refs_0_, bf16[4,2,320,768]{3,2,1,0:T(8,128)(2,1)} %all-to-all-done.1.refs_1_.grads_ref, ...), custom_call_target="tpu_custom_call" | custom-call | tf_op jit(solution)/shard_map/pallas_call | solution.py:259
  497.3 23.6 %all-to-all-done.6.refs_1_.refs_0_ = bf16[8,1,320,768]{3,2,1,0:T(8,128)(2,1)} async-done(((bf16[8,1,320,768]{3,2,1,0:T(8,128)(2,1)}), bf16[8,1,320,768]{3,2,1,0:T(8,128)(2,1)}, u32[]{:S(2)}, u32[]{:S(2)}) %all-to-all-start.6) | async-done | bytes 3932192 | tf_op jit(solution)/shard_map/all_to_all | solution.py:81
  520.8 7.8 all-to-all-start.7
  531.8 7.4 shard_map.429.refs_1_.refs_0_
  542.5 6.9 fusion.35.refs_1_
  551.0 4.2 collective-permute-done.17
  555.2 8.4 fusion.23.refs_1_
  563.6 33.5 %shard_map.434 = (bf16[2,2,2,768,384]{4,3,2,1,0:T(8,128)(2,1)}, bf16[2,2,384,768]{3,2,1,0:T(8,128)(2,1)}) custom-call(s32[2]{0:T(128)} %copy-done.21, bf16[4,2,320,768]{3,2,1,0:T(8,128)(2,1)} %shard_map.427.rows_ref.refs_0_, bf16[4,2,320,768]{3,2,1,0:T(8,128)(2,1)} %all-to-all-done.1.refs_1_.grads_ref, bf16[4,320,768]{2,1,0:T(8,128)(2,1)} %shard_map.433.refs_2_, ...), custom_call_target="tpu_custom_call" | custom-call | tf_op jit(solution)/shard_map/pallas_call | solution.py:402
  597.2 5.2 all-to-all-start.8
  603.0 6.9 fusion.39.refs_1_
  611.6 72.8 %all-gather.21.cloned.1.call-done = bf16[2048,768]{1,0:T(8,128)(2,1)} async-done(((bf16[1024,768]{1,0:T(8,128)(2,1)}), bf16[2048,768]{1,0:T(8,128)(2,1)}) %all-gather.21.cloned.1.call-update) | async-done | bytes 3145744 | tf_op jit(solution)/shard_map/all_gather | solution.py:482
  684.4 10.4 multiply_reduce_fusion
  694.8 10.1 psum.30
  704.9 4.9 convert_bitcast_fusion.1
  717.2 6.3 all-to-all-done.8.refs_0_
  723.5 7.0 fusion.38.refs_1_
  736.3 8.8 fusion.22.refs_1_
  745.1 14.8 %reduce-scatter.5.cloned.1.call-done.refs_0_ = bf16[1024,768]{1,0:T(8,128)(2,1)} async-done(((bf16[2048,768]{1,0:T(8,128)(2,1)}), bf16[1024,768]{1,0:T(8,128)(2,1)}) %reduce-scatter.5.cloned.1.call-update) | async-done | bytes 1572880 | tf_op jit(solution)/shard_map/reduce_scatter | solution.py:687
  761.3 20.7 %shard_map.441.refs_1_ = bf16[1024,1024]{1,0:T(8,128)(2,1)} custom-call(bf16[1024,1024]{1,0:T(8,128)(2,1)S(1)} %copy-done.2, bf16[1024,1024]{1,0:T(8,128)(2,1)S(1)} %copy-done.2, bf16[1024,1024]{1,0:T(8,128)(2,1)S(1)} %copy-done.2, bf16[1024,768]{1,0:T(8,128)(2,1)S(1)} %copy-done.7, f32[6,1,1024]{2,1,0:T(1,128)S(1)} %copy-done.20, s32[1,1024]{1,0:T(1,128)S(1)} %copy-done.16, ...), custom_call_target="tpu_custom_call" | custom-call | tf_op jit(solution)/shard_map/pallas_call | solution.py:187
  782.1 8.5 fusion.42.refs_1_
  793.9 4.3 all-to-all-start.9
  798.2 5.8 fusion.46.refs_1_
  804.6 8.6 bitcast_add_fusion.refs_1_
  813.2 34.5 %all-gather.23.cloned.1.call-done = bf16[2048,1024]{1,0:T(8,128)(2,1)} async-done(((bf16[1024,1024]{1,0:T(8,128)(2,1)}), bf16[2048,1024]{1,0:T(8,128)(2,1)}) %all-gather.23.cloned.1.call-update) | async-done | bytes 4194320 | tf_op jit(solution)/shard_map/all_gather | solution.py:697
  847.7 5.6 fusion.26.refs_1_
  853.5 5.1 add_convert_fusion.1
  858.6 11.2 %all-to-all-done.9.refs_0_.refs_1_ = bf16[2,1024,768]{2,1,0:T(8,128)(2,1)S(1)} async-done(((bf16[2,1024,768]{2,1,0:T(8,128)(2,1)}), bf16[2,1024,768]{2,1,0:T(8,128)(2,1)S(1)}, u32[]{:S(2)}, u32[]{:S(2)}) %all-to-all-start.9) | async-done | bytes 3145760 | tf_op jit(solution)/shard_map/all_to_all | solution.py:81
  871.5 4.7 all-to-all-start.12
  876.3 9.4 copy.372
  887.6 8.4 fusion.30.refs_0_
  896.1 8.7 collective-permute-done.23
  904.9 5.5 add_convert_fusion.refs_1_
  915.0 4.9 psum.31
  920.0 5.2 all-to-all-start.10
  925.2 12.2 %fusion.90 = (bf16[4,384,768]{2,1,0:T(8,128)(2,1)}, f32[4,384,768]{2,1,0:T(8,128)}, f32[4,384,768]{2,1,0:T(8,128)}, f32[4,384,768]{2,1,0:T(8,128)}) fusion(f32[4,384,768]{2,1,0:T(8,128)} %param.49, bf16[4,384,768]{2,1,0:T(8,128)(2,1)} %shard_map.455, f32[4,384,768]{2,1,0:T(8,128)} %param.50, f32[4,384,768]{2,1,0:T(8,128)} %param.51), kind=kLoop, calls=%fused_computation.202 | loop fusion | flops 20054016 | bytes 33030144 | tf_op jit(solution)/shard_map/convert_element_type | solution.py:790
  943.8 4.5 convert_add_fusion.4
  950.3 4.9 reshape.273
  961.2 17.8 %all-to-all-done.10 = bf16[4,2,768,384]{3,1,2,0:T(2,128)(2,1)} async-done(((bf16[4,2,768,384]{3,1,2,0:T(2,128)(2,1)}), bf16[4,2,768,384]{3,1,2,0:T(2,128)(2,1)}, u32[]{:S(2)}, u32[]{:S(2)}) %all-to-all-start.10) | async-done | bytes 4718624 | tf_op jit(solution)/shard_map/all_to_all | solution.py:81
  982.7 33.8 %fusion.91 = (bf16[4,768,2,384]{3,2,1,0:T(2,128)(2,1)}, f32[4,768,2,384]{3,2,1,0:T(2,128)}, f32[4,768,2,384]{3,2,1,0:T(2,128)}, f32[4,768,2,384]{3,2,1,0:T(2,128)}) fusion(f32[4,768,2,384]{3,2,1,0:T(2,128)} %param.46, bf16[4,768,2,384]{3,2,1,0:T(2,128)(2,1)} %shard_map.453, f32[4,768,2,384]{3,2,1,0:T(2,128)} %param.47, f32[4,768,2,384]{3,2,1,0:T(2,128)} %param.48), kind=kLoop, calls=%fused_computation.203 | loop fusion | flops 40108032 | bytes 66060288 | tf_op jit(solution)/shard_map/convert_element_type | solution.py:786
  1016.5 28.4 %all-to-all-done.11 = bf16[8,96,1792]{2,1,0:T(8,128)(2,1)S(1)} async-done(((bf16[8,96,1792]{2,1,0:T(8,128)(2,1)}), bf16[8,96,1792]{2,1,0:T(8,128)(2,1)S(1)}, u32[]{:S(2)}, u32[]{:S(2)}) %all-to-all-start.11) | async-done | bytes 2752544 | tf_op jit(solution)/shard_map/all_to_all | solution.py:81
  (433 shorter events, 156.1 us)
Async XLA Ops:
  7.2 19.5 %all-gather.13.cloned.1.call-start = ((), (), s32[]{:S(2)}) async-start(), calls=%async_computation.17 | async-start | bytes 4718592 | tf_op jit(solution)/shard_map/all_gather | solution.py:493
  9.7 113.4 %reduce-scatter.3.cloned.1.call-start = ((), (), s32[]{:S(2)}) async-start(), calls=%async_computation.15 | async-start | bytes 6291456 | tf_op jit(solution)/shard_map/reduce_scatter | solution.py:507
  9.7 15.1 %collective-permute-start.2 = (s32[1,1024]{1,0:T(1,128)S(1)}, s32[1,1024]{1,0:T(1,128)S(1)}, u32[]{:S(2)}, u32[]{:S(2)}) collective-permute-start(s32[1,1024]{1,0:T(1,128)S(1)} %copy-done.83), channel_id=1, source_target_pairs={{0,1},{1,0},{2,3},{3,2},{4,5},{5,4},{6,7},{7,6},{8,9},{9,8},{10,11... | collective-permute-start | bytes 12296 | tf_op jit(solution)/shard_map/ppermute | solution.py:489
  12.7 12.7 %collective-permute-start.1 = (f32[4,2048]{1,0:T(4,128)S(1)}, f32[4,2048]{1,0:T(4,128)S(1)}, u32[]{:S(2)}, u32[]{:S(2)}) collective-permute-start(f32[4,2048]{1,0:T(4,128)S(1)} %copy-done.80), channel_id=1, source_target_pairs={{0,16},{16,0},{1,17},{17,1},{2,18},{18,2},{3,19},{19,3},{4,20},{20... | collective-permute-start | bytes 98312 | tf_op jit(solution)/shard_map/ppermute | solution.py:496
  15.3 10.2 collective-permute-start
  23.3 200.8 %copy-start.72 = (f32[768]{0:T(1024)}, f32[768]{0:T(1024)S(1)}, u32[]{:S(2)}) copy-start(f32[768]{0:T(1024)S(1)} %get-tuple-element.210) | copy-start | bytes 9220
  40.8 127.1 %all-to-all-start = ((bf16[2,1024,768]{2,1,0:T(8,128)(2,1)}), bf16[2,1024,768]{2,1,0:T(8,128)(2,1)}, u32[]{:S(2)}, u32[]{:S(2)}) async-start(bf16[2,1024,768]{2,1,0:T(8,128)(2,1)} %broadcast_in_dim.64), calls=%async_computation.1 | async-start | bytes 6291456 | tf_op jit(solution)/shard_map/all_to_all | solution.py:81
  46.0 149.6 %all-gather.15.cloned.1.call-start = ((), (), s32[]{:S(2)}) async-start(), calls=%async_computation.18 | async-start | bytes 4718592 | tf_op jit(solution)/shard_map/all_gather | solution.py:610
  46.1 104.6 %collective-permute-start.15 = (bf16[1024,768]{1,0:T(8,128)(2,1)}, bf16[1024,768]{1,0:T(8,128)(2,1)}, u32[]{:S(2)}, u32[]{:S(2)}) collective-permute-start(bf16[1024,768]{1,0:T(8,128)(2,1)} %shard_map.416.refs_0_), channel_id=1, source_target_pairs={{0,2},{2,0},{1,3},{3,1},{4,6},{6,4},{5,7},{7,5},{8,10},{10,8},{9,1... | collective-permute-start | bytes 4718600 | tf_op jit(solution)/shard_map/ppermute | solution.py:489
  46.2 103.6 %collective-permute-start.14 = (bf16[1024,768]{1,0:T(8,128)(2,1)}, bf16[1024,768]{1,0:T(8,128)(2,1)}, u32[]{:S(2)}, u32[]{:S(2)}) collective-permute-start(bf16[1024,768]{1,0:T(8,128)(2,1)} %shard_map.416.refs_0_), channel_id=1, source_target_pairs={{0,1},{1,0},{2,3},{3,2},{4,5},{5,4},{6,7},{7,6},{8,9},{9,8},{10,11... | collective-permute-start | bytes 4718600 | tf_op jit(solution)/shard_map/ppermute | solution.py:489
  50.6 99.2 %copy-start.37 = (s32[2,4,2,2,2048]{4,3,2,1,0:T(2,128)}, s32[2,4,2,2,2048]{4,3,2,1,0:T(2,128)S(1)}, u32[]{:S(2)}) copy-start(s32[2,4,2,2,2048]{4,3,2,1,0:T(2,128)S(1)} %broadcast_select_fusion.1) | copy-start | bytes 786436
  52.3 70.7 %copy-start.15 = (s32[1,1024]{1,0:T(1,128)}, s32[1,1024]{1,0:T(1,128)S(1)}, u32[]{:S(2)}) copy-start(s32[1,1024]{1,0:T(1,128)S(1)} %fusion.83.id_row_ref) | copy-start | bytes 12292
  52.6 70.5 %copy-start.11 = (s32[1024,1]{1,0:T(8,128)}, s32[1024,1]{1,0:T(8,128)S(1)}, u32[]{:S(2)}) copy-start(s32[1024,1]{1,0:T(8,128)S(1)} %copy.337.id_col_ref) | copy-start | bytes 12292
  59.1 175.3 %copy-start.39 = (s32[2,4,2,2,2048]{4,3,2,1,0:T(2,128)}, s32[2,4,2,2,2048]{4,3,2,1,0:T(2,128)S(1)}, u32[]{:S(2)}) copy-start(s32[2,4,2,2,2048]{4,3,2,1,0:T(2,128)S(1)} %broadcast_select_fusion) | copy-start | bytes 786436
  124.6 20.7 %copy-start.67 = (s32[1,4,1,1,2048]{4,3,2,1,0:T(1,128)S(1)}, s32[1,4,1,1,2048]{4,3,2,1,0:T(1,128)}, u32[]{:S(2)}) copy-start(s32[1,4,1,1,2048]{4,3,2,1,0:T(1,128)} %fusion.75) | copy-start | bytes 98308
  149.7 3.7 collective-permute-start.16
  167.9 62.9 %all-to-all-start.1 = ((bf16[4,2,320,768]{3,2,1,0:T(8,128)(2,1)}), bf16[4,2,320,768]{3,2,1,0:T(8,128)(2,1)}, u32[]{:S(2)}, u32[]{:S(2)}) async-start(bf16[4,2,320,768]{3,2,1,0:T(8,128)(2,1)} %shard_map.419), calls=%async_computation.2 | async-start | bytes 7864320 | tf_op jit(solution)/shard_map/all_to_all | solution.py:81
  172.7 35.7 %all-gather.17.cloned.1.call-start = ((), (), s32[]{:S(2)}) async-start(), calls=%async_computation.19 | async-start | bytes 3538944 | tf_op jit(solution)/shard_map/all_gather | solution.py:612
  182.1 45.4 %collective-permute-start.3 = (bf16[1024,768]{1,0:T(8,128)(2,1)}, bf16[1024,768]{1,0:T(8,128)(2,1)}, u32[]{:S(2)}, u32[]{:S(2)}) collective-permute-start(bf16[1024,768]{1,0:T(8,128)(2,1)} %dynamic-slice_bitcast_fusion.1.refs_0_), channel_id=1, source_target_pairs={{0,1},{1,0},{2,3},{3,2},{4,5},{5,4},{6,7},{7,6},{8,9},{9,8},{10,11... | collective-permute-start | bytes 4718600 | tf_op jit(solution)/shard_map/ppermute | solution.py:489
  227.5 2.3 collective-permute-start.8
  227.6 7.7 collective-permute-start.12
  230.6 4.7 collective-permute-start.13
  230.7 18.3 %all-to-all-start.2 = ((f32[4,2,320]{2,1,0:T(2,128)}), f32[4,2,320]{2,1,0:T(2,128)S(1)}, u32[]{:S(2)}, u32[]{:S(2)}) async-start(f32[4,2,320]{2,1,0:T(2,128)} %shard_map.420), calls=%async_computation.3 | async-start | bytes 24576 | tf_op jit(solution)/shard_map/all_to_all | solution.py:81
  250.5 109.8 %all-to-all-start.3 = ((bf16[4,2,320,768]{3,2,1,0:T(8,128)(2,1)}), bf16[4,2,320,768]{3,2,1,0:T(8,128)(2,1)}, u32[]{:S(2)}, u32[]{:S(2)}) async-start(bf16[4,2,320,768]{3,2,1,0:T(8,128)(2,1)} %shard_map.421), calls=%async_computation.4 | async-start | bytes 7864320 | tf_op jit(solution)/shard_map/all_to_all | solution.py:81
  255.3 84.4 %all-gather.19.cloned.1.call-start = ((), (), s32[]{:S(2)}) async-start(), calls=%async_computation.20 | async-start | bytes 4718592 | tf_op jit(solution)/shard_map/all_gather | solution.py:482
  256.0 78.0 %copy-start.8 = (bf16[1,768,2,384]{3,1,2,0:T(8,128)(2,1)S(1)}, bf16[1,768,2,384]{3,1,2,0:T(8,128)(2,1)}, u32[]{:S(2)}) copy-start(bf16[1,768,2,384]{3,1,2,0:T(8,128)(2,1)} %copy.462) | copy-start | bytes 3538948
  256.0 78.0 %copy-start.10 = (bf16[384,768]{1,0:T(8,128)(2,1)S(1)}, bf16[384,768]{1,0:T(8,128)(2,1)}, u32[]{:S(2)}) copy-start(bf16[384,768]{1,0:T(8,128)(2,1)} %get-tuple-element.242.refs_5_.refs_4_) | copy-start | bytes 1769476
  256.0 78.0 %copy-start.14 = (bf16[384,768]{1,0:T(8,128)(2,1)S(1)}, bf16[384,768]{1,0:T(8,128)(2,1)}, u32[]{:S(2)}) copy-start(bf16[384,768]{1,0:T(8,128)(2,1)} %copy-done.13) | copy-start | bytes 1769476
  256.0 77.9 %collective-permute-start.4 = (bf16[2,768,384]{2,1,0:T(8,128)(2,1)}, bf16[2,768,384]{2,1,0:T(8,128)(2,1)S(1)}, u32[]{:S(2)}, u32[]{:S(2)}) collective-permute-start(bf16[2,768,384]{2,1,0:T(8,128)(2,1)} %shard_map.405), channel_id=1, source_target_pairs={{0,1},{1,0},{2,3},{3,2},{4,5},{5,4},{6,7},{7,6},{8,9},{9,8},{10,11... | collective-permute-start | bytes 3538952 | tf_op jit(solution)/shard_map/ppermute | solution.py:621
  256.6 77.3 %collective-permute-start.5 = (bf16[2,768,384]{2,1,0:T(8,128)(2,1)}, bf16[2,768,384]{2,1,0:T(8,128)(2,1)}, u32[]{:S(2)}, u32[]{:S(2)}) collective-permute-start(bf16[2,768,384]{2,1,0:T(8,128)(2,1)} %shard_map.406), channel_id=1, source_target_pairs={{0,2},{1,3},{2,0},{3,1},{4,6},{5,7},{6,4},{7,5},{8,10},{9,11},{10,... | collective-permute-start | bytes 3538952 | tf_op jit(solution)/shard_map/ppermute | solution.py:621
  256.6 77.3 %collective-permute-start.6 = (bf16[2,768,384]{2,1,0:T(8,128)(2,1)}, bf16[2,768,384]{2,1,0:T(8,128)(2,1)}, u32[]{:S(2)}, u32[]{:S(2)}) collective-permute-start(bf16[2,768,384]{2,1,0:T(8,128)(2,1)} %shard_map.407), channel_id=1, source_target_pairs={{0,3},{1,2},{2,1},{3,0},{4,7},{5,6},{6,5},{7,4},{8,11},{9,10},{10,... | collective-permute-start | bytes 3538952 | tf_op jit(solution)/shard_map/ppermute | solution.py:621
  258.2 64.8 %collective-permute-start.7 = (bf16[384,768]{1,0:T(8,128)(2,1)}, bf16[384,768]{1,0:T(8,128)(2,1)S(1)}, u32[]{:S(2)}, u32[]{:S(2)}) collective-permute-start(bf16[384,768]{1,0:T(8,128)(2,1)} %shard_map.408), channel_id=1, source_target_pairs={{0,1},{1,0},{2,3},{3,2},{4,5},{5,4},{6,7},{7,6},{8,9},{9,8},{10,11... | collective-permute-start | bytes 1769480 | tf_op jit(solution)/shard_map/ppermute | solution.py:621
  258.8 75.1 %collective-permute-start.9 = (bf16[384,768]{1,0:T(8,128)(2,1)}, bf16[384,768]{1,0:T(8,128)(2,1)S(1)}, u32[]{:S(2)}, u32[]{:S(2)}) collective-permute-start(bf16[384,768]{1,0:T(8,128)(2,1)} %shard_map.410), channel_id=1, source_target_pairs={{0,3},{1,2},{2,1},{3,0},{4,7},{5,6},{6,5},{7,4},{8,11},{9,10},{10,... | collective-permute-start | bytes 1769480 | tf_op jit(solution)/shard_map/ppermute | solution.py:621
  259.6 76.5 %copy-start.21 = (s32[2]{0:T(128)}, s32[2]{0:T(128)S(1)}, u32[]{:S(2)}) copy-start(s32[2]{0:T(128)S(1)} %pad_add_fusion.1.place_ref) | copy-start | bytes 28
  342.4 4.3 collective-permute-start.11
  360.4 52.6 %all-to-all-start.4 = ((bf16[8,320,768]{2,1,0:T(8,128)(2,1)}), bf16[8,320,768]{2,1,0:T(8,128)(2,1)}, u32[]{:S(2)}, u32[]{:S(2)}) async-start(bf16[8,320,768]{2,1,0:T(8,128)(2,1)} %shard_map.422.refs_1_), calls=%async_computation.5 | async-start | bytes 7864320 | tf_op jit(solution)/shard_map/all_to_all | solution.py:81
  365.1 3.5 collective-permute-start.10
  413.0 53.6 %all-to-all-start.5 = ((bf16[8,320,768]{2,1,0:T(8,128)(2,1)}), bf16[8,320,768]{2,1,0:T(8,128)(2,1)}, u32[]{:S(2)}, u32[]{:S(2)}) async-start(bf16[8,320,768]{2,1,0:T(8,128)(2,1)} %shard_map.425), calls=%async_computation.6 | async-start | bytes 7864320 | tf_op jit(solution)/shard_map/all_to_all | solution.py:81
  466.6 54.2 %all-to-all-start.6 = ((bf16[8,1,320,768]{3,2,1,0:T(8,128)(2,1)}), bf16[8,1,320,768]{3,2,1,0:T(8,128)(2,1)}, u32[]{:S(2)}, u32[]{:S(2)}) async-start(bf16[8,1,320,768]{3,2,1,0:T(8,128)(2,1)} %bitcast.302), calls=%async_computation.7 | async-start | bytes 7864320 | tf_op jit(solution)/shard_map/all_to_all | solution.py:81
  520.8 76.3 %all-to-all-start.7 = ((bf16[8,1,320,768]{3,2,1,0:T(8,128)(2,1)}), bf16[8,1,320,768]{3,2,1,0:T(8,128)(2,1)}, u32[]{:S(2)}, u32[]{:S(2)}) async-start(bf16[8,1,320,768]{3,2,1,0:T(8,128)(2,1)} %bitcast.303), calls=%async_computation.8 | async-start | bytes 7864320 | tf_op jit(solution)/shard_map/all_to_all | solution.py:81
  549.4 5.9 collective-permute-start.17
  597.2 126.3 %all-to-all-start.8 = ((bf16[8,2,320,768]{3,2,1,0:T(8,128)(2,1)}), bf16[8,2,320,768]{3,2,1,0:T(8,128)(2,1)}, u32[]{:S(2)}, u32[]{:S(2)}) async-start(bf16[8,2,320,768]{3,2,1,0:T(8,128)(2,1)} %bitcast.290), calls=%async_computation.9 | async-start | bytes 15728640 | tf_op jit(solution)/shard_map/all_to_all | solution.py:81
  602.4 81.9 %all-gather.21.cloned.1.call-start = ((), (), s32[]{:S(2)}) async-start(), calls=%async_computation.21 | async-start | bytes 4718592 | tf_op jit(solution)/shard_map/all_gather | solution.py:482
  603.0 156.9 %reduce-scatter.5.cloned.1.call-start = ((), (), s32[]{:S(2)}) async-start(), calls=%async_computation.16 | async-start | bytes 4718592 | tf_op jit(solution)/shard_map/reduce_scatter | solution.py:687
  609.9 74.4 %collective-permute-start.18 = (f32[1024,768]{1,0:T(8,128)S(1)}, f32[1024,768]{1,0:T(8,128)}, u32[]{:S(2)}, u32[]{:S(2)}) collective-permute-start(f32[1024,768]{1,0:T(8,128)S(1)} %fusion.39.refs_1_), channel_id=1, source_target_pairs={{0,2},{2,0},{1,3},{3,1},{4,6},{6,4},{5,7},{7,5},{8,10},{10,8},{9,1... | collective-permute-start | bytes 9437192 | tf_op jit(solution)/shard_map/ppermute | solution.py:557
  611.6 72.8 %copy-start.73 = (f32[768]{0:T(1024)S(1)}, f32[768]{0:T(1024)}, u32[]{:S(2)}) copy-start(f32[768]{0:T(1024)} %copy-done.72) | copy-start | bytes 9220
  611.6 72.8 %copy-start.75 = (f32[1024]{0:T(1024)S(1)}, f32[1024]{0:T(1024)}, u32[]{:S(2)}) copy-start(f32[1024]{0:T(1024)} %copy-done.74) | copy-start | bytes 12292
  684.4 20.6 %copy-start.29 = (f32[1024,768]{1,0:T(8,128)S(1)}, f32[1024,768]{1,0:T(8,128)}, u32[]{:S(2)}) copy-start(f32[1024,768]{1,0:T(8,128)} %copy-done.28) | copy-start | bytes 9437188
  717.1 130.5 %all-gather.23.cloned.1.call-start = ((), (), s32[]{:S(2)}) async-start(), calls=%async_computation.22 | async-start | bytes 6291456 | tf_op jit(solution)/shard_map/all_gather | solution.py:697
  730.5 5.9 collective-permute-start.19
  790.6 14.0 %collective-permute-start.20 = (f32[1024,768]{1,0:T(8,128)}, f32[1024,768]{1,0:T(8,128)}, u32[]{:S(2)}, u32[]{:S(2)}) collective-permute-start(f32[1024,768]{1,0:T(8,128)} %fusion.42.refs_1_), channel_id=1, source_target_pairs={{0,2},{2,0},{1,3},{3,1},{4,6},{6,4},{5,7},{7,5},{8,10},{10,8},{9,1... | collective-permute-start | bytes 9437192 | tf_op jit(solution)/shard_map/ppermute | solution.py:557
  793.9 75.9 %all-to-all-start.9 = ((bf16[2,1024,768]{2,1,0:T(8,128)(2,1)}), bf16[2,1024,768]{2,1,0:T(8,128)(2,1)S(1)}, u32[]{:S(2)}, u32[]{:S(2)}) async-start(bf16[2,1024,768]{2,1,0:T(8,128)(2,1)} %broadcast_in_dim.74), calls=%async_computation.11 | async-start | bytes 6291456 | tf_op jit(solution)/shard_map/all_to_all | solution.py:81
  804.1 49.4 %collective-permute-start.22 = (f32[768,768]{1,0:T(8,128)}, f32[768,768]{1,0:T(8,128)}, u32[]{:S(2)}, u32[]{:S(2)}) collective-permute-start(f32[768,768]{1,0:T(8,128)} %fusion.46.refs_1_), channel_id=1, source_target_pairs={{0,2},{2,0},{1,3},{3,1},{4,6},{6,4},{5,7},{7,5},{8,10},{10,8},{9,1... | collective-permute-start | bytes 7077896 | tf_op jit(solution)/shard_map/ppermute | solution.py:714
  853.3 51.6 %collective-permute-start.21 = (f32[768,1024]{1,0:T(8,128)}, f32[768,1024]{1,0:T(8,128)}, u32[]{:S(2)}, u32[]{:S(2)}) collective-permute-start(f32[768,1024]{1,0:T(8,128)} %fusion.26.refs_1_), channel_id=1, source_target_pairs={{0,2},{2,0},{1,3},{3,1},{4,6},{6,4},{5,7},{7,5},{8,10},{10,8},{9,1... | collective-permute-start | bytes 9437192 | tf_op jit(solution)/shard_map/ppermute | solution.py:714
  871.5 48.5 %all-to-all-start.12 = ((bf16[4,384,768]{2,1,0:T(8,128)(2,1)}), bf16[4,384,768]{2,1,0:T(8,128)(2,1)}, u32[]{:S(2)}, u32[]{:S(2)}) async-start(bf16[4,384,768]{2,1,0:T(8,128)(2,1)} %bitcast.310), calls=%async_computation.14 | async-start | bytes 4718592 | tf_op jit(solution)/shard_map/all_to_all | solution.py:81
  885.6 19.1 %collective-permute-start.23 = (f32[2,6]{1,0:T(2,128)S(1)}, f32[2,6]{1,0:T(2,128)S(1)}, u32[]{:S(2)}, u32[]{:S(2)}) collective-permute-start(f32[2,6]{1,0:T(2,128)S(1)} %copy-done.87), channel_id=1, source_target_pairs={{0,1},{1,0},{2,3},{3,2},{4,5},{5,4},{6,7},{7,6},{8,9},{9,8},{10,11... | collective-permute-start | bytes 152 | tf_op jit(solution)/shard_map/ppermute | solution.py:66
  915.0 22.5 %collective-permute-start.24 = (f32[3,768]{1,0:T(4,128)S(1)}, f32[3,768]{1,0:T(4,128)S(1)}, u32[]{:S(2)}, u32[]{:S(2)}) collective-permute-start(f32[3,768]{1,0:T(4,128)S(1)} %pad_maximum_fusion.2), channel_id=1, source_target_pairs={{0,2},{2,0},{1,3},{3,1},{4,6},{6,4},{5,7},{7,5},{8,10},{10,8},{9,1... | collective-permute-start | bytes 27656 | tf_op jit(solution)/shard_map/ppermute | solution.py:66
  920.0 59.0 %all-to-all-start.10 = ((bf16[4,2,768,384]{3,1,2,0:T(2,128)(2,1)}), bf16[4,2,768,384]{3,1,2,0:T(2,128)(2,1)}, u32[]{:S(2)}, u32[]{:S(2)}) async-start(bf16[4,2,768,384]{3,1,2,0:T(2,128)(2,1)} %bitcast.299), calls=%async_computation.12 | async-start | bytes 9437184 | tf_op jit(solution)/shard_map/all_to_all | solution.py:81
  937.5 4.7 collective-permute-start.25
  942.3 6.1 collective-permute-start.26
  948.4 8.9 collective-permute-start.27
  979.0 65.9 %all-to-all-start.11 = ((bf16[8,96,1792]{2,1,0:T(8,128)(2,1)}), bf16[8,96,1792]{2,1,0:T(8,128)(2,1)S(1)}, u32[]{:S(2)}, u32[]{:S(2)}) async-start(bf16[8,96,1792]{2,1,0:T(8,128)(2,1)} %bitcast.104), calls=%async_computation.13 | async-start | bytes 5505024 | tf_op jit(solution)/shard_map/all_to_all | solution.py:81
  1016.5 28.9 %copy-start.54 = (f32[96,1,1024]{2,1,0:T(1,128)S(1)}, f32[96,1,1024]{2,1,0:T(1,128)}, u32[]{:S(2)}) copy-start(f32[96,1,1024]{2,1,0:T(1,128)} %param.40) | copy-start | bytes 1179652
  1016.5 28.9 %copy-start.55 = (f32[96,1,1024]{2,1,0:T(1,128)S(1)}, f32[96,1,1024]{2,1,0:T(1,128)}, u32[]{:S(2)}) copy-start(f32[96,1,1024]{2,1,0:T(1,128)} %param.41) | copy-start | bytes 1179652
  (74 other events, 373.6 us)
Sparse Core Ops, SparseCore 0:
  9.8 14.8 all-gather.12
  34.7 88.3 reduce-scatter.2
  145.5 50.0 all-gather.14
  197.6 10.6 all-gather.16
  258.1 80.2 all-gather.18
  604.6 79.7 all-gather.20
  717.3 42.5 reduce-scatter.4
  790.7 56.8 all-gather.22

commit v3 on v2

--- a/solution.py
+++ b/solution.py
@@ -30,6 +30,7 @@
 QUERIES = 256
 MIB = 1 << 20
 NO_COST = pl.CostEstimate(flops=0, bytes_accessed=0, transcendentals=0)
+LONG = pl.CostEstimate(flops=10**11, bytes_accessed=0, transcendentals=0)
 
 
 def dot(left, right, left_dim=1, right_dim=0):
@@ -218,7 +219,7 @@
         out_ref[0, c] = picked.astype(jnp.bfloat16)
 
 
-def pick_slots(ranks, slots, blocks):
+def pick_slots(ranks, slots, blocks, cost=NO_COST):
     units, count = ranks.shape
     cols = len(blocks[0])
     flat = [block for row in blocks for block in row]
@@ -231,7 +232,7 @@
         out_specs=pl.BlockSpec((1, cols, slots, width), lambda u: (u, 0, 0, 0)),
         out_shape=jax.ShapeDtypeStruct((units, cols, slots, width), jnp.bfloat16),
         compiler_params=pltpu.CompilerParams(vmem_limit_bytes=56 * MIB),
-        cost_estimate=NO_COST,
+        cost_estimate=cost,
     )(ranks[:, None, :], *flat)
 
 
@@ -419,7 +420,7 @@
             jax.ShapeDtypeStruct((row_n, col_n, part, width), jnp.bfloat16),
         ],
         compiler_params=pltpu.CompilerParams(vmem_limit_bytes=58 * MIB),
-        cost_estimate=NO_COST,
+        cost_estimate=LONG,
     )(place, *[array for source in sources for array in source])
 
 
@@ -545,7 +546,11 @@
         chosen = unit_ranks[number][:, :, None, k * tokens_row : (k + 1) * tokens_row]
         return (chosen == jnp.arange(slots, dtype=jnp.int32)[None, None, :, None]).astype(low)
 
-    def token_sums(number, values, half=0):
+    def to_row(part, k, pieces):
+        pairs = [(i, (i + k) % row_n) for i in range(row_n)]
+        return jnp.concatenate([lax.ppermute(piece, "row", pairs) for piece in jnp.split(part, pieces)])
+
+    def token_sums(number, values, half=0, pieces=1):
         def partial(k):
             own = values.reshape(dl_n, col_n, -1, slots, width)[:, :, half]
             return jnp.einsum("dcst,dcsf->tf", hot(number, k), own, preferred_element_type=jnp.float32)
@@ -554,7 +559,7 @@
         for k in range(1, row_n):
             part = partial(k)
             values = after(values, part)
-            part = lax.ppermute(part, "row", [(i, (i + k) % row_n) for i in range(row_n)])
+            part = to_row(part, k, pieces)
             total = part if total is None else total + part
         return partial(0) + total, values
 
@@ -589,8 +594,8 @@
     grad_low = grad_rows.astype(low)
     far_low = to_owners(jnp.broadcast_to(grad_low, (dh_n,) + grad_low.shape), "dh")
 
-    def dispatch_wide(number, blocks):
-        return pick_slots(here_ranks[number], slots, blocks)
+    def dispatch_wide(number, blocks, cost=NO_COST):
+        return pick_slots(here_ranks[number], slots, blocks, cost)
 
     def by_row(blocks):
         parts = [ring(block, "row") for block in blocks]
@@ -608,8 +613,8 @@
     far_low = lax.dynamic_index_in_dim(far_low, dh_n - 1 - dh_i, 0, False)
     far_wide = ring(far_low, "col")
     heads = lax.all_gather(mixed, "col", axis=0)
-    heads = after(heads, *in_pieces, *down_pieces).reshape(seqs_row, KVH, LEN, GROUP * HD)
-    out_row = lax.all_gather(after(w_out[0], packed), "row", axis=0)
+    out_row = jnp.roll(jnp.stack(ring(w_out[0], "row")), row_i, axis=0)
+    heads = after(heads, out_row, *in_pieces, *down_pieces).reshape(seqs_row, KVH, LEN, GROUP * HD)
     attn = jnp.einsum("sgth,ghf->stf", heads, out_row, preferred_element_type=jnp.float32)
     hidden = inputs + attn.reshape(tokens_row, width)
 
@@ -624,7 +629,7 @@
         down_pieces[k] = spread(down_pieces[k], piece_pairs[k])
         in_pieces[k] = spread(in_pieces[k], piece_pairs[k])
     far_wide[-1] = after(far_wide[-1], down_pieces[col_n])
-    far_picked = dispatch_wide(1, by_row(far_wide))
+    far_picked = dispatch_wide(1, by_row(far_wide), LONG)
     far_grads = to_owners(after(far_picked, my_gate), "dl")
     place = jnp.stack([row_i, col_i]).astype(jnp.int32)
     weights_in, weights_down = join_weights(in_pieces, down_pieces, place, row_n, col_n)
@@ -660,10 +665,10 @@
         row_n,
     )
     own_back = after(own_back, in_grad)
-    far_sums = from_far(far_sums)
+    far_sums = lax.ppermute(far_sums, "dh", far_pairs())
     slot_out = after(slot_out, own_back)
     slot_out = to_owners(slot_out.reshape((dl_n * col_n,) + slot_out.shape[2:]), ("dl", "col"))
-    own_sums, _ = token_sums(0, own_back)
+    own_sums, _ = token_sums(0, own_back, pieces=4)
     grad_normed_two = own_sums + far_sums.astype(jnp.float32)
 
     def block_grads(grads):
@@ -691,8 +696,9 @@
     )
     far_out_sums, slot_out = token_sums(1, after(slot_out, terms), 1)
     far_out_sums = far_out_sums.astype(low)
+    far_out_sums = jnp.broadcast_to(far_out_sums, (dh_n,) + far_out_sums.shape)
     grad_heads = after(grad_heads, far_out_sums)
-    far_out_sums = to_owners(jnp.broadcast_to(far_out_sums, (dh_n,) + far_out_sums.shape), "dh")
+    far_out_sums = to_owners(far_out_sums, "dh")
     grad_packed = attend_backward(packed, ids, log_total, grad_heads)
     packed_all = lax.all_gather(grad_packed, "col", axis=0).reshape(seqs_row, KVH, LEN, -1)
 
@@ -737,8 +743,6 @@
     grad_input_norm, grad_gain_one = norm_backward(inputs, factor_one, gains[0], grad_normed_one)
     input_grad = grad_hidden + grad_input_norm
 
-    full_top = butterfly(after(full_top, packed_all), jnp.maximum, ("col",))
-
     tops_row = jnp.pad(full_top.reshape(1, -1), ((0, 0), (0, width - KVH * GROUP)))
     small = jnp.concatenate([grad_gain_one[None], grad_gain_two[None], tops_row])
 
@@ -747,6 +751,7 @@
 
     small = butterfly(small, combine, ("row", "dh", "dl"))
     grad_gains, head_top = small[:2], small[2, : KVH * GROUP].reshape(KVH, GROUP)
+    head_top = butterfly(head_top, jnp.maximum, ("col",))
 
     factors = TAU_CLIP / jnp.maximum(head_top, TAU_CLIP)
     local_factors = lax.dynamic_slice_in_dim(factors, row_i, 1, 0)

time: 1070 us -> 1080 us (level)
  waiting for transfers between devices: 450 us -> 430 us
  blocking collectives: 28.7 us -> 43.8 us
  other arithmetic: 86.3 us -> 99.3 us
    ppermute x4 -> x8, waiting for transfers between devices: 8.41 us -> 99.4 us  [the longest x1 95.4 us: on_device(): far_sums = lax.ppermute(far_sums, 'dh', far_pairs())]
    all_gather x2 -> x1, waiting for transfers between devices: 72.8 us -> 0.01 us  [from_far(): both = lax.all_gather(values, 'dh', axis=0)]
    reduce_scatter x1, waiting for transfers between devices: 63.7 us -> 4.52 us  [on_device(): packed = lax.psum_scatter(terms, 'col', scatter_dimension=0, tiled=True)]
    ppermute x9 -> x10, waiting for transfers between devices: 7.15 us -> 47.8 us  [ring(): lax.ppermute(values, axis, [(i, (i - k) % count) for i in range(count)])]
    all_to_all x13, waiting for transfers between devices: 143 us -> 107 us  [to_owners(): return lax.all_to_all(values, axes, split_axis=0, concat_axis=0, tiled=True)]
    psum x4, blocking collectives: 28.7 us -> 43.8 us  [col_total(): return lax.psum(jnp.sum(values, axis=1), 'col')]
    all_gather x1 -> x0, waiting for transfers between devices: 12.8 us -> none  [on_device(): out_row = lax.all_gather(after(w_out[0], packed), 'row', axis=0)]
    unnamed x191 -> x200, local copies, waits for them, and re-layouts: 43.2 us -> 47.8 us
  transfers between devices with their start and end apart: 49 -> 52, of which waited for: 23 -> 20; matrix products, arithmetic and copies ran while one was open for 22% -> 22% of each run, Pallas kernels for 15% -> 14%
where the time goes in v3:
time: 1080 us
  waiting for transfers between devices  430 us (40%)
  Pallas kernels  176 us (16%)
  matrix products  110 us (10%)
  local copies, waits for them, and re-layouts  106 us (10%)
  other arithmetic  99.3 us (9%)
  starting transfers between devices  94.7 us (9%)
  blocking collectives  43.8 us (4%)
  between operations  16.9 us (2%)
    all_to_all x13, waiting for transfers between devices, to_owners(): return lax.all_to_all(values, axes, split_axis=0, concat_axis=0, tiled=True)  107 us
    ppermute x1, waiting for transfers between devices, on_device(): far_sums = lax.ppermute(far_sums, 'dh', far_pairs())  95.4 us
    ppermute x6, waiting for transfers between devices, spread(): return lax.ppermute(after(piece, normed_two), ('row', 'col'), pairs)  76 us
    all_to_all x13, starting transfers between devices, to_owners(): return lax.all_to_all(values, axes, split_axis=0, concat_axis=0, tiled=True)  72.5 us
    dot_general x8, matrix products, partial(): jnp.einsum('dcst,dcsf->tf', hot(number, k), own, preferred_element_type=j...  63.5 us
    pallas_call x4, Pallas kernels, pick_slots(): pl.pallas_call(pick_kernel, grid=(units,), in_specs=[pl.BlockSpec((1, 1,...  50.2 us
    ppermute x10, waiting for transfers between devices, ring(): lax.ppermute(values, axis, [(i, (i - k) % count) for i in range(count)])  47.8 us
    unnamed x200, local copies, waits for them, and re-layouts  47.8 us
  transfers between devices with their start and end apart: 52, of which 20 were waited for; matrix products, arithmetic and copies ran while one was open for 22% of the time, Pallas kernels for 14%

profile of v3, /device:TPU:0, one launch (start us, length us, event | category | flops | bytes accessed | tf_op | source)
XLA Modules:
  0.0 1077.0 jit_solution(2374861353530118970)
XLA Ops:
  16.6 5.1 psum.28
  25.2 7.8 convolution_convert_fusion
  39.2 5.2 all-to-all-start
  72.3 43.4 %collective-permute-done.15.refs_0_ = bf16[1024,768]{1,0:T(8,128)(2,1)S(1)} collective-permute-done((bf16[1024,768]{1,0:T(8,128)(2,1)}, bf16[1024,768]{1,0:T(8,128)(2,1)S(1)}, u32[]{:S(2)}, u32[]{:S(2)}) %collective-permute-start.15) | collective-permute-done | bytes 1572896 | tf_op jit(solution)/shard_map/ppermute | solution.py:490
  117.1 4.5 reduce-scatter.3.cloned.1.call-done.query_ref.key_ref.value_ref
  123.2 19.5 %shard_map.400 = (bf16[1024,768]{1,0:T(8,128)(2,1)}, f32[6,1,1024]{2,1,0:T(1,128)S(1)}, f32[6,1,1024]{2,1,0:T(1,128)S(1)}) custom-call(bf16[1024,1024]{1,0:T(8,128)(2,1)S(1)} %copy-done.1, bf16[1024,1024]{1,0:T(8,128)(2,1)S(1)} %copy-done.1, bf16[1024,1024]{1,0:T(8,128)(2,1)S(1)} %copy-done.1, s32[1,1024]{1,0:T(1,128)S(1)} %fusion.87.id_row_ref, ...), custom_call_target="tpu_custom_call" | custom-call | tf_op jit(solution)/shard_map/pallas_call | solution.py:132
  145.9 13.1 %shard_map.417.refs_0_ = bf16[4,2,320,768]{3,2,1,0:T(8,128)(2,1)} custom-call(s32[4,1,2048]{2,1,0:T(1,128)} %fusion.119.ranks_ref, bf16[1024,768]{1,0:T(8,128)(2,1)} %shard_map.415.refs_0_, bf16[1024,768]{1,0:T(8,128)(2,1)} %shard_map.416.refs_1_, bf16[1024,768]{1,0:T(8,128)(2,1)} %collective-permute-done.16.refs_2_, bf16[1024,768]{1,0:T(8,128)(2,1)} %copy-done.48), custom_call_target="tpu_custom_call" | custom-call | tf_op jit(solution)/shard_map/pallas_call | solution.py:228
  159.0 4.8 all-to-all-start.1
  164.0 4.9 constant_dynamic-slice_fusion.2
  179.0 5.0 fusion.27.refs_1_
  184.0 12.0 %all-gather.11.cloned.1.call-done = bf16[2048,768]{1,0:T(8,128)(2,1)} async-done(((bf16[1024,768]{1,0:T(8,128)(2,1)}), bf16[2048,768]{1,0:T(8,128)(2,1)}) %all-gather.11.cloned.1.call-update) | async-done | bytes 3145744 | tf_op jit(solution)/shard_map/all_gather | solution.py:615
  197.8 7.0 multiply_reduce_fusion.4
  204.8 17.8 %psum.29 = f32[1024]{0:T(1024)S(1)} all-reduce(f32[1024]{0:T(1024)S(1)} %get-tuple-element.252), channel_id=1, replica_groups=mesh['dh'=2,'dl'=4,'row'=2,'col'=2] {'col'}, use_global_device_ids=true, to_apply=%region_6.8 | all-reduce | flops 1024 | bytes 8192 | tf_op jit(solution)/shard_map/psum | solution.py:58
  234.9 12.7 %shard_map.414.refs_0_ = bf16[4,2,320,768]{3,2,1,0:T(8,128)(2,1)} custom-call(s32[4,1,2048]{2,1,0:T(1,128)} %fusion.120.ranks_ref, bf16[1024,768]{1,0:T(8,128)(2,1)} %dynamic-slice_bitcast_fusion.1.refs_0_, bf16[1024,768]{1,0:T(8,128)(2,1)} %shard_map.413.refs_1_, bf16[1024,768]{1,0:T(8,128)(2,1)} %copy-done.93, ...), custom_call_target="tpu_custom_call" | custom-call | flops 99999997952 | tf_op jit(solution)/shard_map/pallas_call | solution.py:228
  249.1 4.8 all-to-all-start.3
  258.2 63.4 %collective-permute-done.8.refs_5_ = bf16[384,768]{1,0:T(8,128)(2,1)S(1)} collective-permute-done((bf16[384,768]{1,0:T(8,128)(2,1)}, bf16[384,768]{1,0:T(8,128)(2,1)S(1)}, u32[]{:S(2)}, u32[]{:S(2)}) %collective-permute-start.8) | collective-permute-done | bytes 589856 | tf_op jit(solution)/shard_map/ppermute | solution.py:626
  321.5 10.9 %collective-permute-done.10.refs_7_ = bf16[384,768]{1,0:T(8,128)(2,1)S(1)} collective-permute-done((bf16[384,768]{1,0:T(8,128)(2,1)}, bf16[384,768]{1,0:T(8,128)(2,1)S(1)}, u32[]{:S(2)}, u32[]{:S(2)}) %collective-permute-start.10) | collective-permute-done | bytes 589856 | tf_op jit(solution)/shard_map/ppermute | solution.py:626
  346.4 12.2 %shard_map.412 = bf16[8,1,320,768]{3,2,1,0:T(8,128)(2,1)} custom-call(s32[8,1,2048]{2,1,0:T(1,128)} %broadcast_in_dim_reshape.7.ranks_ref, bf16[1024,768]{1,0:T(8,128)(2,1)} %shard_map.411.refs_0_, bf16[1024,768]{1,0:T(8,128)(2,1)} %copy-done.49), custom_call_target="tpu_custom_call" | custom-call | tf_op jit(solution)/shard_map/pallas_call | solution.py:228
  358.7 4.7 all-to-all-start.4
  368.0 12.2 %shard_map.423 = bf16[8,1,320,768]{3,2,1,0:T(8,128)(2,1)} custom-call(s32[8,1,2048]{2,1,0:T(1,128)} %broadcast_in_dim_reshape.6.ranks_ref, bf16[1024,768]{1,0:T(8,128)(2,1)} %shard_map.403.refs_1_.refs_0_, bf16[1024,768]{1,0:T(8,128)(2,1)} %shard_map.422.refs_1_), custom_call_target="tpu_custom_call" | custom-call | tf_op jit(solution)/shard_map/pallas_call | solution.py:228
  380.3 31.0 %all-to-all-done.4 = bf16[8,320,768]{2,1,0:T(8,128)(2,1)} async-done(((bf16[8,320,768]{2,1,0:T(8,128)(2,1)}), bf16[8,320,768]{2,1,0:T(8,128)(2,1)}, u32[]{:S(2)}, u32[]{:S(2)}) %all-to-all-start.4) | async-done | bytes 3932192 | tf_op jit(solution)/shard_map/all_to_all | solution.py:82
  411.3 7.0 all-to-all-start.5
  419.5 21.4 %shard_map.425 = (bf16[4,2,320,768]{3,2,1,0:T(8,128)(2,1)}, bf16[4,320,768]{2,1,0:T(8,128)(2,1)}, bf16[4,320,1536]{2,1,0:T(8,128)(2,1)}) custom-call(s32[2]{0:T(128)} %copy-done.21, bf16[4,2,320,768]{3,2,1,0:T(8,128)(2,1)} %bitcast.46.refs_1_.rows_ref.refs_4_, bf16[4,2,320,768]{3,2,1,0:T(8,128)(2,1)} %all-to-all-done.3.refs_1_.grads_ref.refs_5_, ...), custom_call_target="tpu_custom_call" | custom-call | tf_op jit(solution)/shard_map/pallas_call | solution.py:260
  440.9 24.1 %all-to-all-done.5 = bf16[8,320,768]{2,1,0:T(8,128)(2,1)} async-done(((bf16[8,320,768]{2,1,0:T(8,128)(2,1)}), bf16[8,320,768]{2,1,0:T(8,128)(2,1)}, u32[]{:S(2)}, u32[]{:S(2)}) %all-to-all-start.5) | async-done | bytes 3932192 | tf_op jit(solution)/shard_map/all_to_all | solution.py:82
  465.0 8.5 all-to-all-start.6
  474.7 21.6 %shard_map.427 = (bf16[4,2,320,768]{3,2,1,0:T(8,128)(2,1)}, bf16[4,320,768]{2,1,0:T(8,128)(2,1)}, bf16[4,320,1536]{2,1,0:T(8,128)(2,1)}) custom-call(s32[2]{0:T(128)} %copy-done.21, bf16[4,2,320,768]{3,2,1,0:T(8,128)(2,1)} %shard_map.426.rows_ref.refs_0_, bf16[4,2,320,768]{3,2,1,0:T(8,128)(2,1)} %all-to-all-done.1.refs_1_.grads_ref, ...), custom_call_target="tpu_custom_call" | custom-call | tf_op jit(solution)/shard_map/pallas_call | solution.py:260
  497.8 7.4 shard_map.428.refs_1_.refs_0_
  508.5 11.1 %all-to-all-done.6.refs_1_.refs_0_ = bf16[8,1,320,768]{3,2,1,0:T(8,128)(2,1)} async-done(((bf16[8,1,320,768]{3,2,1,0:T(8,128)(2,1)}), bf16[8,1,320,768]{3,2,1,0:T(8,128)(2,1)}, u32[]{:S(2)}, u32[]{:S(2)}) %all-to-all-start.6) | async-done | bytes 3932192 | tf_op jit(solution)/shard_map/all_to_all | solution.py:82
  519.6 6.9 fusion.39.refs_1_
  528.1 7.7 all-to-all-start.7
  535.9 8.4 fusion.24.refs_1_
  544.3 33.4 %shard_map.433 = (bf16[2,2,2,768,384]{4,3,2,1,0:T(8,128)(2,1)}, bf16[2,2,384,768]{3,2,1,0:T(8,128)(2,1)}) custom-call(s32[2]{0:T(128)} %copy-done.21, bf16[4,2,320,768]{3,2,1,0:T(8,128)(2,1)} %shard_map.426.rows_ref.refs_0_, bf16[4,2,320,768]{3,2,1,0:T(8,128)(2,1)} %all-to-all-done.1.refs_1_.grads_ref, bf16[4,320,768]{2,1,0:T(8,128)(2,1)} %shard_map.432.refs_2_, ...), custom_call_target="tpu_custom_call" | custom-call | flops 99999997952 | tf_op jit(solution)/shard_map/pallas_call | solution.py:403
  577.7 4.2 all-to-all-done.7.refs_0_
  581.9 8.3 all-to-all-start.8
  592.6 8.5 fusion.43.refs_1_
  604.4 7.3 fusion.7
  611.7 95.4 %collective-permute-done.23 = bf16[1024,768]{1,0:T(8,128)(2,1)} collective-permute-done((bf16[1024,768]{1,0:T(8,128)(2,1)}, bf16[1024,768]{1,0:T(8,128)(2,1)}, u32[]{:S(2)}, u32[]{:S(2)}) %collective-permute-start.23) | collective-permute-done | bytes 1572896 | tf_op jit(solution)/shard_map/ppermute | solution.py:668
  707.2 4.5 multiply_reduce_fusion
  711.6 16.0 %psum.30 = f32[1024]{0:T(1024)S(1)} all-reduce(f32[1024]{0:T(1024)S(1)} %get-tuple-element.207), channel_id=1, replica_groups=mesh['dh'=2,'dl'=4,'row'=2,'col'=2] {'col'}, use_global_device_ids=true, to_apply=%region_14.17 | all-reduce | flops 1024 | bytes 8192 | tf_op jit(solution)/shard_map/psum | solution.py:58
  727.7 4.8 convert_bitcast_fusion.1
  740.6 6.9 fusion.42.refs_1_
  753.4 7.9 fusion.23
  761.3 24.7 %reduce-scatter.5.cloned.1.call-done.refs_0_ = bf16[1024,768]{1,0:T(8,128)(2,1)} async-done(((bf16[2048,768]{1,0:T(8,128)(2,1)}), bf16[1024,768]{1,0:T(8,128)(2,1)}) %reduce-scatter.5.cloned.1.call-update) | async-done | bytes 1572880 | tf_op jit(solution)/shard_map/reduce_scatter | solution.py:692
  790.9 20.7 %shard_map.440.refs_1_ = bf16[1024,1024]{1,0:T(8,128)(2,1)} custom-call(bf16[1024,1024]{1,0:T(8,128)(2,1)S(1)} %copy-done.2, bf16[1024,1024]{1,0:T(8,128)(2,1)S(1)} %copy-done.2, bf16[1024,1024]{1,0:T(8,128)(2,1)S(1)} %copy-done.2, bf16[1024,768]{1,0:T(8,128)(2,1)S(1)} %copy-done.6, f32[6,1,1024]{2,1,0:T(1,128)S(1)} %copy-done.20, s32[1,1024]{1,0:T(1,128)S(1)} %copy-done.16, ...), custom_call_target="tpu_custom_call" | custom-call | tf_op jit(solution)/shard_map/pallas_call | solution.py:188
  811.7 8.5 fusion.46.refs_1_
  820.3 4.1 all-to-all-start.9
  824.4 5.4 fusion.50.refs_1_
  830.4 9.1 bitcast_add_fusion.refs_1_
  839.5 37.8 %all-gather.15.cloned.1.call-done = bf16[2048,1024]{1,0:T(8,128)(2,1)} async-done(((bf16[1024,1024]{1,0:T(8,128)(2,1)}), bf16[2048,1024]{1,0:T(8,128)(2,1)}) %all-gather.15.cloned.1.call-update) | async-done | bytes 4194320 | tf_op jit(solution)/shard_map/all_gather | solution.py:703
  877.3 5.6 fusion.30.refs_1_
  883.2 5.1 add_convert_fusion.1
  888.3 7.7 all-to-all-done.9.refs_0_.refs_1_
  897.7 4.7 all-to-all-start.12
  902.4 9.4 copy.370
  913.7 7.5 fusion.34.refs_0_
  921.2 4.9 add_convert_fusion.refs_1_
  931.2 4.9 psum.31
  936.1 5.2 all-to-all-start.10
  941.3 12.2 %fusion.93 = (bf16[4,384,768]{2,1,0:T(8,128)(2,1)}, f32[4,384,768]{2,1,0:T(8,128)}, f32[4,384,768]{2,1,0:T(8,128)}, f32[4,384,768]{2,1,0:T(8,128)}) fusion(f32[4,384,768]{2,1,0:T(8,128)} %param.49, bf16[4,384,768]{2,1,0:T(8,128)(2,1)} %shard_map.453, f32[4,384,768]{2,1,0:T(8,128)} %param.50, f32[4,384,768]{2,1,0:T(8,128)} %param.51), kind=kLoop, calls=%fused_computation.209 | loop fusion | flops 20054016 | bytes 33030144 | tf_op jit(solution)/shard_map/convert_element_type | solution.py:795
  959.9 4.5 convert_add_fusion.4
  966.4 4.9 reshape.264
  976.1 19.0 %collective-permute-done.32 = f32[2,6]{1,0:T(2,128)S(1)} collective-permute-done((f32[2,6]{1,0:T(2,128)S(1)}, f32[2,6]{1,0:T(2,128)S(1)}, u32[]{:S(2)}, u32[]{:S(2)}) %collective-permute-start.32) | collective-permute-done | bytes 80 | tf_op jit(solution)/shard_map/ppermute | solution.py:67
  1000.8 33.8 %fusion.94 = (bf16[4,768,2,384]{3,2,1,0:T(2,128)(2,1)}, f32[4,768,2,384]{3,2,1,0:T(2,128)}, f32[4,768,2,384]{3,2,1,0:T(2,128)}, f32[4,768,2,384]{3,2,1,0:T(2,128)}) fusion(f32[4,768,2,384]{3,2,1,0:T(2,128)} %param.46, bf16[4,768,2,384]{3,2,1,0:T(2,128)(2,1)} %shard_map.451, f32[4,768,2,384]{3,2,1,0:T(2,128)} %param.47, f32[4,768,2,384]{3,2,1,0:T(2,128)} %param.48), kind=kLoop, calls=%fused_computation.210 | loop fusion | flops 40108032 | bytes 66060288 | tf_op jit(solution)/shard_map/convert_element_type | solution.py:791
  1034.7 28.5 %all-to-all-done.11 = bf16[8,96,1792]{2,1,0:T(8,128)(2,1)S(1)} async-done(((bf16[8,96,1792]{2,1,0:T(8,128)(2,1)}), bf16[8,96,1792]{2,1,0:T(8,128)(2,1)S(1)}, u32[]{:S(2)}, u32[]{:S(2)}) %all-to-all-start.11) | async-done | bytes 2752544 | tf_op jit(solution)/shard_map/all_to_all | solution.py:82
  (447 shorter events, 168.6 us)
Async XLA Ops:
  7.2 18.0 %all-gather.9.cloned.1.call-start = ((), (), s32[]{:S(2)}) async-start(), calls=%async_computation.17 | async-start | bytes 4718592 | tf_op jit(solution)/shard_map/all_gather | solution.py:494
  7.9 113.7 %reduce-scatter.3.cloned.1.call-start = ((), (), s32[]{:S(2)}) async-start(), calls=%async_computation.15 | async-start | bytes 6291456 | tf_op jit(solution)/shard_map/reduce_scatter | solution.py:508
  8.0 15.3 %collective-permute-start.2 = (s32[1,1024]{1,0:T(1,128)}, s32[1,1024]{1,0:T(1,128)S(1)}, u32[]{:S(2)}, u32[]{:S(2)}) collective-permute-start(s32[1,1024]{1,0:T(1,128)} %param.32), channel_id=1, source_target_pairs={{0,1},{1,0},{2,3},{3,2},{4,5},{5,4},{6,7},{7,6},{8,9},{9,8},{10,11... | collective-permute-start | bytes 12296 | tf_op jit(solution)/shard_map/ppermute | solution.py:490
  11.0 12.9 %collective-permute-start.1 = (f32[4,2048]{1,0:T(4,128)}, f32[4,2048]{1,0:T(4,128)S(1)}, u32[]{:S(2)}, u32[]{:S(2)}) collective-permute-start(f32[4,2048]{1,0:T(4,128)} %param.31), channel_id=1, source_target_pairs={{0,16},{16,0},{1,17},{17,1},{2,18},{18,2},{3,19},{19,3},{4,20},{20... | collective-permute-start | bytes 98312 | tf_op jit(solution)/shard_map/ppermute | solution.py:497
  13.6 10.3 collective-permute-start
  21.7 200.9 %copy-start.72 = (f32[768]{0:T(1024)}, f32[768]{0:T(1024)S(1)}, u32[]{:S(2)}) copy-start(f32[768]{0:T(1024)S(1)} %get-tuple-element.210) | copy-start | bytes 9220
  39.2 119.8 %all-to-all-start = ((bf16[2,1024,768]{2,1,0:T(8,128)(2,1)}), bf16[2,1024,768]{2,1,0:T(8,128)(2,1)}, u32[]{:S(2)}, u32[]{:S(2)}) async-start(bf16[2,1024,768]{2,1,0:T(8,128)(2,1)} %broadcast_in_dim.64), calls=%async_computation.1 | async-start | bytes 6291456 | tf_op jit(solution)/shard_map/all_to_all | solution.py:82
  44.5 151.5 %all-gather.11.cloned.1.call-start = ((), (), s32[]{:S(2)}) async-start(), calls=%async_computation.18 | async-start | bytes 4718592 | tf_op jit(solution)/shard_map/all_gather | solution.py:615
  44.5 100.2 %collective-permute-start.16 = (bf16[1024,768]{1,0:T(8,128)(2,1)}, bf16[1024,768]{1,0:T(8,128)(2,1)}, u32[]{:S(2)}, u32[]{:S(2)}) collective-permute-start(bf16[1024,768]{1,0:T(8,128)(2,1)} %shard_map.415.refs_0_), channel_id=1, source_target_pairs={{0,2},{2,0},{1,3},{3,1},{4,6},{6,4},{5,7},{7,5},{8,10},{10,8},{9,1... | collective-permute-start | bytes 4718600 | tf_op jit(solution)/shard_map/ppermute | solution.py:490
  44.6 71.0 %collective-permute-start.15 = (bf16[1024,768]{1,0:T(8,128)(2,1)}, bf16[1024,768]{1,0:T(8,128)(2,1)S(1)}, u32[]{:S(2)}, u32[]{:S(2)}) collective-permute-start(bf16[1024,768]{1,0:T(8,128)(2,1)} %shard_map.415.refs_0_), channel_id=1, source_target_pairs={{0,1},{1,0},{2,3},{3,2},{4,5},{5,4},{6,7},{7,6},{8,9},{9,8},{10,11... | collective-permute-start | bytes 4718600 | tf_op jit(solution)/shard_map/ppermute | solution.py:490
  53.4 90.5 %copy-start.40 = (s32[2,4,2,2,2048]{4,3,2,1,0:T(2,128)}, s32[2,4,2,2,2048]{4,3,2,1,0:T(2,128)S(1)}, u32[]{:S(2)}) copy-start(s32[2,4,2,2,2048]{4,3,2,1,0:T(2,128)S(1)} %broadcast_select_fusion.1) | copy-start | bytes 786436
  67.6 161.6 %copy-start.42 = (s32[2,4,2,2,2048]{4,3,2,1,0:T(2,128)}, s32[2,4,2,2,2048]{4,3,2,1,0:T(2,128)S(1)}, u32[]{:S(2)}) copy-start(s32[2,4,2,2,2048]{4,3,2,1,0:T(2,128)S(1)} %broadcast_select_fusion) | copy-start | bytes 786436
  68.0 47.7 %copy-start.60 = (s32[4,2048]{1,0:T(4,128)}, s32[4,2048]{1,0:T(4,128)S(1)}, u32[]{:S(2)}) copy-start(s32[4,2048]{1,0:T(4,128)S(1)} %get-tuple-element.258.refs_4_) | copy-start | bytes 98308
  116.8 28.0 %collective-permute-start.17 = (bf16[1024,768]{1,0:T(8,128)(2,1)}, bf16[1024,768]{1,0:T(8,128)(2,1)S(1)}, u32[]{:S(2)}, u32[]{:S(2)}) collective-permute-start(bf16[1024,768]{1,0:T(8,128)(2,1)} %shard_map.416.refs_1_), channel_id=1, source_target_pairs={{0,2},{2,0},{1,3},{3,1},{4,6},{6,4},{5,7},{7,5},{8,10},{10,8},{9,1... | collective-permute-start | bytes 4718600 | tf_op jit(solution)/shard_map/ppermute | solution.py:490
  159.0 71.1 %all-to-all-start.1 = ((bf16[4,2,320,768]{3,2,1,0:T(8,128)(2,1)}), bf16[4,2,320,768]{3,2,1,0:T(8,128)(2,1)}, u32[]{:S(2)}, u32[]{:S(2)}) async-start(bf16[4,2,320,768]{3,2,1,0:T(8,128)(2,1)} %shard_map.418), calls=%async_computation.2 | async-start | bytes 7864320 | tf_op jit(solution)/shard_map/all_to_all | solution.py:82
  163.8 15.2 %collective-permute-start.3 = (bf16[768,768]{1,0:T(8,128)(2,1)}, bf16[768,768]{1,0:T(8,128)(2,1)}, u32[]{:S(2)}, u32[]{:S(2)}) collective-permute-start(bf16[768,768]{1,0:T(8,128)(2,1)} %bitcast.8), channel_id=1, source_target_pairs={{0,2},{2,0},{1,3},{3,1},{4,6},{6,4},{5,7},{7,5},{8,10},{10,8},{9,1... | collective-permute-start | bytes 3538952 | tf_op jit(solution)/shard_map/ppermute | solution.py:490
  178.7 47.3 %collective-permute-start.4 = (bf16[1024,768]{1,0:T(8,128)(2,1)}, bf16[1024,768]{1,0:T(8,128)(2,1)}, u32[]{:S(2)}, u32[]{:S(2)}) collective-permute-start(bf16[1024,768]{1,0:T(8,128)(2,1)} %dynamic-slice_bitcast_fusion.1.refs_0_), channel_id=1, source_target_pairs={{0,1},{1,0},{2,3},{3,2},{4,5},{5,4},{6,7},{7,6},{8,9},{9,8},{10,11... | collective-permute-start | bytes 4718600 | tf_op jit(solution)/shard_map/ppermute | solution.py:490
  226.0 2.3 collective-permute-start.9
  226.1 7.7 collective-permute-start.13
  229.1 4.7 collective-permute-start.14
  230.1 17.5 %all-to-all-start.2 = ((f32[4,2,320]{2,1,0:T(2,128)}), f32[4,2,320]{2,1,0:T(2,128)S(1)}, u32[]{:S(2)}, u32[]{:S(2)}) async-start(f32[4,2,320]{2,1,0:T(2,128)} %shard_map.419), calls=%async_computation.3 | async-start | bytes 24576 | tf_op jit(solution)/shard_map/all_to_all | solution.py:82
  249.1 109.6 %all-to-all-start.3 = ((bf16[4,2,320,768]{3,2,1,0:T(8,128)(2,1)}), bf16[4,2,320,768]{3,2,1,0:T(8,128)(2,1)}, u32[]{:S(2)}, u32[]{:S(2)}) async-start(bf16[4,2,320,768]{3,2,1,0:T(8,128)(2,1)} %shard_map.420), calls=%async_computation.4 | async-start | bytes 7864320 | tf_op jit(solution)/shard_map/all_to_all | solution.py:82
  253.9 84.4 %all-gather.13.cloned.1.call-start = ((), (), s32[]{:S(2)}) async-start(), calls=%async_computation.19 | async-start | bytes 4718592 | tf_op jit(solution)/shard_map/all_gather | solution.py:483
  254.5 78.0 %copy-start.7 = (bf16[1,768,2,384]{3,1,2,0:T(8,128)(2,1)S(1)}, bf16[1,768,2,384]{3,1,2,0:T(8,128)(2,1)}, u32[]{:S(2)}) copy-start(bf16[1,768,2,384]{3,1,2,0:T(8,128)(2,1)} %copy.458) | copy-start | bytes 3538948
  254.5 78.0 %copy-start.9 = (bf16[384,768]{1,0:T(8,128)(2,1)S(1)}, bf16[384,768]{1,0:T(8,128)(2,1)}, u32[]{:S(2)}) copy-start(bf16[384,768]{1,0:T(8,128)(2,1)} %get-tuple-element.240.refs_6_.refs_4_) | copy-start | bytes 1769476
  254.5 78.0 %copy-start.13 = (bf16[384,768]{1,0:T(8,128)(2,1)S(1)}, bf16[384,768]{1,0:T(8,128)(2,1)}, u32[]{:S(2)}) copy-start(bf16[384,768]{1,0:T(8,128)(2,1)} %copy-done.12) | copy-start | bytes 1769476
  254.5 77.9 %collective-permute-start.5 = (bf16[2,768,384]{2,1,0:T(8,128)(2,1)}, bf16[2,768,384]{2,1,0:T(8,128)(2,1)S(1)}, u32[]{:S(2)}, u32[]{:S(2)}) collective-permute-start(bf16[2,768,384]{2,1,0:T(8,128)(2,1)} %shard_map.404), channel_id=1, source_target_pairs={{0,1},{1,0},{2,3},{3,2},{4,5},{5,4},{6,7},{7,6},{8,9},{9,8},{10,11... | collective-permute-start | bytes 3538952 | tf_op jit(solution)/shard_map/ppermute | solution.py:626
  255.1 77.3 %collective-permute-start.6 = (bf16[2,768,384]{2,1,0:T(8,128)(2,1)}, bf16[2,768,384]{2,1,0:T(8,128)(2,1)}, u32[]{:S(2)}, u32[]{:S(2)}) collective-permute-start(bf16[2,768,384]{2,1,0:T(8,128)(2,1)} %shard_map.405), channel_id=1, source_target_pairs={{0,2},{1,3},{2,0},{3,1},{4,6},{5,7},{6,4},{7,5},{8,10},{9,11},{10,... | collective-permute-start | bytes 3538952 | tf_op jit(solution)/shard_map/ppermute | solution.py:626
  255.1 77.3 %collective-permute-start.7 = (bf16[2,768,384]{2,1,0:T(8,128)(2,1)}, bf16[2,768,384]{2,1,0:T(8,128)(2,1)}, u32[]{:S(2)}, u32[]{:S(2)}) collective-permute-start(bf16[2,768,384]{2,1,0:T(8,128)(2,1)} %shard_map.406), channel_id=1, source_target_pairs={{0,3},{1,2},{2,1},{3,0},{4,7},{5,6},{6,5},{7,4},{8,11},{9,10},{10,... | collective-permute-start | bytes 3538952 | tf_op jit(solution)/shard_map/ppermute | solution.py:626
  256.7 64.8 %collective-permute-start.8 = (bf16[384,768]{1,0:T(8,128)(2,1)}, bf16[384,768]{1,0:T(8,128)(2,1)S(1)}, u32[]{:S(2)}, u32[]{:S(2)}) collective-permute-start(bf16[384,768]{1,0:T(8,128)(2,1)} %shard_map.407), channel_id=1, source_target_pairs={{0,1},{1,0},{2,3},{3,2},{4,5},{5,4},{6,7},{7,6},{8,9},{9,8},{10,11... | collective-permute-start | bytes 1769480 | tf_op jit(solution)/shard_map/ppermute | solution.py:626
  257.3 75.1 %collective-permute-start.10 = (bf16[384,768]{1,0:T(8,128)(2,1)}, bf16[384,768]{1,0:T(8,128)(2,1)S(1)}, u32[]{:S(2)}, u32[]{:S(2)}) collective-permute-start(bf16[384,768]{1,0:T(8,128)(2,1)} %shard_map.409), channel_id=1, source_target_pairs={{0,3},{1,2},{2,1},{3,0},{4,7},{5,6},{6,5},{7,4},{8,11},{9,10},{10,... | collective-permute-start | bytes 1769480 | tf_op jit(solution)/shard_map/ppermute | solution.py:626
  258.2 76.5 %copy-start.21 = (s32[2]{0:T(128)}, s32[2]{0:T(128)S(1)}, u32[]{:S(2)}) copy-start(s32[2]{0:T(128)S(1)} %pad_add_fusion.1.place_ref) | copy-start | bytes 28
  340.9 4.3 collective-permute-start.12
  358.7 52.6 %all-to-all-start.4 = ((bf16[8,320,768]{2,1,0:T(8,128)(2,1)}), bf16[8,320,768]{2,1,0:T(8,128)(2,1)}, u32[]{:S(2)}, u32[]{:S(2)}) async-start(bf16[8,320,768]{2,1,0:T(8,128)(2,1)} %shard_map.421.refs_1_), calls=%async_computation.5 | async-start | bytes 7864320 | tf_op jit(solution)/shard_map/all_to_all | solution.py:82
  363.4 3.5 collective-permute-start.11
  411.3 53.7 %all-to-all-start.5 = ((bf16[8,320,768]{2,1,0:T(8,128)(2,1)}), bf16[8,320,768]{2,1,0:T(8,128)(2,1)}, u32[]{:S(2)}, u32[]{:S(2)}) async-start(bf16[8,320,768]{2,1,0:T(8,128)(2,1)} %shard_map.424), calls=%async_computation.6 | async-start | bytes 7864320 | tf_op jit(solution)/shard_map/all_to_all | solution.py:82
  465.0 54.6 %all-to-all-start.6 = ((bf16[8,1,320,768]{3,2,1,0:T(8,128)(2,1)}), bf16[8,1,320,768]{3,2,1,0:T(8,128)(2,1)}, u32[]{:S(2)}, u32[]{:S(2)}) async-start(bf16[8,1,320,768]{3,2,1,0:T(8,128)(2,1)} %bitcast.294), calls=%async_computation.7 | async-start | bytes 7864320 | tf_op jit(solution)/shard_map/all_to_all | solution.py:82
  526.4 9.4 collective-permute-start.18
  528.1 53.8 %all-to-all-start.7 = ((bf16[8,1,320,768]{3,2,1,0:T(8,128)(2,1)}), bf16[8,1,320,768]{3,2,1,0:T(8,128)(2,1)}, u32[]{:S(2)}, u32[]{:S(2)}) async-start(bf16[8,1,320,768]{3,2,1,0:T(8,128)(2,1)} %bitcast.295), calls=%async_computation.8 | async-start | bytes 7864320 | tf_op jit(solution)/shard_map/all_to_all | solution.py:82
  581.9 158.0 %all-to-all-start.8 = ((bf16[8,2,320,768]{3,2,1,0:T(8,128)(2,1)}), bf16[8,2,320,768]{3,2,1,0:T(8,128)(2,1)}, u32[]{:S(2)}, u32[]{:S(2)}) async-start(bf16[8,2,320,768]{3,2,1,0:T(8,128)(2,1)} %bitcast.282), calls=%async_computation.9 | async-start | bytes 15728640 | tf_op jit(solution)/shard_map/all_to_all | solution.py:82
  590.2 195.8 %reduce-scatter.5.cloned.1.call-start = ((), (), s32[]{:S(2)}) async-start(), calls=%async_computation.16 | async-start | bytes 4718592 | tf_op jit(solution)/shard_map/reduce_scatter | solution.py:692
  590.4 116.7 %collective-permute-start.23 = (bf16[1024,768]{1,0:T(8,128)(2,1)}, bf16[1024,768]{1,0:T(8,128)(2,1)}, u32[]{:S(2)}, u32[]{:S(2)}) collective-permute-start(bf16[1024,768]{1,0:T(8,128)(2,1)} %fusion.24.refs_1_), channel_id=1, source_target_pairs={{0,16},{16,0},{1,17},{17,1},{2,18},{18,2},{3,19},{19,3},{4,20},{20... | collective-permute-start | bytes 4718600 | tf_op jit(solution)/shard_map/ppermute | solution.py:668
  603.3 103.8 %collective-permute-start.19 = (f32[256,768]{1,0:T(8,128)S(1)}, f32[256,768]{1,0:T(8,128)S(1)}, u32[]{:S(2)}, u32[]{:S(2)}) collective-permute-start(f32[256,768]{1,0:T(8,128)S(1)} %get-tuple-element.242), channel_id=1, source_target_pairs={{0,2},{2,0},{1,3},{3,1},{4,6},{6,4},{5,7},{7,5},{8,10},{10,8},{9,1... | collective-permute-start | bytes 2359304 | tf_op jit(solution)/shard_map/ppermute | solution.py:551
  603.4 103.7 %collective-permute-start.22 = (f32[256,768]{1,0:T(8,128)S(1)}, f32[256,768]{1,0:T(8,128)S(1)}, u32[]{:S(2)}, u32[]{:S(2)}) collective-permute-start(f32[256,768]{1,0:T(8,128)S(1)} %get-tuple-element.243), channel_id=1, source_target_pairs={{0,2},{2,0},{1,3},{3,1},{4,6},{6,4},{5,7},{7,5},{8,10},{10,8},{9,1... | collective-permute-start | bytes 2359304 | tf_op jit(solution)/shard_map/ppermute | solution.py:551
  603.9 103.2 %collective-permute-start.21 = (f32[256,768]{1,0:T(8,128)S(1)}, f32[256,768]{1,0:T(8,128)S(1)}, u32[]{:S(2)}, u32[]{:S(2)}) collective-permute-start(f32[256,768]{1,0:T(8,128)S(1)} %get-tuple-element.244), channel_id=1, source_target_pairs={{0,2},{2,0},{1,3},{3,1},{4,6},{6,4},{5,7},{7,5},{8,10},{10,8},{9,1... | collective-permute-start | bytes 2359304 | tf_op jit(solution)/shard_map/ppermute | solution.py:551
  604.0 103.2 %collective-permute-start.20 = (f32[256,768]{1,0:T(8,128)S(1)}, f32[256,768]{1,0:T(8,128)S(1)}, u32[]{:S(2)}, u32[]{:S(2)}) collective-permute-start(f32[256,768]{1,0:T(8,128)S(1)} %get-tuple-element.245), channel_id=1, source_target_pairs={{0,2},{2,0},{1,3},{3,1},{4,6},{6,4},{5,7},{7,5},{8,10},{10,8},{9,1... | collective-permute-start | bytes 2359304 | tf_op jit(solution)/shard_map/ppermute | solution.py:551
  604.4 102.7 %copy-start.26 = (f32[1024,768]{1,0:T(8,128)S(1)}, f32[1024,768]{1,0:T(8,128)}, u32[]{:S(2)}) copy-start(f32[1024,768]{1,0:T(8,128)} %get-tuple-element.253) | copy-start | bytes 9437188
  604.4 102.8 %copy-start.73 = (f32[768]{0:T(1024)S(1)}, f32[768]{0:T(1024)}, u32[]{:S(2)}) copy-start(f32[768]{0:T(1024)} %copy-done.72) | copy-start | bytes 9220
  604.4 102.8 %copy-start.75 = (f32[1024]{0:T(1024)S(1)}, f32[1024]{0:T(1024)}, u32[]{:S(2)}) copy-start(f32[1024]{0:T(1024)} %copy-done.74) | copy-start | bytes 12292
  611.7 116.0 %copy-start.79 = (f32[1024]{0:T(1024)S(1)}, f32[1024]{0:T(1024)}, u32[]{:S(2)}) copy-start(f32[1024]{0:T(1024)} %copy-done.78) | copy-start | bytes 12292
  739.9 137.5 %all-gather.15.cloned.1.call-start = ((), (), s32[]{:S(2)}) async-start(), calls=%async_computation.20 | async-start | bytes 6291456 | tf_op jit(solution)/shard_map/all_gather | solution.py:703
  747.5 5.9 collective-permute-start.24
  820.2 10.2 collective-permute-start.25
  820.3 75.7 %all-to-all-start.9 = ((bf16[2,1024,768]{2,1,0:T(8,128)(2,1)}), bf16[2,1024,768]{2,1,0:T(8,128)(2,1)S(1)}, u32[]{:S(2)}, u32[]{:S(2)}) async-start(bf16[2,1024,768]{2,1,0:T(8,128)(2,1)} %broadcast_in_dim.74.refs_1_), calls=%async_computation.11 | async-start | bytes 6291456 | tf_op jit(solution)/shard_map/all_to_all | solution.py:82
  829.8 53.4 %collective-permute-start.27 = (f32[768,768]{1,0:T(8,128)}, f32[768,768]{1,0:T(8,128)}, u32[]{:S(2)}, u32[]{:S(2)}) collective-permute-start(f32[768,768]{1,0:T(8,128)} %fusion.50.refs_1_), channel_id=1, source_target_pairs={{0,2},{2,0},{1,3},{3,1},{4,6},{6,4},{5,7},{7,5},{8,10},{10,8},{9,1... | collective-permute-start | bytes 7077896 | tf_op jit(solution)/shard_map/ppermute | solution.py:720
  882.9 38.3 %collective-permute-start.26 = (f32[768,1024]{1,0:T(8,128)}, f32[768,1024]{1,0:T(8,128)}, u32[]{:S(2)}, u32[]{:S(2)}) collective-permute-start(f32[768,1024]{1,0:T(8,128)} %fusion.30.refs_1_), channel_id=1, source_target_pairs={{0,2},{2,0},{1,3},{3,1},{4,6},{6,4},{5,7},{7,5},{8,10},{10,8},{9,1... | collective-permute-start | bytes 9437192 | tf_op jit(solution)/shard_map/ppermute | solution.py:720
  897.7 38.4 %all-to-all-start.12 = ((bf16[4,384,768]{2,1,0:T(8,128)(2,1)}), bf16[4,384,768]{2,1,0:T(8,128)(2,1)}, u32[]{:S(2)}, u32[]{:S(2)}) async-start(bf16[4,384,768]{2,1,0:T(8,128)(2,1)} %bitcast.301), calls=%async_computation.14 | async-start | bytes 4718592 | tf_op jit(solution)/shard_map/all_to_all | solution.py:82
  930.6 23.0 %collective-permute-start.28 = (f32[3,768]{1,0:T(4,128)S(1)}, f32[3,768]{1,0:T(4,128)S(1)}, u32[]{:S(2)}, u32[]{:S(2)}) collective-permute-start(f32[3,768]{1,0:T(4,128)S(1)} %pad_maximum_fusion.2), channel_id=1, source_target_pairs={{0,2},{2,0},{1,3},{3,1},{4,6},{6,4},{5,7},{7,5},{8,10},{10,8},{9,1... | collective-permute-start | bytes 27656 | tf_op jit(solution)/shard_map/ppermute | solution.py:67
  936.1 61.1 %all-to-all-start.10 = ((bf16[4,2,768,384]{3,1,2,0:T(2,128)(2,1)}), bf16[4,2,768,384]{3,1,2,0:T(2,128)(2,1)}, u32[]{:S(2)}, u32[]{:S(2)}) async-start(bf16[4,2,768,384]{3,1,2,0:T(2,128)(2,1)} %bitcast.290), calls=%async_computation.12 | async-start | bytes 9437184 | tf_op jit(solution)/shard_map/all_to_all | solution.py:82
  953.6 4.7 collective-permute-start.29
  958.4 6.1 collective-permute-start.30
  964.5 8.9 collective-permute-start.31
  973.5 21.6 %collective-permute-start.32 = (f32[2,6]{1,0:T(2,128)S(1)}, f32[2,6]{1,0:T(2,128)S(1)}, u32[]{:S(2)}, u32[]{:S(2)}) collective-permute-start(f32[2,6]{1,0:T(2,128)S(1)} %reshape_squeeze.3), channel_id=1, source_target_pairs={{0,1},{1,0},{2,3},{3,2},{4,5},{5,4},{6,7},{7,6},{8,9},{9,8},{10,11... | collective-permute-start | bytes 152 | tf_op jit(solution)/shard_map/ppermute | solution.py:67
  997.2 65.9 %all-to-all-start.11 = ((bf16[8,96,1792]{2,1,0:T(8,128)(2,1)}), bf16[8,96,1792]{2,1,0:T(8,128)(2,1)S(1)}, u32[]{:S(2)}, u32[]{:S(2)}) async-start(bf16[8,96,1792]{2,1,0:T(8,128)(2,1)} %bitcast.102), calls=%async_computation.13 | async-start | bytes 5505024 | tf_op jit(solution)/shard_map/all_to_all | solution.py:82
  (82 other events, 566.5 us)
Sparse Core Ops, SparseCore 0:
  9.6 14.8 all-gather.8
  33.1 88.4 reduce-scatter.2
  144.0 51.8 all-gather.10
  256.6 80.2 all-gather.12
  740.0 45.9 reduce-scatter.4
  820.4 56.9 all-gather.14
